TPU v7x, 768 devices: a whole 4x8x12 slice. The times are simulated.
768 devices in a mesh: group: 8 (over x, y_hi), replica: 96 (over y_lo, z, core).
Axes of the slice: x: 4, y: 8 (y_hi: 2, y_lo: 4; y = y_hi * 4 + y_lo), z: 12, core: 2. Of those that a mesh axis runs over, the one named last changes fastest.
Arguments:
- hidden_in: bfloat16 [98304, 4096], P(('group', 'replica')), may hold values from -40 to 40
- norm_gain: bfloat16 [4096], P('group'), may hold values from 0.099609375 to 1.8984375
- key_codes: bfloat16 [4096, 512], P('group'), may hold values from -4 to 4
- key_scales: bfloat16 [4096, 2], P('group'), may hold values from 0.0049743652 to 0.049804688
- key_cotangent: bfloat16 [98304, 512], P(('group', 'replica')), may hold values from -17 to 17
Outputs:
- keys_out: bfloat16 [98304, 512], P(('group', 'replica'))
- input_gradient: bfloat16 [98304, 4096], P(('group', 'replica'))
- weight_grad: bfloat16 [4096, 512], P('group')
- gain_gradient: float32 [4096], replicated
All inputs are finite; a program needn't handle non-finite values.
Results may differ from a plain program's by a relative error of at most 0.017.
Values may be sent and summed in bfloat16 or wider, within the bound.
No kernel may reach another device: no remote copies, remote signals or barrier semaphores. Data moves between devices by JAX's collectives and lax.ppermute only.
A program may use at most 64 MiB of HBM per device.

v0:
```python
import jax
import jax.numpy as jnp
from jax import lax
from jax.sharding import PartitionSpec as P


def dequantize(codes, scales, block_len):
    rows = codes.shape[0]
    grouped = (
        codes.astype(jnp.float32).reshape(rows, -1, block_len)
        * scales.astype(jnp.float32)[:, :, None]
    )
    return grouped.reshape(rows, -1).astype(jnp.bfloat16)


def body(hidden_in, norm_gain, key_codes, key_scales, key_cotangent):
    tok_rows = hidden_in.shape[0]
    key_cols = key_codes.shape[1]
    block_len = key_cols // key_scales.shape[1]
    hidden_rows = hidden_in.astype(jnp.float32)
    inverse_norm = lax.rsqrt(jnp.mean(hidden_rows * hidden_rows, axis=1, keepdims=True) + 1e-05)
    unit_rows = hidden_rows * inverse_norm
    codes, scales, gain_all = (
        lax.all_gather(key_codes, "group", axis=0, tiled=True),
        lax.all_gather(key_scales, "group", axis=0, tiled=True),
        lax.all_gather(norm_gain, "group", axis=0, tiled=True),
    )
    weight = dequantize(codes, scales, block_len)
    gain_vector = gain_all.astype(jnp.float32)
    normalized_rows = (unit_rows * gain_vector).astype(jnp.bfloat16)
    keys = jnp.dot(normalized_rows, weight, preferred_element_type=jnp.float32)
    keys_out = keys.astype(jnp.bfloat16)
    normalized_gradient = lax.dot_general(
        key_cotangent, weight, (((1,), (1,)), ((), ())), preferred_element_type=jnp.float32
    )
    unit_input_gradient = normalized_gradient * gain_vector
    input_gradient = (
        inverse_norm
        * (
            unit_input_gradient
            - unit_rows * jnp.mean(unit_input_gradient * unit_rows, axis=1, keepdims=True)
        )
    ).astype(jnp.bfloat16)
    gain_portion = jnp.sum(normalized_gradient * unit_rows, axis=0)
    owners = lax.axis_size("group")
    group_sum = lax.psum_scatter(
        lax.dot_general(
            normalized_rows,
            key_cotangent,
            (((0,), (0,)), ((), ())),
            preferred_element_type=jnp.float32,
        ).astype(jnp.bfloat16),
        "group",
        scatter_dimension=0,
        tiled=True,
    ).astype(jnp.float32)
    total = lax.psum(group_sum, "replica")
    gain_total = lax.psum(gain_portion, ("group", "replica"))
    total_tokens = tok_rows * owners * lax.axis_size("replica")
    scale_multiplier = 1.0 / jnp.sqrt(jnp.float32(total_tokens))
    weight_grad = (total * scale_multiplier).astype(jnp.bfloat16)
    gain_gradient = gain_total * scale_multiplier
    return (keys_out, input_gradient, weight_grad, gain_gradient)


def solution(mesh):
    in_specs = (
        P(("group", "replica"), None),
        P("group"),
        P("group", None),
        P("group", None),
        P(("group", "replica"), None),
    )
    out_specs = (
        P(("group", "replica"), None),
        P(("group", "replica"), None),
        P("group", None),
        P(),
    )
    return jax.shard_map(body, mesh=mesh, in_specs=in_specs, out_specs=out_specs, check_vma=False)
```

profile of v0, /device:TPU:1, one launch (start us, length us, event | category | flops | bytes accessed | tf_op | source)
XLA Modules:
  0.0 680.3 jit_solution(17268260393538917336)
XLA Ops:
  7.2 0.0 copy-start
  7.2 0.0 copy-start.2
  7.2 0.0 all-gather.3.cloned.1.call-start
  7.2 0.7 all-gather.3.cloned.1.call-update
  7.9 0.0 reduce-scatter.2.cloned.1.call-start
  8.0 1.6 copy.12
  9.6 0.0 copy-done.2
  9.6 35.8 %all-gather = bf16[8,1,512]{2,1,0:T(2,128)(2,1)S(1)} all-gather(bf16[1,1,512]{2,1,0:T(2,128)(2,1)S(1)} %reshape.25), channel_id=1, replica_groups=mesh['group'=8,'replica'=96] {'group'}, dimensions={0}, use_global_device_ids=true | all-gather | bytes 9216 | tf_op jit(solution)/shard_map/all_gather | solution.py:26
  45.5 0.6 fusion.10
  46.0 0.0 copy-done
  46.0 2.8 convolution_convert_fusion
  48.9 0.0 copy-start.1
  48.9 0.0 reduce-scatter.2.cloned.1.call-update
  48.9 0.7 copy-done.1
  49.5 34.8 %all_gather.11 = bf16[4096,2]{0,1:T(2,128)(2,1)S(1)} all-gather(bf16[512,2]{0,1:T(2,128)(2,1)S(1)} %copy-done.1), channel_id=1, replica_groups=mesh['group'=8,'replica'=96] {'group'}, dimensions={0}, use_global_device_ids=true | all-gather | bytes 18432 | tf_op jit(solution)/shard_map/all_gather | solution.py:25
  84.3 0.4 copy.13
  84.8 4.9 mul.73
  89.7 4.2 copy.15
  93.9 36.8 %all-gather.3.cloned.1.call-done = bf16[4096,512]{1,0:T(8,128)(2,1)} async-done(((bf16[512,512]{1,0:T(8,128)(2,1)}), bf16[4096,512]{1,0:T(8,128)(2,1)}) %all-gather.3.cloned.1.call-update) | async-done | bytes 4194320 | tf_op jit(solution)/shard_map/all_gather | solution.py:24
  130.7 5.5 fusion.9
  136.2 0.8 fusion.8
  137.0 1.3 copy.14
  138.3 126.8 %psum.15 = f32[4096]{0:T(1024)S(1)} all-reduce(f32[4096]{0:T(1024)S(1)} %get-tuple-element.12), channel_id=1, replica_groups=mesh['group'=8,'replica'=96] {'group','replica'}, use_global_device_ids=true, to_apply=%region_5.0 | all-reduce | flops 4096 | bytes 32768 | tf_op jit(solution)/shard_map/psum | solution.py:58
  265.1 0.6 broadcast_multiply_fusion
  265.7 6.4 convolution_convert_fusion.1
  272.0 0.0 reduce-scatter.2.cloned.1.call-done
  272.0 400.5 %all-reduce.1 = f32[512,512]{1,0:T(8,128)S(1)} all-reduce(bf16[512,512]{1,0:T(8,128)(2,1)} %reduce-scatter.2.cloned.1.call-done), channel_id=1, replica_groups=mesh['group'=8,'replica'=96] {'replica'}, use_global_device_ids=true, to_apply=%region_3.0 | all-reduce | flops 262144 | bytes 1572864 | tf_op jit(solution)/shard_map/psum | solution.py:57
  672.5 0.9 multiply_convert_fusion.1
  (4 shorter events, 0.0 us)
Async XLA Ops:
  7.2 38.9 %copy-start = (bf16[128,512]{1,0:T(8,128)(2,1)S(1)}, bf16[128,512]{1,0:T(8,128)(2,1)}, u32[]{:S(2)}) copy-start(bf16[128,512]{1,0:T(8,128)(2,1)} %param.9) | copy-start | bytes 393220
  7.2 2.4 copy-start.2
  7.2 123.5 %all-gather.3.cloned.1.call-start = ((), (), s32[]{:S(2)}) async-start(), calls=%async_computation.1 | async-start | bytes 4718592 | tf_op jit(solution)/shard_map/all_gather | solution.py:24
  7.9 264.1 %reduce-scatter.2.cloned.1.call-start = ((), (), s32[]{:S(2)}) async-start(), calls=%async_computation.2 | async-start | bytes 4718592 | tf_op jit(solution)/shard_map/reduce_scatter | solution.py:46
  48.9 0.7 copy-start.1
Sparse Core Ops, SparseCore 0:
  11.8 118.7 all-gather.2
  136.0 131.8 reduce-scatter.1
where the time goes:
time: 686 us; the launch traced here: 680 us
  blocking collectives  598 us (87%)
  waiting for transfers between devices  37.5 us (5%)
  matrix products  14.7 us (2%)
  between operations  14.1 us (2%)
  local copies, waits for them, and re-layouts  13.1 us (2%)
    psum x1, blocking collectives, body(): total = lax.psum(group_sum, 'replica')  400 us
    psum x1, blocking collectives, body(): gain_total = lax.psum(gain_portion, ('group', 'replica'))  127 us
    all_gather x1, waiting for transfers between devices, body(): lax.all_gather(key_codes, 'group', axis=0, tiled=True)  36.8 us
    all_gather x1, blocking collectives, body(): lax.all_gather(norm_gain, 'group', axis=0, tiled=True)  35.8 us
    all_gather x1, blocking collectives, body(): lax.all_gather(key_scales, 'group', axis=0, tiled=True)  34.8 us
  transfers between devices with their start and end apart: 2, of which 1 were waited for; matrix products, arithmetic and copies ran while one was open for 4% of the time, Pallas kernels for 0%

commit v1 on v0

v1 whole, which is shorter than its diff:
```python
import jax
import jax.numpy as jnp
from jax import lax
from jax.sharding import Mesh
from jax.sharding import PartitionSpec as P

F32 = jnp.float32
BF16 = jnp.bfloat16


def spread(value, axes, size):
    copies = jnp.broadcast_to(value[None], (size,) + value.shape)
    return lax.all_to_all(copies, axes, 0, 0)


def by_core(own, other):
    first = lax.axis_index("c") == 0
    return jnp.where(first, own, other), jnp.where(first, other, own)


def body(hidden_in, norm_gain, key_codes, key_scales, key_cotangent):
    nx, nh, nl, nz, nc = (lax.axis_size(a) for a in ("x", "yh", "yl", "z", "c"))
    tok, width = hidden_in.shape
    rows, cols = key_codes.shape
    block = cols // key_scales.shape[1]
    total_tokens = tok * nx * nh * nl * nz * nc
    half = rows // nc
    core = lax.axis_index("c")
    swap_c = [(0, 1), (1, 0)]

    gain = norm_gain.astype(F32)[:, None]
    scales = jnp.repeat(key_scales.astype(F32), block, axis=1)
    scaled = key_codes.astype(F32) * scales

    mine = lax.dynamic_slice_in_dim((scaled * gain).astype(BF16), core * half, half, 0)
    hidden_rows = hidden_in.astype(F32)
    inv = lax.rsqrt(jnp.mean(hidden_rows * hidden_rows, axis=1, keepdims=True) + 1e-05)
    cot_inv = (key_cotangent.astype(F32) * inv).astype(BF16)

    pieces = hidden_in.reshape(tok, nx, nh, nc, half).transpose(1, 3, 0, 2, 4)
    pieces = pieces.reshape(nx * nc, tok, nh * half)
    copies = jnp.broadcast_to(cot_inv[None], (nx * nc, tok, cols))
    sent, mine = lax.optimization_barrier((jnp.concatenate([pieces, copies], axis=2), mine))
    mate = lax.ppermute(mine, "yh", [(0, 1), (1, 0)])
    got = lax.all_to_all(sent, ("x", "c"), 0, 0)

    got, mate = lax.optimization_barrier((got, mate))
    low = lax.axis_index("yh") == 0
    pair = jnp.stack([jnp.where(low, mine, mate), jnp.where(low, mate, mine)])
    pair = pair.reshape(nh * half, cols)
    got, pair = lax.optimization_barrier((got, pair))
    own_half = lax.all_gather(pair, "x", axis=0, tiled=True)
    got = got.reshape(nx * nc * tok, nh * half + cols)
    product = lax.dot_general(
        got[:, : nh * half], got[:, nh * half :], (((0,), (0,)), ((), ())), preferred_element_type=F32
    ).astype(BF16)

    quarter = half // nl
    terms = lax.all_to_all(product.reshape(nh * nl, quarter, cols), ("yh", "yl"), 0, 0)
    summed = jnp.sum(terms.astype(F32), axis=0).astype(BF16)
    piece = -(-quarter // nz)
    summed = jnp.pad(summed, ((0, piece * nz - quarter), (0, 0))).reshape(nz, piece, cols)
    total = jnp.sum(lax.all_to_all(summed, "z", 0, 0).astype(F32), axis=0)
    scale = 1.0 / jnp.sqrt(F32(total_tokens))
    total = (total * scale).astype(BF16)

    whole = spread(total, "z", nz).reshape(nz * piece, cols)[:quarter]
    whole, own_half = lax.optimization_barrier((whole, own_half))
    other_half = lax.ppermute(own_half, "c", swap_c)
    whole = spread(whole, "yl", nl).reshape(half, cols)
    whole, other_half = lax.optimization_barrier((whole, other_half))
    whole = jnp.concatenate(by_core(whole, lax.ppermute(whole, "c", swap_c)), axis=0).astype(F32)
    weight_grad = (whole * gain).astype(BF16)
    gain_part = jnp.sum(whole * scaled.astype(BF16).astype(F32), axis=1)
    gain_gradient = spread(gain_part.reshape(-1, 128), ("x", "yh"), nx * nh).reshape(width)

    parts = by_core(own_half, other_half)
    gained = jnp.stack([p.reshape(nx * nh, half, cols) for p in parts], axis=1)
    gained = gained.reshape(width, cols)
    keys = jnp.dot(hidden_in, gained, preferred_element_type=F32) * inv
    keys_out = keys.astype(BF16)
    mean = jnp.sum(keys * key_cotangent.astype(F32), axis=1, keepdims=True) / width
    unit_gradient = lax.dot_general(
        key_cotangent, gained, (((1,), (1,)), ((), ())), preferred_element_type=F32
    )
    input_gradient = (inv * (unit_gradient - hidden_rows * inv * mean)).astype(BF16)
    return (keys_out, input_gradient, weight_grad, gain_gradient)


def solution(mesh):
    fine = Mesh(mesh.devices.reshape(4, 2, 4, 12, 2), ("x", "yh", "yl", "z", "c"))
    tokens = P(("x", "yh", "yl", "z", "c"), None)
    group = ("x", "yh")
    in_specs = (tokens, P(group), P(group, None), P(group, None), tokens)
    out_specs = (tokens, tokens, P(group, None), P())
    return jax.shard_map(body, mesh=fine, in_specs=in_specs, out_specs=out_specs, check_vma=False)
```

time: 686 us -> 163 us (0.24)
  blocking collectives: 598 us -> 51.5 us
  starting transfers between devices: 0.08 us -> 33.6 us
  matrix products: 14.7 us -> 7.01 us
    psum x2 -> x0, blocking collectives: 527 us -> none  [the longest x1 400 us: body(): total = lax.psum(group_sum, 'replica')]
    all_gather x2 -> x0, blocking collectives: 70.6 us -> none  [the longest x1 35.8 us: body(): lax.all_gather(norm_gain, 'group', axis=0, tiled=True)]
    all_to_all x0 -> x3, blocking collectives: none -> 51.5 us  [the longest x1 20.4 us: body(): total = jnp.sum(lax.all_to_all(summed, 'z', 0, 0).astype(F32), axis=0)]
    all_gather x1, waiting for transfers between devices: 36.8 us -> 0.02 us  [body(): own_half = lax.all_gather(pair, 'x', axis=0, tiled=True)]
    all_to_all x0 -> x3, waiting for transfers between devices: none -> 22.5 us  [the longest x2 11.3 us: spread(): return lax.all_to_all(copies, axes, 0, 0)]
    all_to_all x0 -> x3, starting transfers between devices: none -> 20.8 us  [the longest x1 14 us: body(): got = lax.all_to_all(sent, ('x', 'c'), 0, 0)]
    ppermute x0 -> x3, waiting for transfers between devices: none -> 13.3 us  [the longest x1 13.3 us: body(): mate = lax.ppermute(mine, 'yh', [(0, 1), (1, 0)])]
    ppermute x0 -> x3, starting transfers between devices: none -> 12.8 us  [the longest x1 7.2 us: body(): other_half = lax.ppermute(own_half, 'c', swap_c)]
  transfers between devices with their start and end apart: 2 -> 7, of which waited for: 1 -> 4; matrix products, arithmetic and copies ran while one was open for 4% -> 9% of each run, Pallas kernels for 0% -> 0%
where the time goes in v1:
time: 163 us; the launch traced here: 162 us
  blocking collectives  51.5 us (32%)
  waiting for transfers between devices  35.8 us (22%)
  starting transfers between devices  33.6 us (21%)
  between operations  14.4 us (9%)
  local copies, waits for them, and re-layouts  11.6 us (7%)
  other arithmetic  8.64 us (5%)
  matrix products  7.01 us (4%)
    all_to_all x1, blocking collectives, body(): total = jnp.sum(lax.all_to_all(summed, 'z', 0, 0).astype(F32), axis=0)  20.4 us
    all_to_all x1, blocking collectives, body(): lax.all_to_all(product.reshape(nh * nl, quarter, cols), ('yh', 'yl'), 0, 0)  18.6 us
    all_to_all x1, starting transfers between devices, body(): got = lax.all_to_all(sent, ('x', 'c'), 0, 0)  14 us
    ppermute x1, waiting for transfers between devices, body(): mate = lax.ppermute(mine, 'yh', [(0, 1), (1, 0)])  13.3 us
    all_to_all x1, blocking collectives, spread(): return lax.all_to_all(copies, axes, 0, 0)  12.5 us
    all_to_all x2, waiting for transfers between devices, spread(): return lax.all_to_all(copies, axes, 0, 0)  11.3 us
    all_to_all x1, waiting for transfers between devices, body(): got = lax.all_to_all(sent, ('x', 'c'), 0, 0)  11.1 us
    ppermute x1, starting transfers between devices, body(): other_half = lax.ppermute(own_half, 'c', swap_c)  7.2 us
  transfers between devices with their start and end apart: 7, of which 4 were waited for; matrix products, arithmetic and copies ran while one was open for 9% of the time, Pallas kernels for 0%

profile of v1, /device:TPU:1, one launch (start us, length us, event | category | flops | bytes accessed | tf_op | source)
XLA Modules:
  0.0 162.5 jit_solution(12501701024363126768)
XLA Ops:
  7.2 0.0 copy-start.3
  7.2 0.9 copy.32
  8.1 0.6 broadcast_in_dim.13
  8.7 0.1 copy.36
  8.8 0.0 copy-done.3
  8.8 0.0 copy-start.5
  8.8 0.7 copy.28
  9.5 0.0 copy-start.7
  9.5 0.6 fusion.3
  10.1 0.0 copy-done.5
  10.1 0.1 copy.30
  10.2 0.1 copy.29
  10.3 0.0 copy-done.7
  10.3 0.1 dynamic-slice
  10.4 1.2 convert_multiply_fusion.4
  11.6 0.0 copy-start
  11.6 1.0 copy-done
  12.5 0.1 fusion.10
  12.7 0.1 broadcast_in_dim.12
  12.8 1.5 pad_maximum_fusion.1
  14.3 14.0 %all-to-all-start = ((bf16[8,128,1024]{1,2,0:T(8,128)(2,1)}), bf16[8,128,1024]{1,2,0:T(8,128)(2,1)S(1)}, u32[]{:S(2)}, u32[]{:S(2)}) async-start(bf16[8,128,1024]{1,2,0:T(8,128)(2,1)} %pad_maximum_fusion.1), calls=%async_computation | async-start | bytes 4194304 | tf_op jit(solution)/shard_map/all_to_all | solution.py:45
  28.3 0.0 all-gather.2.cloned.1.call-start
  28.3 1.9 %collective-permute-start = (bf16[256,512]{1,0:T(8,128)(2,1)S(1)}, bf16[256,512]{1,0:T(8,128)(2,1)}, u32[]{:S(2)}, u32[]{:S(2)}) collective-permute-start(bf16[256,512]{1,0:T(8,128)(2,1)S(1)} %fusion.10), channel_id=1, source_target_pairs={{0,96},{96,0},{1,97},{97,1},{2,98},{98,2},{3,99},{99,3},{4,100},{1... | collective-permute-start | bytes 786440 | tf_op jit(solution)/shard_map/ppermute | solution.py:44
  30.2 13.3 %collective-permute-done = bf16[256,512]{1,0:T(8,128)(2,1)} collective-permute-done((bf16[256,512]{1,0:T(8,128)(2,1)S(1)}, bf16[256,512]{1,0:T(8,128)(2,1)}, u32[]{:S(2)}, u32[]{:S(2)}) %collective-permute-start) | collective-permute-done | bytes 262176 | tf_op jit(solution)/shard_map/ppermute | solution.py:44
  43.6 11.1 %all-to-all-done = bf16[8,128,1024]{1,2,0:T(8,128)(2,1)S(1)} async-done(((bf16[8,128,1024]{1,2,0:T(8,128)(2,1)}), bf16[8,128,1024]{1,2,0:T(8,128)(2,1)S(1)}, u32[]{:S(2)}, u32[]{:S(2)}) %all-to-all-start) | async-done | bytes 2097184 | tf_op jit(solution)/shard_map/all_to_all | solution.py:45
  54.7 1.0 select_bitcast_fusion.1
  55.7 0.8 pad_maximum_fusion.2
  56.5 0.0 all-gather.2.cloned.1.call-update
  56.5 2.6 %copy.33 = bf16[8,128,1024]{2,1,0:T(8,128)(2,1)} copy(bf16[8,128,1024]{1,2,0:T(8,128)(2,1)S(1)} %all-to-all-done) | data formatting | bytes 4194304 | tf_op jit(solution)/shard_map/optimization_barrier | solution.py:51
  59.1 2.3 %convolution_convert_fusion = bf16[512,512]{1,0:T(8,128)(2,1)S(1)} fusion(bf16[1024,1024]{1,0:T(8,128)(2,1)} %bitcast.41), kind=kOutput, calls=%fused_computation.14 | convolution fusion | flops 537133056 | bytes 2621440 | tf_op jit(solution)/shard_map/dot_general | solution.py:54
  61.4 18.6 %all_to_all.30 = bf16[8,64,512]{2,1,0:T(8,128)(2,1)S(1)} all-to-all(bf16[8,64,512]{2,1,0:T(8,128)(2,1)S(1)} %bitcast.45), channel_id=1, replica_groups=mesh['x'=4,'yh'=2,'yl'=4,'z'=12,'c'=2] {'yh','yl'}, dimensions={0} | all-to-all | bytes 1048576 | tf_op jit(solution)/shard_map/all_to_all | solution.py:59
  80.0 0.1 reduce_sum.49
  80.1 20.4 %all_to_all.31 = bf16[12,6,512]{2,1,0:T(8,128)(2,1)S(1)} all-to-all(bf16[12,6,512]{2,1,0:T(8,128)(2,1)S(1)} %reshape.67), channel_id=1, replica_groups=mesh['x'=4,'yh'=2,'yl'=4,'z'=12,'c'=2] {'z'}, dimensions={0} | all-to-all | bytes 147456 | tf_op jit(solution)/shard_map/all_to_all | solution.py:63
  100.6 12.5 %all_to_all.32 = bf16[12,6,512]{2,1,0:T(8,128)(2,1)S(1)} all-to-all(bf16[12,6,512]{2,1,0:T(8,128)(2,1)S(1)} %broadcast_in_dim.14), channel_id=1, replica_groups=mesh['x'=4,'yh'=2,'yl'=4,'z'=12,'c'=2] {'z'}, dimensions={0} | all-to-all | bytes 147456 | tf_op jit(solution)/shard_map/all_to_all | solution.py:13
  113.1 0.0 all-gather.2.cloned.1.call-done
  113.1 7.2 %collective-permute-start.1 = (bf16[2048,512]{1,0:T(8,128)(2,1)}, bf16[2048,512]{1,0:T(8,128)(2,1)S(1)}, u32[]{:S(2)}, u32[]{:S(2)}) collective-permute-start(bf16[2048,512]{1,0:T(8,128)(2,1)} %all-gather.2.cloned.1.call-done), channel_id=1, source_target_pairs={{0,1},{1,0},{2,3},{3,2},{4,5},{5,4},{6,7},{7,6},{8,9},{9,8},{10,11... | collective-permute-start | bytes 6291464 | tf_op jit(solution)/shard_map/ppermute | solution.py:69
  120.3 0.7 broadcast_in_dim.15
  121.1 3.4 %all-to-all-start.4 = ((bf16[4,64,512]{2,1,0:T(8,128)(2,1)}), bf16[4,64,512]{2,1,0:T(8,128)(2,1)S(1)}, u32[]{:S(2)}, u32[]{:S(2)}) async-start(bf16[4,64,512]{2,1,0:T(8,128)(2,1)} %broadcast_in_dim.15), calls=%async_computation.4 | async-start | bytes 524288 | tf_op jit(solution)/shard_map/all_to_all | solution.py:13
  124.5 8.0 %all-to-all-done.4 = bf16[4,64,512]{2,1,0:T(8,128)(2,1)S(1)} async-done(((bf16[4,64,512]{2,1,0:T(8,128)(2,1)}), bf16[4,64,512]{2,1,0:T(8,128)(2,1)S(1)}, u32[]{:S(2)}, u32[]{:S(2)}) %all-to-all-start.4) | async-done | bytes 262176 | tf_op jit(solution)/shard_map/all_to_all | solution.py:13
  132.5 0.0 collective-permute-done.1
  132.5 3.7 %collective-permute-start.2 = (bf16[256,512]{1,0:T(8,128)(2,1)S(1)}, bf16[256,512]{1,0:T(8,128)(2,1)S(1)}, u32[]{:S(2)}, u32[]{:S(2)}) collective-permute-start(bf16[256,512]{1,0:T(8,128)(2,1)S(1)} %bitcast.43), channel_id=1, source_target_pairs={{0,1},{1,0},{2,3},{3,2},{4,5},{5,4},{6,7},{7,6},{8,9},{9,8},{10,11... | collective-permute-start | bytes 786440 | tf_op jit(solution)/shard_map/ppermute | solution.py:72
  136.2 1.9 %broadcast_select_fusion.1 = (bf16[2048,512]{1,0:T(8,128)(2,1)S(1)}, bf16[2048,512]{1,0:T(8,128)(2,1)S(1)}) fusion(bf16[2048,512]{1,0:T(8,128)(2,1)} %all-gather.2.cloned.1.call-done, bf16[2048,512]{1,0:T(8,128)(2,1)S(1)} %collective-permute-done.1, pred[]{:T(512)S(6)} %eq.7), kind=kLoop, calls=%fused_computation.11 | loop fusion | flops 2097152 | bytes 8388609 | tf_op jit(solution)/shard_map/jit(_where)/select_n | solution.py:18
  138.1 0.0 copy-start.4
  138.1 0.4 pad_maximum_fusion
  138.5 0.0 copy-start.2
  138.5 0.8 copy-done.4
  139.3 0.0 copy-start.1
  139.3 1.3 fusion.12
  140.6 0.0 copy-done.2
  140.6 0.0 copy-start.6
  140.6 0.0 collective-permute-done.2
  140.7 0.5 copy-done.1
  141.1 1.0 fusion.7
  142.2 0.6 broadcast_in_dim.17
  142.8 3.3 %all-to-all-start.5 = ((f32[8,4,128]{2,1,0:T(4,128)}), f32[8,4,128]{2,1,0:T(4,128)S(1)}, u32[]{:S(2)}, u32[]{:S(2)}) async-start(f32[8,4,128]{2,1,0:T(4,128)} %broadcast_in_dim.17), calls=%async_computation.5 | async-start | bytes 32768 | tf_op jit(solution)/shard_map/all_to_all | solution.py:13
  146.1 0.0 copy-done.6
  146.1 3.4 %fusion.2 = bf16[128,4096]{0,1:T(8,128)(2,1)S(1)} fusion(bf16[4096,512]{1,0:T(8,128)(2,1)} %bitcast.38, bf16[128,512]{1,0:T(8,128)(2,1)S(1)} %copy-done.6, bf16[128,4096]{0,1:T(8,128)(2,1)S(1)} %copy.28, f32[128]{0:T(128)S(1)} %broadcast_multiply_fusion, f32[128]{0:T(128)S(1)} %add_rsqrt_fusion), kind=kOutput, calls=%fused_computation.3 | convolution fusion | flops 540016640 | bytes 6423552 | tf_op jit(solution)/shard_map/dot_general | solution.py:83
  149.6 1.3 copy.35
  150.9 0.8 copy.34
  151.7 3.4 %all-to-all-done.5 = f32[8,4,128]{2,1,0:T(4,128)S(1)} async-done(((f32[8,4,128]{2,1,0:T(4,128)}), f32[8,4,128]{2,1,0:T(4,128)S(1)}, u32[]{:S(2)}, u32[]{:S(2)}) %all-to-all-start.5) | async-done | bytes 16416 | tf_op jit(solution)/shard_map/all_to_all | solution.py:13
  155.0 0.6 copy.38
  (12 shorter events, 0.2 us)
Async XLA Ops:
  7.2 1.6 %copy-start.3 = (bf16[128,4096]{1,0:T(8,128)(2,1)S(1)}, bf16[128,4096]{1,0:T(8,128)(2,1)}, u32[]{:S(2)}) copy-start(bf16[128,4096]{1,0:T(8,128)(2,1)} %param.5) | copy-start | bytes 3145732
  8.8 1.3 copy-start.5
  9.5 0.8 copy-start.7
  11.6 1.0 copy-start
  14.3 40.4 %all-to-all-start = ((bf16[8,128,1024]{1,2,0:T(8,128)(2,1)}), bf16[8,128,1024]{1,2,0:T(8,128)(2,1)S(1)}, u32[]{:S(2)}, u32[]{:S(2)}) async-start(bf16[8,128,1024]{1,2,0:T(8,128)(2,1)} %pad_maximum_fusion.1), calls=%async_computation | async-start | bytes 4194304 | tf_op jit(solution)/shard_map/all_to_all | solution.py:45
  28.3 84.8 %all-gather.2.cloned.1.call-start = ((), (), s32[]{:S(2)}) async-start(), calls=%async_computation.6 | async-start | bytes 2621440 | tf_op jit(solution)/shard_map/all_gather | solution.py:52
  28.3 15.2 %collective-permute-start = (bf16[256,512]{1,0:T(8,128)(2,1)S(1)}, bf16[256,512]{1,0:T(8,128)(2,1)}, u32[]{:S(2)}, u32[]{:S(2)}) collective-permute-start(bf16[256,512]{1,0:T(8,128)(2,1)S(1)} %fusion.10), channel_id=1, source_target_pairs={{0,96},{96,0},{1,97},{97,1},{2,98},{98,2},{3,99},{99,3},{4,100},{1... | collective-permute-start | bytes 786440 | tf_op jit(solution)/shard_map/ppermute | solution.py:44
  113.1 19.3 %collective-permute-start.1 = (bf16[2048,512]{1,0:T(8,128)(2,1)}, bf16[2048,512]{1,0:T(8,128)(2,1)S(1)}, u32[]{:S(2)}, u32[]{:S(2)}) collective-permute-start(bf16[2048,512]{1,0:T(8,128)(2,1)} %all-gather.2.cloned.1.call-done), channel_id=1, source_target_pairs={{0,1},{1,0},{2,3},{3,2},{4,5},{5,4},{6,7},{7,6},{8,9},{9,8},{10,11... | collective-permute-start | bytes 6291464 | tf_op jit(solution)/shard_map/ppermute | solution.py:69
  121.1 11.4 %all-to-all-start.4 = ((bf16[4,64,512]{2,1,0:T(8,128)(2,1)}), bf16[4,64,512]{2,1,0:T(8,128)(2,1)S(1)}, u32[]{:S(2)}, u32[]{:S(2)}) async-start(bf16[4,64,512]{2,1,0:T(8,128)(2,1)} %broadcast_in_dim.15), calls=%async_computation.4 | async-start | bytes 524288 | tf_op jit(solution)/shard_map/all_to_all | solution.py:13
  132.5 8.1 %collective-permute-start.2 = (bf16[256,512]{1,0:T(8,128)(2,1)S(1)}, bf16[256,512]{1,0:T(8,128)(2,1)S(1)}, u32[]{:S(2)}, u32[]{:S(2)}) collective-permute-start(bf16[256,512]{1,0:T(8,128)(2,1)S(1)} %bitcast.43), channel_id=1, source_target_pairs={{0,1},{1,0},{2,3},{3,2},{4,5},{5,4},{6,7},{7,6},{8,9},{9,8},{10,11... | collective-permute-start | bytes 786440 | tf_op jit(solution)/shard_map/ppermute | solution.py:72
  138.1 1.2 copy-start.4
  138.5 2.1 %copy-start.2 = (bf16[8,2,256,512]{3,2,1,0:T(8,128)(2,1)}, bf16[8,2,256,512]{3,2,1,0:T(8,128)(2,1)S(1)}, u32[]{:S(2)}) copy-start(bf16[8,2,256,512]{3,2,1,0:T(8,128)(2,1)S(1)} %pad_maximum_fusion) | copy-start | bytes 12582916
  139.3 1.9 %copy-start.1 = (f32[512,512]{1,0:T(8,128)S(1)}, f32[512,512]{1,0:T(8,128)}, u32[]{:S(2)}) copy-start(f32[512,512]{1,0:T(8,128)} %copy-done) | copy-start | bytes 3145732
  140.6 5.5 %copy-start.6 = (bf16[128,512]{1,0:T(8,128)(2,1)S(1)}, bf16[128,512]{1,0:T(8,128)(2,1)}, u32[]{:S(2)}) copy-start(bf16[128,512]{1,0:T(8,128)(2,1)} %param.9) | copy-start | bytes 393220
  142.8 12.2 %all-to-all-start.5 = ((f32[8,4,128]{2,1,0:T(4,128)}), f32[8,4,128]{2,1,0:T(4,128)S(1)}, u32[]{:S(2)}, u32[]{:S(2)}) async-start(f32[8,4,128]{2,1,0:T(4,128)} %broadcast_in_dim.17), calls=%async_computation.5 | async-start | bytes 32768 | tf_op jit(solution)/shard_map/all_to_all | solution.py:13
Sparse Core Ops, SparseCore 0:
  56.7 35.7 all-gather.1

commit v2 on v1

v2 whole, which is shorter than its diff:
```python
import jax
import jax.numpy as jnp
from jax import lax
from jax.experimental import pallas as pl
from jax.experimental.pallas import tpu as pltpu
from jax.sharding import Mesh
from jax.sharding import PartitionSpec as P

F32 = jnp.float32
BF16 = jnp.bfloat16
VMEM = pl.BlockSpec(memory_space=pltpu.VMEM)
SMEM = pl.BlockSpec(memory_space=pltpu.SMEM)
PARAMS = pltpu.CompilerParams(vmem_limit_bytes=40 * 1024 * 1024)
SWAP = [(0, 1), (1, 0)]


def shape(dims, dtype):
    return jax.ShapeDtypeStruct(dims, dtype)


def prepare_kernel(hidden_ref, cot_ref, sent_ref, inv_ref):
    peers, tok, wide = sent_ref.shape
    cols = cot_ref.shape[1]
    part = wide - cols
    square = jnp.zeros((tok, 1), F32)
    for i in range(peers):
        piece = hidden_ref[:, i * part : (i + 1) * part]
        sent_ref[i, :, :part] = piece
        piece = piece.astype(F32)
        square = square + jnp.sum(piece * piece, axis=1, keepdims=True)
    inv = lax.rsqrt(square / (peers * part) + 1e-05)
    inv_ref[...] = inv
    scaled = (cot_ref[...].astype(F32) * inv).astype(BF16)
    for i in range(peers):
        sent_ref[i, :, part:] = scaled


def product_kernel(core_ref, got_ref, keep_ref, send_ref):
    peers, tok, wide = got_ref.shape
    groups, half, cols = keep_ref.shape
    part = wide - cols
    core = core_ref[0]
    cot = got_ref[:, :, part:].reshape(peers * tok, cols)
    for out_ref, which in ((send_ref, 1 - core), (keep_ref, core)):
        for g in range(groups):
            at = pl.multiple_of(g * 2 * half + which * half, half)
            left = got_ref[:, :, pl.ds(at, half)].reshape(peers * tok, half)
            value = lax.dot_general(left, cot, (((0,), (0,)), ((), ())), preferred_element_type=F32)
            out_ref[g] = value.astype(out_ref.dtype)


def finish_kernel(core_ref, own_ref, other_ref, weight_ref, gain_ref, grad_ref, part_ref):
    half = own_ref.shape[0]
    core = core_ref[0]
    for ref, which in ((own_ref, core), (other_ref, 1 - core)):
        rows = pl.ds(pl.multiple_of(which * half, half), half)
        value = ref[...].astype(F32)
        grad_ref[rows, :] = (value * gain_ref[rows, :]).astype(BF16)
        dots = jnp.sum(value * weight_ref[rows, :].astype(F32), axis=1, keepdims=True)
        part_ref[:, rows] = jnp.broadcast_to(dots, (half, 128)).T[:8]


def tokens_kernel(core_ref, hidden_ref, inv_ref, cot_ref, own_ref, other_ref, keys_ref, grad_ref):
    shifts, pairs, half, cols = own_ref.shape
    width = hidden_ref.shape[1]
    core, here = core_ref[0], core_ref[1]
    inv = inv_ref[...]
    cot = cot_ref[...]
    places = []
    for s in range(shifts):
        x = lax.rem(here - s + shifts, shifts)
        for g in range(pairs):
            for ref, which in ((own_ref, core), (other_ref, 1 - core)):
                at = pl.multiple_of(((x * pairs + g) * 2 + which) * half, half)
                places.append((ref.at[s, g], pl.ds(at, half)))
    keys = jnp.zeros(keys_ref.shape, F32)
    for ref, columns in places:
        keys = keys + jnp.dot(hidden_ref[:, columns], ref[...], preferred_element_type=F32)
    keys = keys * inv
    keys_ref[...] = keys.astype(BF16)
    mean = jnp.sum(keys * cot.astype(F32), axis=1, keepdims=True) / width
    for ref, columns in places:
        value = lax.dot_general(cot, ref[...], (((1,), (1,)), ((), ())), preferred_element_type=F32)
        unit = hidden_ref[:, columns].astype(F32) * inv
        grad_ref[:, columns] = (inv * (value - unit * mean)).astype(BF16)


def call(kernel, outs, specs, flops, moved):
    return pl.pallas_call(
        kernel,
        out_shape=outs,
        in_specs=specs,
        out_specs=jax.tree.map(lambda _: VMEM, outs),
        compiler_params=PARAMS,
        cost_estimate=pl.CostEstimate(flops=flops, bytes_accessed=moved, transcendentals=0),
    )


def spread(value, axes, size):
    copies = jnp.broadcast_to(value[None], (size,) + value.shape)
    return lax.all_to_all(copies, axes, 0, 0)


def tie(*values):
    return lax.optimization_barrier(values)


def body(hidden_in, norm_gain, key_codes, key_scales, key_cotangent):
    nx, nh, nl, nz, nc = (lax.axis_size(a) for a in ("x", "yh", "yl", "z", "c"))
    tok, width = hidden_in.shape
    rows, cols = key_codes.shape
    block = cols // key_scales.shape[1]
    total_tokens = tok * nx * nh * nl * nz * nc
    half = rows // nc
    core = lax.axis_index("c")
    core_at = jnp.stack([core, lax.axis_index("x")]).astype(jnp.int32)
    part = width // nx

    sent, inv = call(
        prepare_kernel,
        [shape((nx, tok, part + cols), BF16), shape((tok, 1), F32)],
        [VMEM, VMEM],
        4 * tok * width,
        4 * tok * width,
    )(hidden_in, key_cotangent)
    sent, key_codes = tie(sent, key_codes)
    got = lax.all_to_all(sent, "x", 0, 0)

    gain = norm_gain.astype(F32)[:, None]
    scales = jnp.repeat(key_scales.astype(F32), block, axis=1)
    scaled = key_codes.astype(F32) * scales
    weight = scaled.astype(BF16)
    mine = lax.dynamic_slice_in_dim((scaled * gain).astype(BF16), core * half, half, 0)
    mate = lax.ppermute(mine, "yh", SWAP)
    low = lax.axis_index("yh") == 0
    got, mine, mate, weight = tie(got, mine, mate, weight)

    keep, send = call(
        product_kernel,
        [shape((nh, half, cols), F32), shape((nh, half, cols), BF16)],
        [SMEM, VMEM],
        2 * nx * tok * part * cols,
        2 * nx * tok * (part + cols) + 6 * nh * half * cols,
    )(core_at, got)
    passed = lax.ppermute(send, "c", SWAP)
    pair = jnp.stack([jnp.where(low, mine, mate), jnp.where(low, mate, mine)])
    passed, pair = tie(passed, pair)
    product = (keep + passed.astype(F32)).astype(BF16)

    quarter = half // nl
    product, pair = tie(product.reshape(nh * nl, quarter, cols), pair)
    own = [pair]
    for s in range(1, nx):
        own.append(lax.ppermute(pair, "x", [(i, (i + s) % nx) for i in range(nx)]))
    terms = lax.all_to_all(product, ("yh", "yl"), 0, 0)
    summed = jnp.sum(terms.astype(F32), axis=0).astype(BF16)
    piece = -(-quarter // nz)
    summed = jnp.pad(summed, ((0, piece * nz - quarter), (0, 0))).reshape(nz, piece, cols)
    total = jnp.sum(lax.all_to_all(summed, "z", 0, 0).astype(F32), axis=0)
    scale = 1.0 / jnp.sqrt(F32(total_tokens))
    total = (total * scale).astype(BF16)

    whole = spread(total, "z", nz).reshape(nz * piece, cols)[:quarter]
    whole, *own = tie(whole, *own)
    own_half = jnp.stack(own)
    other_half = lax.ppermute(own_half, "c", SWAP)
    whole = spread(whole, "yl", nl).reshape(half, cols)
    passed = lax.ppermute(whole, "c", SWAP)
    weight_grad, gain_part = call(
        finish_kernel,
        [shape((rows, cols), BF16), shape((8, rows), F32)],
        [SMEM, VMEM, VMEM, VMEM, VMEM],
        4 * rows * cols,
        6 * rows * cols,
    )(core_at, whole, passed, weight, gain)
    gain_part, own_half, other_half = tie(gain_part[0].reshape(-1, 128), own_half, other_half)
    gain_gradient = spread(gain_part, ("x", "yh"), nx * nh).reshape(width)

    keys_out, input_gradient = call(
        tokens_kernel,
        [shape((tok, cols), BF16), shape((tok, width), BF16)],
        [SMEM, VMEM, VMEM, VMEM, VMEM, VMEM],
        4 * tok * width * cols,
        4 * tok * width + 2 * width * cols,
    )(core_at, hidden_in, inv, key_cotangent, own_half, other_half)
    return (keys_out, input_gradient, weight_grad, gain_gradient)


def solution(mesh):
    fine = Mesh(mesh.devices.reshape(4, 2, 4, 12, 2), ("x", "yh", "yl", "z", "c"))
    tokens = P(("x", "yh", "yl", "z", "c"), None)
    group = ("x", "yh")
    in_specs = (tokens, P(group), P(group, None), P(group, None), tokens)
    out_specs = (tokens, tokens, P(group, None), P())
    return jax.shard_map(body, mesh=fine, in_specs=in_specs, out_specs=out_specs, check_vma=False)
```

time: 163 us -> 149 us (0.914)
  starting transfers between devices: 33.6 us -> 60.6 us
  waiting for transfers between devices: 35.8 us -> 12.9 us
  between operations: 14.4 us -> 0.91 us
  Pallas kernels: 0 us -> 9.55 us
  matrix products: 7.01 us -> 0 us
  other arithmetic: 8.64 us -> 3.99 us
  blocking collectives: 51.5 us -> 49.3 us
    ppermute x3 -> x7, starting transfers between devices: 12.8 us -> 36.8 us  [the longest x1 14.3 us: body(): passed = lax.ppermute(send, 'c', SWAP)]
    all_to_all x2 -> x1, blocking collectives: 39 us -> 19.8 us  [body(): terms = lax.all_to_all(product, ('yh', 'yl'), 0, 0)]
    all_to_all x1 -> x2, blocking collectives: 12.5 us -> 29.6 us  [spread(): return lax.all_to_all(copies, axes, 0, 0)]
    all_to_all x1 -> x2, waiting for transfers between devices: 11.1 us -> 0.52 us  [the longest x1 0.52 us: body(): total = jnp.sum(lax.all_to_all(summed, 'z', 0, 0).astype(F32), axis=0)]
    pallas_call x0 -> x4, Pallas kernels: none -> 9.55 us  [the longest x1 4.78 us: body(): call(tokens_kernel, [shape((tok, cols), BF16), shape((tok, width), BF16)]...]
    all_to_all x2 -> x1, waiting for transfers between devices: 11.3 us -> 3.34 us  [spread(): return lax.all_to_all(copies, axes, 0, 0)]
    dot_general x3 -> x0, matrix products: 7.01 us -> none  [the longest x1 3.44 us: body(): lax.dot_general(key_cotangent, gained, (((1,), (1,)), ((), ())), preferre...]
    all_to_all x1 -> x2, starting transfers between devices: 14 us -> 19.8 us  [the longest x1 14.9 us: body(): total = jnp.sum(lax.all_to_all(summed, 'z', 0, 0).astype(F32), axis=0)]
  transfers between devices with their start and end apart: 7 -> 10, of which waited for: 4 -> 6; matrix products, arithmetic and copies ran while one was open for 9% -> 3% of each run, Pallas kernels for 0% -> 5%
where the time goes in v2:
time: 149 us; the launch traced here: 148 us
  starting transfers between devices  60.6 us (41%)
  blocking collectives  49.3 us (33%)
  waiting for transfers between devices  12.9 us (9%)
  local copies, waits for them, and re-layouts  10.9 us (7%)
  Pallas kernels  9.55 us (6%)
  other arithmetic  3.99 us (3%)
    all_to_all x2, blocking collectives, spread(): return lax.all_to_all(copies, axes, 0, 0)  29.6 us
    all_to_all x1, blocking collectives, body(): terms = lax.all_to_all(product, ('yh', 'yl'), 0, 0)  19.8 us
    all_to_all x1, starting transfers between devices, body(): total = jnp.sum(lax.all_to_all(summed, 'z', 0, 0).astype(F32), axis=0)  14.9 us
    ppermute x1, starting transfers between devices, body(): passed = lax.ppermute(send, 'c', SWAP)  14.3 us
    ppermute x3, starting transfers between devices, body(): own.append(lax.ppermute(pair, 'x', [(i, (i + s) % nx) for i in range(nx)]))  9.56 us
    unnamed x30, local copies, waits for them, and re-layouts  7.88 us
    ppermute x1, starting transfers between devices, body(): mate = lax.ppermute(mine, 'yh', SWAP)  7.45 us
    all_to_all x1, starting transfers between devices, body(): got = lax.all_to_all(sent, 'x', 0, 0)  4.84 us
  transfers between devices with their start and end apart: 10, of which 6 were waited for; matrix products, arithmetic and copies ran while one was open for 3% of the time, Pallas kernels for 5%

profile of v2, /device:TPU:1, one launch (start us, length us, event | category | flops | bytes accessed | tf_op | source)
XLA Modules:
  0.0 148.1 jit_solution(3140045091755043932)
XLA Ops:
  0.6 0.0 copy-start
  0.6 1.2 copy-done
  1.9 0.0 copy-start.4
  1.9 0.9 copy-done.4
  2.8 0.0 copy-start.13
  2.8 1.5 %shard_map.84 = (bf16[4,128,1536]{2,1,0:T(8,128)(2,1)}, f32[128,1]{1,0:T(8,128)S(1)}) custom-call(bf16[128,4096]{1,0:T(8,128)(2,1)S(1)} %copy-done, bf16[128,512]{1,0:T(8,128)(2,1)S(1)} %copy-done.4), custom_call_target="tpu_custom_call" | custom-call | flops 2097152 | bytes 2097152 | tf_op jit(solution)/shard_map/pallas_call | solution.py:119
  4.2 0.0 copy-start.6
  4.2 0.6 copy-done.6
  4.9 4.8 %all-to-all-start = ((bf16[4,128,1536]{2,1,0:T(8,128)(2,1)}), bf16[4,128,1536]{2,1,0:T(8,128)(2,1)S(1)}, u32[]{:S(2)}, u32[]{:S(2)}) async-start(bf16[4,128,1536]{2,1,0:T(8,128)(2,1)} %get-tuple-element.32), calls=%async_computation | async-start | bytes 3145728 | tf_op jit(solution)/shard_map/all_to_all | solution.py:127
  9.7 0.0 copy-done.13
  9.7 0.2 copy.12
  9.9 0.6 broadcast_in_dim.10
  10.5 0.1 copy.14
  10.6 0.0 copy-done.12
  10.6 0.1 dynamic-slice
  10.7 0.1 copy-done.9
  10.8 1.0 fusion.1
  11.8 0.1 fusion
  11.9 7.5 %collective-permute-start = (bf16[256,512]{1,0:T(8,128)(2,1)S(1)}, bf16[256,512]{1,0:T(8,128)(2,1)S(1)}, u32[]{:S(2)}, u32[]{:S(2)}) collective-permute-start(bf16[256,512]{1,0:T(8,128)(2,1)S(1)} %fusion), channel_id=1, source_target_pairs={{0,96},{96,0},{1,97},{97,1},{2,98},{98,2},{3,99},{99,3},{4,100},{1... | collective-permute-start | bytes 786440 | tf_op jit(solution)/shard_map/ppermute | solution.py:134
  19.3 0.1 pad_add_fusion.core_ref
  19.4 3.8 %collective-permute-done = bf16[256,512]{1,0:T(8,128)(2,1)S(1)} collective-permute-done((bf16[256,512]{1,0:T(8,128)(2,1)S(1)}, bf16[256,512]{1,0:T(8,128)(2,1)S(1)}, u32[]{:S(2)}, u32[]{:S(2)}) %collective-permute-start) | collective-permute-done | bytes 262176 | tf_op jit(solution)/shard_map/ppermute | solution.py:134
  23.2 0.0 all-to-all-done.got_ref
  23.2 0.7 copy-done.11
  23.9 1.3 shard_map.85
  25.2 14.3 %collective-permute-start.1 = (bf16[2,256,512]{2,1,0:T(8,128)(2,1)S(1)}, bf16[2,256,512]{2,1,0:T(8,128)(2,1)S(1)}, u32[]{:S(2)}, u32[]{:S(2)}) collective-permute-start(bf16[2,256,512]{2,1,0:T(8,128)(2,1)S(1)} %get-tuple-element.36), channel_id=1, source_target_pairs={{0,1},{1,0},{2,3},{3,2},{4,5},{5,4},{6,7},{7,6},{8,9},{9,8},{10,11... | collective-permute-start | bytes 1572872 | tf_op jit(solution)/shard_map/ppermute | solution.py:145
  39.5 1.0 select_bitcast_fusion.1
  40.5 0.1 pad_maximum_fusion.1
  40.5 0.0 copy-start.8
  40.5 0.4 collective-permute-done.1
  41.0 0.2 add_convert_fusion
  41.2 19.8 %all_to_all.30 = bf16[8,64,512]{2,1,0:T(8,128)(2,1)S(1)} all-to-all(bf16[8,64,512]{2,1,0:T(8,128)(2,1)S(1)} %bitcast.21), channel_id=1, replica_groups=mesh['x'=4,'yh'=2,'yl'=4,'z'=12,'c'=2] {'yh','yl'}, dimensions={0} | all-to-all | bytes 1048576 | tf_op jit(solution)/shard_map/all_to_all | solution.py:155
  60.9 0.1 reduce_sum.21
  61.0 0.7 reshape.35
  61.7 14.9 %all-to-all-start.2 = ((bf16[12,6,512]{2,1,0:T(8,128)(2,1)}), bf16[12,6,512]{2,1,0:T(8,128)(2,1)S(1)}, u32[]{:S(2)}, u32[]{:S(2)}) async-start(bf16[12,6,512]{2,1,0:T(8,128)(2,1)} %reshape.35), calls=%async_computation.2 | async-start | bytes 196608 | tf_op jit(solution)/shard_map/all_to_all | solution.py:159
  76.6 4.6 %collective-permute-start.4 = (bf16[2,256,512]{2,1,0:T(8,128)(2,1)S(1)}, bf16[2,256,512]{2,1,0:T(8,128)(2,1)S(1)}, u32[]{:S(2)}, u32[]{:S(2)}) collective-permute-start(bf16[2,256,512]{2,1,0:T(8,128)(2,1)S(1)} %pad_maximum_fusion.1), channel_id=1, source_target_pairs={{0,576},{192,0},{384,192},{576,384},{1,577},{193,1},{385,193},{577... | collective-permute-start | bytes 1572872 | tf_op jit(solution)/shard_map/ppermute | solution.py:154
  81.2 2.5 %collective-permute-start.3 = (bf16[2,256,512]{2,1,0:T(8,128)(2,1)S(1)}, bf16[2,256,512]{2,1,0:T(8,128)(2,1)S(1)}, u32[]{:S(2)}, u32[]{:S(2)}) collective-permute-start(bf16[2,256,512]{2,1,0:T(8,128)(2,1)S(1)} %pad_maximum_fusion.1), channel_id=1, source_target_pairs={{0,384},{192,576},{384,0},{576,192},{1,385},{193,577},{385,1},{577... | collective-permute-start | bytes 1572872 | tf_op jit(solution)/shard_map/ppermute | solution.py:154
  83.7 0.0 copy-done.8
  83.7 2.5 %collective-permute-start.2 = (bf16[2,256,512]{2,1,0:T(8,128)(2,1)S(1)}, bf16[2,256,512]{2,1,0:T(8,128)(2,1)S(1)}, u32[]{:S(2)}, u32[]{:S(2)}) collective-permute-start(bf16[2,256,512]{2,1,0:T(8,128)(2,1)S(1)} %pad_maximum_fusion.1), channel_id=1, source_target_pairs={{0,192},{192,384},{384,576},{576,0},{1,193},{193,385},{385,577},{5... | collective-permute-start | bytes 1572872 | tf_op jit(solution)/shard_map/ppermute | solution.py:154
  86.2 0.5 all-to-all-done.2
  86.8 18.5 %all_to_all.31 = bf16[12,6,512]{2,1,0:T(8,128)(2,1)S(1)} all-to-all(bf16[12,6,512]{2,1,0:T(8,128)(2,1)S(1)} %broadcast_in_dim.11), channel_id=1, replica_groups=mesh['x'=4,'yh'=2,'yl'=4,'z'=12,'c'=2] {'z'}, dimensions={0} | all-to-all | bytes 147456 | tf_op jit(solution)/shard_map/all_to_all | solution.py:101
  105.3 0.0 collective-permute-done.4
  105.3 0.0 collective-permute-done.3
  105.3 4.4 %collective-permute-done.2 = bf16[2,256,512]{2,1,0:T(8,128)(2,1)S(1)} collective-permute-done((bf16[2,256,512]{2,1,0:T(8,128)(2,1)S(1)}, bf16[2,256,512]{2,1,0:T(8,128)(2,1)S(1)}, u32[]{:S(2)}, u32[]{:S(2)}) %collective-permute-start.2) | collective-permute-done | bytes 524320 | tf_op jit(solution)/shard_map/ppermute | solution.py:154
  109.7 0.8 copy-done.10
  110.5 1.5 %pad_maximum_fusion.own_ref = bf16[4,2,256,512]{3,2,1,0:T(8,128)(2,1)S(1)} fusion(bf16[1,2,256,512]{3,2,1,0:T(8,128)(2,1)S(1)} %bitcast.23, bf16[1,2,256,512]{3,2,1,0:T(8,128)(2,1)S(1)} %bitcast.24, bf16[1,2,256,512]{3,2,1,0:T(8,128)(2,1)} %bitcast.25, bf16[1,2,256,512]{3,2,1,0:T(8,128)(2,1)} %bitcast.22), kind=kLoop, calls=%fused_computation | loop fusion | flops 3145728 | bytes 4194304 | tf_op jit(solution)/shard_map/stack | solution.py:165
  112.0 0.0 copy-start.1
  112.0 2.5 %collective-permute-start.6 = (bf16[4,2,256,512]{3,2,1,0:T(8,128)(2,1)S(1)}, bf16[4,2,256,512]{3,2,1,0:T(8,128)(2,1)}, u32[]{:S(2)}, u32[]{:S(2)}) collective-permute-start(bf16[4,2,256,512]{3,2,1,0:T(8,128)(2,1)S(1)} %pad_maximum_fusion.own_ref), channel_id=1, source_target_pairs={{0,1},{1,0},{2,3},{3,2},{4,5},{5,4},{6,7},{7,6},{8,9},{9,8},{10,11... | collective-permute-start | bytes 6291464 | tf_op jit(solution)/shard_map/ppermute | solution.py:166
  114.6 11.1 %all_to_all.32 = bf16[4,64,512]{2,1,0:T(8,128)(2,1)S(1)} all-to-all(bf16[4,64,512]{2,1,0:T(8,128)(2,1)S(1)} %broadcast_in_dim.12), channel_id=1, replica_groups=mesh['x'=4,'yh'=2,'yl'=4,'z'=12,'c'=2] {'yl'}, dimensions={0} | all-to-all | bytes 524288 | tf_op jit(solution)/shard_map/all_to_all | solution.py:101
  125.7 3.0 %collective-permute-start.5 = (bf16[256,512]{1,0:T(8,128)(2,1)S(1)}, bf16[256,512]{1,0:T(8,128)(2,1)}, u32[]{:S(2)}, u32[]{:S(2)}) collective-permute-start(bf16[256,512]{1,0:T(8,128)(2,1)S(1)} %bitcast.17), channel_id=1, source_target_pairs={{0,1},{1,0},{2,3},{3,2},{4,5},{5,4},{6,7},{7,6},{8,9},{9,8},{10,11... | collective-permute-start | bytes 786440 | tf_op jit(solution)/shard_map/ppermute | solution.py:168
  128.7 0.9 copy.13.gain_ref
  129.5 0.4 collective-permute-done.5.other_ref
  129.9 1.0 copy-done.2
  131.0 0.9 copy-done.3
  131.9 2.0 %shard_map.86 = (bf16[512,512]{1,0:T(8,128)(2,1)}, f32[8,512]{1,0:T(8,128)S(1)}) custom-call(s32[2]{0:T(128)S(1)} %pad_add_fusion.core_ref, bf16[256,512]{1,0:T(8,128)(2,1)S(1)} %bitcast.18, bf16[256,512]{1,0:T(8,128)(2,1)} %collective-permute-done.5.other_ref, bf16[512,512]{1,0:T(8,128)(2,1)S(1)} %copy-done.2, f32[512,1]{1,0:T(8,128)S(1)} %copy-done.3), custom_call_target="tpu_custom_call" | custom-call | flops 1048576 | bytes 1572864 | tf_op jit(solution)/shard_map/pallas_call | solution.py:169
  134.0 0.0 collective-permute-done.6.other_ref
  134.0 0.6 broadcast_in_dim.28
  134.6 4.0 %all-to-all-start.5 = ((f32[8,4,128]{2,1,0:T(4,128)}), f32[8,4,128]{2,1,0:T(4,128)S(1)}, u32[]{:S(2)}, u32[]{:S(2)}) async-start(f32[8,4,128]{2,1,0:T(4,128)} %broadcast_in_dim.28), calls=%async_computation.5 | async-start | bytes 32768 | tf_op jit(solution)/shard_map/all_to_all | solution.py:101
  138.5 0.0 copy-done.5
  138.5 0.0 copy-done.1
  138.6 0.0 copy-start.7
  138.6 0.8 copy-done.7
  139.4 4.8 %shard_map.87 = (bf16[128,512]{1,0:T(8,128)(2,1)}, bf16[128,4096]{1,0:T(8,128)(2,1)}) custom-call(s32[2]{0:T(128)S(1)} %pad_add_fusion.core_ref, bf16[128,4096]{1,0:T(8,128)(2,1)S(1)} %copy-done.1, f32[128,1]{1,0:T(8,128)S(1)} %copy-done.7, bf16[128,512]{1,0:T(8,128)(2,1)S(1)} %copy-done.5, bf16[4,2,256,512]{3,2,1,0:T(8,128)(2,1)S(1)} %pad_maximum_fusion.own_ref, ...), custom_call_target="tpu_custom_call" | custom-call | flops 1073741824 | bytes 6291456 | tf_op jit(solution)/shard_map/pallas_call | solution.py:179
  144.2 3.3 %all-to-all-done.5 = f32[8,4,128]{2,1,0:T(4,128)S(1)} async-done(((f32[8,4,128]{2,1,0:T(4,128)}), f32[8,4,128]{2,1,0:T(4,128)S(1)}, u32[]{:S(2)}, u32[]{:S(2)}) %all-to-all-start.5) | async-done | bytes 16416 | tf_op jit(solution)/shard_map/all_to_all | solution.py:101
  147.5 0.6 copy.16
  (16 shorter events, 0.1 us)
Async XLA Ops:
  0.6 1.2 copy-start
  1.9 0.9 copy-start.4
  2.8 7.0 %copy-start.13 = (bf16[512,2]{0,1:T(2,128)(2,1)S(1)}, bf16[512,2]{0,1:T(2,128)(2,1)}, u32[]{:S(2)}) copy-start(bf16[512,2]{0,1:T(2,128)(2,1)} %param.8) | copy-start | bytes 6148
  4.2 0.6 copy-start.6
  4.9 18.3 %all-to-all-start = ((bf16[4,128,1536]{2,1,0:T(8,128)(2,1)}), bf16[4,128,1536]{2,1,0:T(8,128)(2,1)S(1)}, u32[]{:S(2)}, u32[]{:S(2)}) async-start(bf16[4,128,1536]{2,1,0:T(8,128)(2,1)} %get-tuple-element.32), calls=%async_computation | async-start | bytes 3145728 | tf_op jit(solution)/shard_map/all_to_all | solution.py:127
  9.7 0.9 copy-start.12
  9.7 1.1 copy-start.9
  11.9 11.3 %collective-permute-start = (bf16[256,512]{1,0:T(8,128)(2,1)S(1)}, bf16[256,512]{1,0:T(8,128)(2,1)S(1)}, u32[]{:S(2)}, u32[]{:S(2)}) collective-permute-start(bf16[256,512]{1,0:T(8,128)(2,1)S(1)} %fusion), channel_id=1, source_target_pairs={{0,96},{96,0},{1,97},{97,1},{2,98},{98,2},{3,99},{99,3},{4,100},{1... | collective-permute-start | bytes 786440 | tf_op jit(solution)/shard_map/ppermute | solution.py:134
  23.2 0.7 copy-start.11
  25.2 15.8 %collective-permute-start.1 = (bf16[2,256,512]{2,1,0:T(8,128)(2,1)S(1)}, bf16[2,256,512]{2,1,0:T(8,128)(2,1)S(1)}, u32[]{:S(2)}, u32[]{:S(2)}) collective-permute-start(bf16[2,256,512]{2,1,0:T(8,128)(2,1)S(1)} %get-tuple-element.36), channel_id=1, source_target_pairs={{0,1},{1,0},{2,3},{3,2},{4,5},{5,4},{6,7},{7,6},{8,9},{9,8},{10,11... | collective-permute-start | bytes 1572872 | tf_op jit(solution)/shard_map/ppermute | solution.py:145
  40.5 43.2 %copy-start.8 = (bf16[2,256,512]{2,1,0:T(8,128)(2,1)}, bf16[2,256,512]{2,1,0:T(8,128)(2,1)S(1)}, u32[]{:S(2)}) copy-start(bf16[2,256,512]{2,1,0:T(8,128)(2,1)S(1)} %pad_maximum_fusion.1) | copy-start | bytes 1572868
  61.7 25.0 %all-to-all-start.2 = ((bf16[12,6,512]{2,1,0:T(8,128)(2,1)}), bf16[12,6,512]{2,1,0:T(8,128)(2,1)S(1)}, u32[]{:S(2)}, u32[]{:S(2)}) async-start(bf16[12,6,512]{2,1,0:T(8,128)(2,1)} %reshape.35), calls=%async_computation.2 | async-start | bytes 196608 | tf_op jit(solution)/shard_map/all_to_all | solution.py:159
  76.6 28.7 %collective-permute-start.4 = (bf16[2,256,512]{2,1,0:T(8,128)(2,1)S(1)}, bf16[2,256,512]{2,1,0:T(8,128)(2,1)S(1)}, u32[]{:S(2)}, u32[]{:S(2)}) collective-permute-start(bf16[2,256,512]{2,1,0:T(8,128)(2,1)S(1)} %pad_maximum_fusion.1), channel_id=1, source_target_pairs={{0,576},{192,0},{384,192},{576,384},{1,577},{193,1},{385,193},{577... | collective-permute-start | bytes 1572872 | tf_op jit(solution)/shard_map/ppermute | solution.py:154
  81.2 24.1 %collective-permute-start.3 = (bf16[2,256,512]{2,1,0:T(8,128)(2,1)S(1)}, bf16[2,256,512]{2,1,0:T(8,128)(2,1)S(1)}, u32[]{:S(2)}, u32[]{:S(2)}) collective-permute-start(bf16[2,256,512]{2,1,0:T(8,128)(2,1)S(1)} %pad_maximum_fusion.1), channel_id=1, source_target_pairs={{0,384},{192,576},{384,0},{576,192},{1,385},{193,577},{385,1},{577... | collective-permute-start | bytes 1572872 | tf_op jit(solution)/shard_map/ppermute | solution.py:154
  83.7 26.0 %collective-permute-start.2 = (bf16[2,256,512]{2,1,0:T(8,128)(2,1)S(1)}, bf16[2,256,512]{2,1,0:T(8,128)(2,1)S(1)}, u32[]{:S(2)}, u32[]{:S(2)}) collective-permute-start(bf16[2,256,512]{2,1,0:T(8,128)(2,1)S(1)} %pad_maximum_fusion.1), channel_id=1, source_target_pairs={{0,192},{192,384},{384,576},{576,0},{1,193},{193,385},{385,577},{5... | collective-permute-start | bytes 1572872 | tf_op jit(solution)/shard_map/ppermute | solution.py:154
  109.7 0.8 copy-start.10
  110.5 28.1 %copy-start.5 = (bf16[128,512]{1,0:T(8,128)(2,1)S(1)}, bf16[128,512]{1,0:T(8,128)(2,1)}, u32[]{:S(2)}) copy-start(bf16[128,512]{1,0:T(8,128)(2,1)} %cot_ref.3) | copy-start | bytes 393220
  112.0 26.6 %copy-start.1 = (bf16[128,4096]{1,0:T(8,128)(2,1)S(1)}, bf16[128,4096]{1,0:T(8,128)(2,1)}, u32[]{:S(2)}) copy-start(bf16[128,4096]{1,0:T(8,128)(2,1)} %hidden_ref.3) | copy-start | bytes 3145732
  112.0 22.0 %collective-permute-start.6 = (bf16[4,2,256,512]{3,2,1,0:T(8,128)(2,1)S(1)}, bf16[4,2,256,512]{3,2,1,0:T(8,128)(2,1)}, u32[]{:S(2)}, u32[]{:S(2)}) collective-permute-start(bf16[4,2,256,512]{3,2,1,0:T(8,128)(2,1)S(1)} %pad_maximum_fusion.own_ref), channel_id=1, source_target_pairs={{0,1},{1,0},{2,3},{3,2},{4,5},{5,4},{6,7},{7,6},{8,9},{9,8},{10,11... | collective-permute-start | bytes 6291464 | tf_op jit(solution)/shard_map/ppermute | solution.py:166
  125.7 4.3 %collective-permute-start.5 = (bf16[256,512]{1,0:T(8,128)(2,1)S(1)}, bf16[256,512]{1,0:T(8,128)(2,1)}, u32[]{:S(2)}, u32[]{:S(2)}) collective-permute-start(bf16[256,512]{1,0:T(8,128)(2,1)S(1)} %bitcast.17), channel_id=1, source_target_pairs={{0,1},{1,0},{2,3},{3,2},{4,5},{5,4},{6,7},{7,6},{8,9},{9,8},{10,11... | collective-permute-start | bytes 786440 | tf_op jit(solution)/shard_map/ppermute | solution.py:168
  129.9 1.0 copy-start.2
  131.0 0.9 copy-start.3
  134.6 12.9 %all-to-all-start.5 = ((f32[8,4,128]{2,1,0:T(4,128)}), f32[8,4,128]{2,1,0:T(4,128)S(1)}, u32[]{:S(2)}, u32[]{:S(2)}) async-start(f32[8,4,128]{2,1,0:T(4,128)} %broadcast_in_dim.28), calls=%async_computation.5 | async-start | bytes 32768 | tf_op jit(solution)/shard_map/all_to_all | solution.py:101
  138.6 0.8 copy-start.7

commit v3 on v2

v3 whole, which is shorter than its diff:
```python
import functools

import jax
import jax.numpy as jnp
from jax import lax
from jax.experimental import pallas as pl
from jax.experimental.pallas import tpu as pltpu
from jax.sharding import Mesh
from jax.sharding import PartitionSpec as P

F32 = jnp.float32
BF16 = jnp.bfloat16
VMEM = pl.BlockSpec(memory_space=pltpu.VMEM)
SMEM = pl.BlockSpec(memory_space=pltpu.SMEM)
HBM = pl.BlockSpec(memory_space=pltpu.HBM)
PARAMS = pltpu.CompilerParams(vmem_limit_bytes=12 * 1024 * 1024)
SWAP = [(0, 1), (1, 0)]
LANES = 128


def shape(dims, dtype):
    return jax.ShapeDtypeStruct(dims, dtype)


def down(row):
    return jnp.broadcast_to(row, (LANES, row.shape[1])).T


def gained_kernel(place_ref, codes_ref, scales_ref, gain_ref, out_ref):
    half, cols = out_ref.shape
    blocks = scales_ref.shape[0]
    rows = pl.ds(pl.multiple_of(place_ref[0] * half, half), half)
    gain = gain_ref[:, rows].astype(F32)
    for b in range(blocks):
        factor = down(scales_ref[b : b + 1, rows].astype(F32) * gain)
        for at in range(b * cols // blocks, (b + 1) * cols // blocks, LANES):
            columns = slice(at, at + LANES)
            out_ref[:, columns] = (codes_ref[rows, columns].astype(F32) * factor).astype(BF16)


def prepare_kernel(hidden_ref, cot_ref, sent_ref, hidden, cot, come, go):
    peers, tok, part = hidden.shape
    loads = [
        pltpu.make_async_copy(hidden_ref.at[:, pl.ds(i * part, part)], hidden.at[i], come.at[i]) for i in range(peers)
    ]
    loads.append(pltpu.make_async_copy(cot_ref, cot, come.at[peers]))
    for load in loads:
        load.start()
    stores = []
    square = jnp.zeros((tok, 1), F32)
    for i in range(peers):
        loads[i].wait()
        stores.append(pltpu.make_async_copy(hidden.at[i], sent_ref.at[i, :, pl.ds(0, part)], go.at[i]))
        stores[-1].start()
        piece = hidden[i].astype(F32)
        square = square + jnp.sum(piece * piece, axis=1, keepdims=True)
    inv = lax.rsqrt(square / (peers * part) + 1e-05)
    loads[peers].wait()
    cot[...] = (cot[...].astype(F32) * inv).astype(BF16)
    for i in range(peers):
        stores.append(pltpu.make_async_copy(cot, sent_ref.at[i, :, pl.ds(part, cot.shape[1])], go.at[peers + i]))
        stores[-1].start()
    for store in stores:
        store.wait()


def stack_kernel(*refs):
    for i, ref in enumerate(refs[:-1]):
        refs[-1][i] = ref[...]


def product_kernel(place_ref, got_ref, keep_ref, send_ref):
    peers, tok, wide = got_ref.shape
    groups, half, cols = keep_ref.shape
    part = wide - cols
    core = place_ref[0]
    cot = got_ref[:, :, part:].reshape(peers * tok, cols)
    for out_ref, which in ((send_ref, 1 - core), (keep_ref, core)):
        for g in range(groups):
            at = pl.multiple_of(g * 2 * half + which * half, half)
            left = got_ref[:, :, pl.ds(at, half)].reshape(peers * tok, half)
            value = lax.dot_general(left, cot, (((0,), (0,)), ((), ())), preferred_element_type=F32)
            out_ref[g] = value.astype(out_ref.dtype)


def finish_kernel(place_ref, total_ref, codes_ref, scales_ref, gain_ref, grad_ref, part_ref):
    half, cols = total_ref.shape
    blocks = scales_ref.shape[0]
    rows = pl.ds(pl.multiple_of(place_ref[0] * half, half), half)
    gain = down(gain_ref[:, rows].astype(F32))
    dots = jnp.zeros((half, LANES), F32)
    for b in range(blocks):
        scale = down(scales_ref[b : b + 1, rows].astype(F32))
        for at in range(b * cols // blocks, (b + 1) * cols // blocks, LANES):
            columns = slice(at, at + LANES)
            value = total_ref[:, columns].astype(F32)
            weight = (codes_ref[rows, columns].astype(F32) * scale).astype(BF16)
            dots = dots + value * weight.astype(F32)
            grad_ref[:, columns] = (value * gain).astype(BF16)
    for i in range(half // LANES):
        row = jnp.sum(dots[i * LANES : (i + 1) * LANES].T, axis=0, keepdims=True)
        for peer in range(part_ref.shape[0]):
            part_ref[peer, i : i + 1, :] = row


def tokens_kernel(place_ref, hidden_ref, cot_ref, own_ref, other_ref, keys_ref, grad_ref):
    shifts, pairs, half, cols = own_ref.shape
    width = hidden_ref.shape[1]
    core, here, side = place_ref[0], place_ref[1], place_ref[2]
    square = jnp.zeros((hidden_ref.shape[0], 1), F32)
    for at in range(0, width, width // 4):
        piece = hidden_ref[:, at : at + width // 4].astype(F32)
        square = square + jnp.sum(piece * piece, axis=1, keepdims=True)
    inv = lax.rsqrt(square / width + 1e-05)
    cot = cot_ref[...]
    places = []
    for s in range(shifts):
        x = lax.rem(here - s + shifts, shifts)
        for j in range(pairs):
            y = lax.rem(side + j, pairs)
            for ref, which in ((own_ref, core), (other_ref, 1 - core)):
                at = pl.multiple_of(((x * pairs + y) * 2 + which) * half, half)
                places.append((ref.at[s, j], pl.ds(at, half)))
    keys = jnp.zeros(keys_ref.shape, F32)
    for ref, columns in places:
        keys = keys + jnp.dot(hidden_ref[:, columns], ref[...], preferred_element_type=F32)
    keys = keys * inv
    keys_ref[...] = keys.astype(BF16)
    mean = jnp.sum(keys * cot.astype(F32), axis=1, keepdims=True) / width
    for ref, columns in places:
        value = lax.dot_general(cot, ref[...], (((1,), (1,)), ((), ())), preferred_element_type=F32)
        unit = hidden_ref[:, columns].astype(F32) * inv
        grad_ref[:, columns] = (inv * (value - unit * mean)).astype(BF16)


def halve_kernel(place_ref, terms_ref, keep_ref, send_ref):
    rows = keep_ref.shape[0]
    mine = place_ref[3]
    for ref, which in ((send_ref, 1 - mine), (keep_ref, mine)):
        at = pl.ds(pl.multiple_of(which * rows, rows), rows)
        total = terms_ref[0, at, :].astype(F32)
        for i in range(1, terms_ref.shape[0]):
            total = total + terms_ref[i, at, :].astype(F32)
        ref[...] = total.astype(BF16)


def add_kernel(keep_ref, came_ref, copies_ref):
    total = (keep_ref[...].astype(F32) + came_ref[...].astype(F32)).astype(BF16)
    for i in range(copies_ref.shape[0]):
        copies_ref[i] = total


def total_kernel(scale, terms_ref, copies_ref):
    total = terms_ref[0].astype(F32)
    for i in range(1, terms_ref.shape[0]):
        total = total + terms_ref[i].astype(F32)
    total = (total * scale).astype(BF16)
    for i in range(copies_ref.shape[0]):
        copies_ref[i] = total


def gains_kernel(place_ref, own_ref, other_ref, out_ref):
    groups, deep, _ = own_ref.shape
    core = place_ref[0]
    for g in range(groups):
        for ref, which in ((own_ref, core), (other_ref, 1 - core)):
            out_ref[pl.ds((g * 2 + which) * deep, deep), :] = ref[g]


def call(kernel, outs, specs, flops, moved, after=()):
    count = len(specs)

    def run(*refs):
        kernel(*refs[:count], *refs[count + len(after) :])

    made = pl.pallas_call(
        run,
        out_shape=outs,
        in_specs=specs + [pl.BlockSpec(memory_space=pl.ANY)] * len(after),
        out_specs=jax.tree.map(lambda _: VMEM, outs),
        compiler_params=PARAMS,
        cost_estimate=pl.CostEstimate(flops=flops, bytes_accessed=moved, transcendentals=0),
    )
    return lambda *operands: made(*operands, *after)


def tie(*values):
    return lax.optimization_barrier(values)


def by_core(own, other):
    first = lax.axis_index("c") == 0
    return jnp.where(first, own, other), jnp.where(first, other, own)


def body(hidden_in, norm_gain, key_codes, key_scales, key_cotangent):
    nx, nh, nl, nz, np, nc = (lax.axis_size(a) for a in ("x", "yh", "yl", "z", "zp", "c"))
    tok, width = hidden_in.shape
    rows, cols = key_codes.shape
    total_tokens = tok * nx * nh * nl * nz * np * nc
    half = rows // nc
    part = width // nx
    place = jnp.stack([lax.axis_index(a) for a in ("c", "x", "yh", "zp")]).astype(jnp.int32)
    scales, gain = key_scales.T, norm_gain[None]

    sent = pl.pallas_call(
        prepare_kernel,
        out_shape=shape((nx, tok, part + cols), BF16),
        in_specs=[HBM] * 2,
        out_specs=HBM,
        scratch_shapes=[
            pltpu.VMEM((nx, tok, part), BF16),
            pltpu.VMEM((tok, cols), BF16),
            pltpu.SemaphoreType.DMA((nx + 1,)),
            pltpu.SemaphoreType.DMA((2 * nx,)),
        ],
        compiler_params=PARAMS,
        cost_estimate=pl.CostEstimate(flops=4 * tok * width, bytes_accessed=4 * tok * width, transcendentals=0),
    )(hidden_in, key_cotangent)
    got = lax.all_to_all(sent, "x", 0, 0)

    mine = call(gained_kernel, shape((half, cols), BF16), [SMEM, VMEM, VMEM, VMEM], half * cols, 4 * half * cols, [sent])(
        place, key_codes, scales, gain
    )
    mate = lax.ppermute(mine, "yh", SWAP)

    keep, send = call(
        product_kernel,
        [shape((nh, half, cols), F32), shape((nh, half, cols), BF16)],
        [SMEM, VMEM],
        2 * nx * tok * part * cols,
        2 * nx * tok * (part + cols) + 6 * nh * half * cols,
        [mate],
    )(place, got)
    product = (keep + lax.ppermute(send, "c", SWAP).astype(F32)).astype(BF16)
    pair = call(stack_kernel, shape((nh, half, cols), BF16), [VMEM] * 2, 0, 4 * nh * half * cols, [product])(mine, mate)

    quarter = half // nl
    eighth = quarter // np
    own = [pair] + [lax.ppermute(pair, "x", [(i, (i + s) % nx) for i in range(nx)]) for s in range(1, nx)]
    terms = lax.all_to_all(product.reshape(nh * nl, quarter, cols), ("yh", "yl"), 0, 0)
    keep, send = call(
        halve_kernel, [shape((eighth, cols), BF16)] * 2, [SMEM, VMEM], nh * nl * quarter * cols, 2 * half * cols
    )(place, terms)
    copies = call(
        add_kernel, shape((nz, eighth, cols), BF16), [VMEM, VMEM], eighth * cols, 2 * nz * eighth * cols
    )(keep, lax.ppermute(send, "zp", SWAP))
    own = call(stack_kernel, shape((nx, nh, half, cols), BF16), [VMEM] * nx, 0, 4 * width * cols, [keep])(*own)
    other = lax.ppermute(own, "c", SWAP)
    scale = float(total_tokens) ** -0.5
    copies = call(
        functools.partial(total_kernel, scale),
        shape((nl * np, eighth, cols), BF16),
        [VMEM],
        nz * eighth * cols,
        2 * (nz + nl * np) * eighth * cols,
        [other],
    )(lax.all_to_all(copies, "z", 0, 0))

    whole = lax.all_to_all(copies, ("yl", "zp"), 0, 0).reshape(half, cols)
    keys_out, input_gradient = call(
        tokens_kernel,
        [shape((tok, cols), BF16), shape((tok, width), BF16)],
        [SMEM, VMEM, VMEM, VMEM, VMEM],
        4 * tok * width * cols,
        4 * tok * width + 2 * width * cols,
    )(place, hidden_in, key_cotangent, own, other)
    whole, keys_out = tie(whole, keys_out)
    grad_half, gain_half = call(
        finish_kernel,
        [shape((half, cols), BF16), shape((nx * nh, half // LANES, LANES), F32)],
        [SMEM, VMEM, VMEM, VMEM, VMEM],
        4 * half * cols,
        6 * half * cols,
    )(place, whole, key_codes, scales, gain)
    gains = lax.all_to_all(gain_half, ("x", "yh"), 0, 0)
    weight_grad = jnp.concatenate(by_core(grad_half, lax.ppermute(grad_half, "c", SWAP)), axis=0)
    gains, weight_grad = tie(gains, weight_grad)
    gain_gradient = call(
        gains_kernel, shape((width // LANES, LANES), F32), [SMEM, VMEM, VMEM], width, 8 * width
    )(place, gains, lax.ppermute(gains, "c", SWAP)).reshape(width)
    return (keys_out, input_gradient, weight_grad, gain_gradient)


def solution(mesh):
    axes = ("x", "yh", "yl", "z", "zp", "c")
    fine = Mesh(mesh.devices.reshape(4, 2, 4, 6, 2, 2), axes)
    tokens = P(axes, None)
    group = ("x", "yh")
    in_specs = (tokens, P(group), P(group, None), P(group, None), tokens)
    out_specs = (tokens, tokens, P(group, None), P())
    return jax.shard_map(body, mesh=fine, in_specs=in_specs, out_specs=out_specs, check_vma=False)
```

time: 149 us -> 155 us (1.040)
  blocking collectives: 49.3 us -> 23.4 us
  waiting for transfers between devices: 12.9 us -> 35.9 us
  starting transfers between devices: 60.6 us -> 71 us
  other arithmetic: 3.99 us -> 1.91 us
  Pallas kernels: 9.55 us -> 11.6 us
    all_to_all x3 -> x1, blocking collectives: 49.3 us -> 23.4 us  [body(): lax.all_to_all(copies, 'z', 0, 0)]
    ppermute x6 -> x8, starting transfers between devices: 29.4 us -> 43.2 us  [the longest x1 13.8 us: body(): product = (keep + lax.ppermute(send, 'c', SWAP).astype(F32)).astype(BF16)]
    all_to_all x2 -> x3, waiting for transfers between devices: 3.85 us -> 17.2 us  [the longest x1 8.06 us: body(): gains = lax.all_to_all(gain_half, ('x', 'yh'), 0, 0)]
    ppermute x6 -> x8, waiting for transfers between devices: 5.23 us -> 14.4 us  [the longest x3 10.3 us: body(): lax.ppermute(pair, 'x', [(i, (i + s) % nx) for i in range(nx)])]
    all_to_all x2 -> x3, starting transfers between devices: 18.9 us -> 15.3 us  [the longest x1 6.23 us: body(): gains = lax.all_to_all(gain_half, ('x', 'yh'), 0, 0)]
    another operation x4 -> x1, other arithmetic: 2.62 us -> 0.08 us  [body(): jnp.stack([lax.axis_index(a) for a in ('c', 'x', 'yh', 'zp')])]
    broadcast_in_dim x5 -> x1, local copies, waits for them, and re-layouts: 2.1 us -> 0.01 us  [body(): scales, gain = (key_scales.T, norm_gain[None])]
    pallas_call x4 -> x11, Pallas kernels: 9.55 us -> 11.6 us  [the longest x10 9.86 us: call(): return lambda *operands: made(*operands, *after)]
  transfers between devices with their start and end apart: 10 -> 13, of which waited for: 6 -> 10; matrix products, arithmetic and copies ran while one was open for 3% -> 1% of each run, Pallas kernels for 5% -> 3%
where the time goes in v3:
time: 155 us; the launch traced here: 154 us
  starting transfers between devices  71 us (46%)
  waiting for transfers between devices  35.9 us (23%)
  blocking collectives  23.4 us (15%)
  Pallas kernels  11.6 us (7%)
  local copies, waits for them, and re-layouts  9.8 us (6%)
  other arithmetic  1.91 us (1%)
    all_to_all x1, blocking collectives, body(): lax.all_to_all(copies, 'z', 0, 0)  23.4 us
    ppermute x1, starting transfers between devices, body(): product = (keep + lax.ppermute(send, 'c', SWAP).astype(F32)).astype(BF16)  13.8 us
    ppermute x3, waiting for transfers between devices, body(): lax.ppermute(pair, 'x', [(i, (i + s) % nx) for i in range(nx)])  10.3 us
    ppermute x3, starting transfers between devices, body(): lax.ppermute(pair, 'x', [(i, (i + s) % nx) for i in range(nx)])  10.2 us
    pallas_call x10, Pallas kernels, call(): return lambda *operands: made(*operands, *after)  9.86 us
    unnamed x28, local copies, waits for them, and re-layouts  9.79 us
    ppermute x1, starting transfers between devices, body(): lax.ppermute(grad_half, 'c', SWAP)  8.19 us
    all_to_all x1, waiting for transfers between devices, body(): gains = lax.all_to_all(gain_half, ('x', 'yh'), 0, 0)  8.06 us
  transfers between devices with their start and end apart: 13, of which 10 were waited for; matrix products, arithmetic and copies ran while one was open for 1% of the time, Pallas kernels for 3%

profile of v3, /device:TPU:1, one launch (start us, length us, event | category | flops | bytes accessed | tf_op | source)
XLA Modules:
  0.0 154.5 jit_solution(12370430812961146654)
XLA Ops:
  0.6 0.0 copy-start.2
  0.6 1.2 copy-done.2
  1.9 0.0 copy-start.10
  1.9 0.9 copy-done.10
  2.8 1.7 %shard_map.84.refs_4_ = bf16[4,128,1536]{2,1,0:T(8,128)(2,1)} custom-call(bf16[128,4096]{1,0:T(8,128)(2,1)S(1)} %copy-done.2, bf16[128,512]{1,0:T(8,128)(2,1)S(1)} %copy-done.10), custom_call_target="tpu_custom_call" | custom-call | flops 2097152 | bytes 2097152 | tf_op jit(solution)/shard_map/pallas_call | solution.py:206
  4.5 0.0 copy-start.13
  4.5 0.0 copy-start.4
  4.5 0.0 copy-start.12
  4.5 5.0 %all-to-all-start = ((bf16[4,128,1536]{2,1,0:T(8,128)(2,1)}), bf16[4,128,1536]{2,1,0:T(8,128)(2,1)S(1)}, u32[]{:S(2)}, u32[]{:S(2)}) async-start(bf16[4,128,1536]{2,1,0:T(8,128)(2,1)} %shard_map.84.refs_4_), calls=%async_computation | async-start | bytes 3145728 | tf_op jit(solution)/shard_map/all_to_all | solution.py:220
  9.5 0.0 copy-done.13
  9.5 0.1 pad_add_fusion.refs_0_
  9.6 0.0 copy-done.4
  9.6 0.0 copy-done.12
  9.6 0.7 shard_map.85.refs_0_
  10.3 7.5 %collective-permute-start = (bf16[256,512]{1,0:T(8,128)(2,1)S(1)}, bf16[256,512]{1,0:T(8,128)(2,1)S(1)}, u32[]{:S(2)}, u32[]{:S(2)}) collective-permute-start(bf16[256,512]{1,0:T(8,128)(2,1)S(1)} %shard_map.85.refs_0_), channel_id=1, source_target_pairs={{0,96},{96,0},{1,97},{97,1},{2,98},{98,2},{3,99},{99,3},{4,100},{1... | collective-permute-start | bytes 786440 | tf_op jit(solution)/shard_map/ppermute | solution.py:225
  17.8 3.8 %collective-permute-done.refs_2_.refs_1_ = bf16[256,512]{1,0:T(8,128)(2,1)S(1)} collective-permute-done((bf16[256,512]{1,0:T(8,128)(2,1)S(1)}, bf16[256,512]{1,0:T(8,128)(2,1)S(1)}, u32[]{:S(2)}, u32[]{:S(2)}) %collective-permute-start) | collective-permute-done | bytes 262176 | tf_op jit(solution)/shard_map/ppermute | solution.py:225
  21.6 0.5 all-to-all-done.refs_1_
  22.1 1.3 shard_map.86
  23.4 13.8 %collective-permute-start.1 = (bf16[2,256,512]{2,1,0:T(8,128)(2,1)S(1)}, bf16[2,256,512]{2,1,0:T(8,128)(2,1)S(1)}, u32[]{:S(2)}, u32[]{:S(2)}) collective-permute-start(bf16[2,256,512]{2,1,0:T(8,128)(2,1)S(1)} %get-tuple-element.17), channel_id=1, source_target_pairs={{0,1},{1,0},{2,3},{3,2},{4,5},{5,4},{6,7},{7,6},{8,9},{9,8},{10,11... | collective-permute-start | bytes 1572872 | tf_op jit(solution)/shard_map/ppermute | solution.py:235
  37.2 1.5 collective-permute-done.1
  38.7 1.0 add_convert_fusion.refs_2_
  39.7 4.0 %all-to-all-start.1 = ((bf16[8,64,512]{2,1,0:T(8,128)(2,1)}), bf16[8,64,512]{2,1,0:T(8,128)(2,1)S(1)}, u32[]{:S(2)}, u32[]{:S(2)}) async-start(bf16[8,64,512]{2,1,0:T(8,128)(2,1)} %bitcast.5), calls=%async_computation.1 | async-start | bytes 1048576 | tf_op jit(solution)/shard_map/all_to_all | solution.py:241
  43.7 2.9 %collective-permute-start.3 = (bf16[2,256,512]{2,1,0:T(8,128)(2,1)S(1)}, bf16[2,256,512]{2,1,0:T(8,128)(2,1)S(1)}, u32[]{:S(2)}, u32[]{:S(2)}) collective-permute-start(bf16[2,256,512]{2,1,0:T(8,128)(2,1)S(1)} %shard_map.89.refs_0_), channel_id=1, source_target_pairs={{0,192},{192,384},{384,576},{576,0},{1,193},{193,385},{385,577},{5... | collective-permute-start | bytes 1572872 | tf_op jit(solution)/shard_map/ppermute | solution.py:240
  46.6 4.3 %collective-permute-start.4 = (bf16[2,256,512]{2,1,0:T(8,128)(2,1)S(1)}, bf16[2,256,512]{2,1,0:T(8,128)(2,1)S(1)}, u32[]{:S(2)}, u32[]{:S(2)}) collective-permute-start(bf16[2,256,512]{2,1,0:T(8,128)(2,1)S(1)} %shard_map.89.refs_0_), channel_id=1, source_target_pairs={{0,384},{192,576},{384,0},{576,192},{1,385},{193,577},{385,1},{577... | collective-permute-start | bytes 1572872 | tf_op jit(solution)/shard_map/ppermute | solution.py:240
  50.9 3.1 %collective-permute-start.5 = (bf16[2,256,512]{2,1,0:T(8,128)(2,1)S(1)}, bf16[2,256,512]{2,1,0:T(8,128)(2,1)S(1)}, u32[]{:S(2)}, u32[]{:S(2)}) collective-permute-start(bf16[2,256,512]{2,1,0:T(8,128)(2,1)S(1)} %shard_map.89.refs_0_), channel_id=1, source_target_pairs={{0,576},{192,0},{384,192},{576,384},{1,577},{193,1},{385,193},{577... | collective-permute-start | bytes 1572872 | tf_op jit(solution)/shard_map/ppermute | solution.py:240
  54.0 7.6 %all-to-all-done.1.refs_1_ = bf16[8,64,512]{2,1,0:T(8,128)(2,1)S(1)} async-done(((bf16[8,64,512]{2,1,0:T(8,128)(2,1)}), bf16[8,64,512]{2,1,0:T(8,128)(2,1)S(1)}, u32[]{:S(2)}, u32[]{:S(2)}) %all-to-all-start.1) | async-done | bytes 524320 | tf_op jit(solution)/shard_map/all_to_all | solution.py:241
  61.7 0.6 shard_map.87
  62.3 0.0 collective-permute-done.3.refs_1_
  62.3 9.6 %collective-permute-done.4.refs_2_ = bf16[2,256,512]{2,1,0:T(8,128)(2,1)S(1)} collective-permute-done((bf16[2,256,512]{2,1,0:T(8,128)(2,1)S(1)}, bf16[2,256,512]{2,1,0:T(8,128)(2,1)S(1)}, u32[]{:S(2)}, u32[]{:S(2)}) %collective-permute-start.4) | collective-permute-done | bytes 524320 | tf_op jit(solution)/shard_map/ppermute | solution.py:240
  71.9 0.0 copy-start.6
  71.9 0.8 copy-done.6
  72.6 0.8 collective-permute-done.5.refs_3_
  73.4 0.0 copy-start.8
  73.4 0.8 copy-done.8
  74.2 0.0 copy-start.7
  74.2 1.0 copy-done.7
  75.2 1.0 copy-done.9
  76.3 0.1 shard_map.90.refs_3_
  76.4 0.0 copy-start.3
  76.4 0.0 copy-start.11
  76.4 3.6 %collective-permute-start.6 = (bf16[4,2,256,512]{3,2,1,0:T(8,128)(2,1)S(1)}, bf16[4,2,256,512]{3,2,1,0:T(8,128)(2,1)S(1)}, u32[]{:S(2)}, u32[]{:S(2)}) collective-permute-start(bf16[4,2,256,512]{3,2,1,0:T(8,128)(2,1)S(1)} %shard_map.90.refs_3_), channel_id=1, source_target_pairs={{0,1},{1,0},{2,3},{3,2},{4,5},{5,4},{6,7},{7,6},{8,9},{9,8},{10,11... | collective-permute-start | bytes 6291464 | tf_op jit(solution)/shard_map/ppermute | solution.py:249
  80.0 4.0 %collective-permute-start.2 = (bf16[32,512]{1,0:T(8,128)(2,1)S(1)}, bf16[32,512]{1,0:T(8,128)(2,1)S(1)}, u32[]{:S(2)}, u32[]{:S(2)}) collective-permute-start(bf16[32,512]{1,0:T(8,128)(2,1)S(1)} %get-tuple-element.19), channel_id=1, source_target_pairs={{0,2},{2,0},{1,3},{3,1},{4,6},{6,4},{5,7},{7,5},{8,10},{10,8},{9,1... | collective-permute-start | bytes 98312 | tf_op jit(solution)/shard_map/ppermute | solution.py:247
  84.1 1.7 %collective-permute-done.2.refs_1_ = bf16[32,512]{1,0:T(8,128)(2,1)S(1)} collective-permute-done((bf16[32,512]{1,0:T(8,128)(2,1)S(1)}, bf16[32,512]{1,0:T(8,128)(2,1)S(1)}, u32[]{:S(2)}, u32[]{:S(2)}) %collective-permute-start.2) | collective-permute-done | bytes 32800 | tf_op jit(solution)/shard_map/ppermute | solution.py:247
  85.8 23.4 %all_to_all.25.refs_0_ = bf16[6,32,512]{2,1,0:T(8,128)(2,1)S(1)} all-to-all(bf16[6,32,512]{2,1,0:T(8,128)(2,1)S(1)} %shard_map.88), channel_id=1, replica_groups=mesh['x'=4,'yh'=2,'yl'=4,'z'=6,'zp'=2,'c'=2] {'z'}, dimensions={0} | all-to-all | bytes 393216 | tf_op jit(solution)/shard_map/all_to_all | solution.py:258
  109.2 0.0 collective-permute-done.6.refs_1_.refs_4_
  109.2 0.7 shard_map.91
  109.9 1.3 copy-done
  111.3 5.1 %all-to-all-start.3 = ((bf16[8,32,512]{2,1,0:T(8,128)(2,1)}), bf16[8,32,512]{2,1,0:T(8,128)(2,1)S(1)}, u32[]{:S(2)}, u32[]{:S(2)}) async-start(bf16[8,32,512]{2,1,0:T(8,128)(2,1)} %shard_map.91), calls=%async_computation.3 | async-start | bytes 524288 | tf_op jit(solution)/shard_map/all_to_all | solution.py:260
  116.4 0.0 copy-done.3
  116.4 0.0 copy-done.11
  116.4 0.0 copy-start.1
  116.4 1.6 %copy-done.1 = bf16[4,2,256,512]{3,2,1,0:T(8,128)(2,1)S(1)} copy-done((bf16[4,2,256,512]{3,2,1,0:T(8,128)(2,1)S(1)}, bf16[4,2,256,512]{3,2,1,0:T(8,128)(2,1)}, u32[]{:S(2)}) %copy-start.1) | copy-done | bytes 2097176
  118.0 3.7 %shard_map.92 = (bf16[128,512]{1,0:T(8,128)(2,1)}, bf16[128,4096]{1,0:T(8,128)(2,1)}) custom-call(s32[4]{0:T(128)S(1)} %pad_add_fusion.refs_0_, bf16[128,4096]{1,0:T(8,128)(2,1)S(1)} %copy-done.3, bf16[128,512]{1,0:T(8,128)(2,1)S(1)} %copy-done.11, bf16[4,2,256,512]{3,2,1,0:T(8,128)(2,1)S(1)} %shard_map.90.refs_3_, bf16[4,2,256,512]{3,2,1,0:T(8,128)(2,1)S(1)} %copy-done.1), custom_call_target="tpu_custom_call" | custom-call | flops 1073741824 | bytes 6291456 | tf_op jit(solution)/shard_map/pallas_call | solution.py:184
  121.7 1.5 all-to-all-done.3
  123.3 1.0 copy-done.5
  124.3 1.5 shard_map.93
  125.8 8.2 %collective-permute-start.7 = (bf16[256,512]{1,0:T(8,128)(2,1)S(1)}, bf16[256,512]{1,0:T(8,128)(2,1)S(1)}, u32[]{:S(2)}, u32[]{:S(2)}) collective-permute-start(bf16[256,512]{1,0:T(8,128)(2,1)S(1)} %get-tuple-element.25), channel_id=1, source_target_pairs={{0,1},{1,0},{2,3},{3,2},{4,5},{5,4},{6,7},{7,6},{8,9},{9,8},{10,11... | collective-permute-start | bytes 786440 | tf_op jit(solution)/shard_map/ppermute | solution.py:277
  134.0 6.2 %all-to-all-start.4 = ((f32[8,2,128]{2,1,0:T(2,128)}), f32[8,2,128]{2,1,0:T(2,128)S(1)}, u32[]{:S(2)}, u32[]{:S(2)}) async-start(f32[8,2,128]{2,1,0:T(2,128)} %get-tuple-element.24), calls=%async_computation.4 | async-start | bytes 16384 | tf_op jit(solution)/shard_map/all_to_all | solution.py:276
  140.2 0.0 collective-permute-done.7
  140.2 0.8 pad_maximum_fusion
  141.1 8.1 %all-to-all-done.4.refs_1_ = f32[8,2,128]{2,1,0:T(2,128)S(1)} async-done(((f32[8,2,128]{2,1,0:T(2,128)}), f32[8,2,128]{2,1,0:T(2,128)S(1)}, u32[]{:S(2)}, u32[]{:S(2)}) %all-to-all-start.4) | async-done | bytes 8224 | tf_op jit(solution)/shard_map/all_to_all | solution.py:276
  149.1 3.3 %collective-permute-start.8 = (f32[8,2,128]{2,1,0:T(2,128)S(1)}, f32[8,2,128]{2,1,0:T(2,128)S(1)}, u32[]{:S(2)}, u32[]{:S(2)}) collective-permute-start(f32[8,2,128]{2,1,0:T(2,128)S(1)} %all-to-all-done.4.refs_1_), channel_id=1, source_target_pairs={{0,1},{1,0},{2,3},{3,2},{4,5},{5,4},{6,7},{7,6},{8,9},{9,8},{10,11... | collective-permute-start | bytes 24584 | tf_op jit(solution)/shard_map/ppermute | solution.py:281
  152.5 0.8 collective-permute-done.8.refs_2_
  153.3 1.2 shard_map.94
  (7 shorter events, 0.1 us)
Async XLA Ops:
  0.6 1.2 copy-start.2
  1.9 0.9 copy-start.10
  4.5 5.0 %copy-start.13 = (bf16[512]{0:T(512)(128)(2,1)S(1)}, bf16[512]{0:T(512)(128)(2,1)}, u32[]{:S(2)}) copy-start(bf16[512]{0:T(512)(128)(2,1)} %param.6) | copy-start | bytes 3076
  4.5 5.1 %copy-start.4 = (bf16[512,512]{1,0:T(8,128)(2,1)S(1)}, bf16[512,512]{1,0:T(8,128)(2,1)}, u32[]{:S(2)}) copy-start(bf16[512,512]{1,0:T(8,128)(2,1)} %refs_2_.3) | copy-start | bytes 1572868
  4.5 5.1 %copy-start.12 = (bf16[512,2]{0,1:T(2,128)(2,1)S(1)}, bf16[512,2]{0,1:T(2,128)(2,1)}, u32[]{:S(2)}) copy-start(bf16[512,2]{0,1:T(2,128)(2,1)} %param.8) | copy-start | bytes 6148
  4.5 17.5 %all-to-all-start = ((bf16[4,128,1536]{2,1,0:T(8,128)(2,1)}), bf16[4,128,1536]{2,1,0:T(8,128)(2,1)S(1)}, u32[]{:S(2)}, u32[]{:S(2)}) async-start(bf16[4,128,1536]{2,1,0:T(8,128)(2,1)} %shard_map.84.refs_4_), calls=%async_computation | async-start | bytes 3145728 | tf_op jit(solution)/shard_map/all_to_all | solution.py:220
  10.3 11.3 %collective-permute-start = (bf16[256,512]{1,0:T(8,128)(2,1)S(1)}, bf16[256,512]{1,0:T(8,128)(2,1)S(1)}, u32[]{:S(2)}, u32[]{:S(2)}) collective-permute-start(bf16[256,512]{1,0:T(8,128)(2,1)S(1)} %shard_map.85.refs_0_), channel_id=1, source_target_pairs={{0,96},{96,0},{1,97},{97,1},{2,98},{98,2},{3,99},{99,3},{4,100},{1... | collective-permute-start | bytes 786440 | tf_op jit(solution)/shard_map/ppermute | solution.py:225
  23.4 15.4 %collective-permute-start.1 = (bf16[2,256,512]{2,1,0:T(8,128)(2,1)S(1)}, bf16[2,256,512]{2,1,0:T(8,128)(2,1)S(1)}, u32[]{:S(2)}, u32[]{:S(2)}) collective-permute-start(bf16[2,256,512]{2,1,0:T(8,128)(2,1)S(1)} %get-tuple-element.17), channel_id=1, source_target_pairs={{0,1},{1,0},{2,3},{3,2},{4,5},{5,4},{6,7},{7,6},{8,9},{9,8},{10,11... | collective-permute-start | bytes 1572872 | tf_op jit(solution)/shard_map/ppermute | solution.py:235
  39.7 22.0 %all-to-all-start.1 = ((bf16[8,64,512]{2,1,0:T(8,128)(2,1)}), bf16[8,64,512]{2,1,0:T(8,128)(2,1)S(1)}, u32[]{:S(2)}, u32[]{:S(2)}) async-start(bf16[8,64,512]{2,1,0:T(8,128)(2,1)} %bitcast.5), calls=%async_computation.1 | async-start | bytes 1048576 | tf_op jit(solution)/shard_map/all_to_all | solution.py:241
  43.7 18.5 %collective-permute-start.3 = (bf16[2,256,512]{2,1,0:T(8,128)(2,1)S(1)}, bf16[2,256,512]{2,1,0:T(8,128)(2,1)S(1)}, u32[]{:S(2)}, u32[]{:S(2)}) collective-permute-start(bf16[2,256,512]{2,1,0:T(8,128)(2,1)S(1)} %shard_map.89.refs_0_), channel_id=1, source_target_pairs={{0,192},{192,384},{384,576},{576,0},{1,193},{193,385},{385,577},{5... | collective-permute-start | bytes 1572872 | tf_op jit(solution)/shard_map/ppermute | solution.py:240
  46.6 25.2 %collective-permute-start.4 = (bf16[2,256,512]{2,1,0:T(8,128)(2,1)S(1)}, bf16[2,256,512]{2,1,0:T(8,128)(2,1)S(1)}, u32[]{:S(2)}, u32[]{:S(2)}) collective-permute-start(bf16[2,256,512]{2,1,0:T(8,128)(2,1)S(1)} %shard_map.89.refs_0_), channel_id=1, source_target_pairs={{0,384},{192,576},{384,0},{576,192},{1,385},{193,577},{385,1},{577... | collective-permute-start | bytes 1572872 | tf_op jit(solution)/shard_map/ppermute | solution.py:240
  50.9 22.5 %collective-permute-start.5 = (bf16[2,256,512]{2,1,0:T(8,128)(2,1)S(1)}, bf16[2,256,512]{2,1,0:T(8,128)(2,1)S(1)}, u32[]{:S(2)}, u32[]{:S(2)}) collective-permute-start(bf16[2,256,512]{2,1,0:T(8,128)(2,1)S(1)} %shard_map.89.refs_0_), channel_id=1, source_target_pairs={{0,576},{192,0},{384,192},{576,384},{1,577},{193,1},{385,193},{577... | collective-permute-start | bytes 1572872 | tf_op jit(solution)/shard_map/ppermute | solution.py:240
  71.9 0.8 copy-start.6
  73.4 0.8 copy-start.8
  74.2 1.0 copy-start.7
  75.2 1.0 copy-start.9
  76.4 40.0 %copy-start.3 = (bf16[128,4096]{1,0:T(8,128)(2,1)S(1)}, bf16[128,4096]{1,0:T(8,128)(2,1)}, u32[]{:S(2)}) copy-start(bf16[128,4096]{1,0:T(8,128)(2,1)} %refs_1_.3) | copy-start | bytes 3145732
  76.4 40.0 %copy-start.11 = (bf16[128,512]{1,0:T(8,128)(2,1)S(1)}, bf16[128,512]{1,0:T(8,128)(2,1)}, u32[]{:S(2)}) copy-start(bf16[128,512]{1,0:T(8,128)(2,1)} %refs_2_.2) | copy-start | bytes 393220
  76.4 32.8 %collective-permute-start.6 = (bf16[4,2,256,512]{3,2,1,0:T(8,128)(2,1)S(1)}, bf16[4,2,256,512]{3,2,1,0:T(8,128)(2,1)S(1)}, u32[]{:S(2)}, u32[]{:S(2)}) collective-permute-start(bf16[4,2,256,512]{3,2,1,0:T(8,128)(2,1)S(1)} %shard_map.90.refs_3_), channel_id=1, source_target_pairs={{0,1},{1,0},{2,3},{3,2},{4,5},{5,4},{6,7},{7,6},{8,9},{9,8},{10,11... | collective-permute-start | bytes 6291464 | tf_op jit(solution)/shard_map/ppermute | solution.py:249
  80.0 5.7 %collective-permute-start.2 = (bf16[32,512]{1,0:T(8,128)(2,1)S(1)}, bf16[32,512]{1,0:T(8,128)(2,1)S(1)}, u32[]{:S(2)}, u32[]{:S(2)}) collective-permute-start(bf16[32,512]{1,0:T(8,128)(2,1)S(1)} %get-tuple-element.19), channel_id=1, source_target_pairs={{0,2},{2,0},{1,3},{3,1},{4,6},{6,4},{5,7},{7,5},{8,10},{10,8},{9,1... | collective-permute-start | bytes 98312 | tf_op jit(solution)/shard_map/ppermute | solution.py:247
  109.9 1.3 copy-start
  111.3 12.0 %all-to-all-start.3 = ((bf16[8,32,512]{2,1,0:T(8,128)(2,1)}), bf16[8,32,512]{2,1,0:T(8,128)(2,1)S(1)}, u32[]{:S(2)}, u32[]{:S(2)}) async-start(bf16[8,32,512]{2,1,0:T(8,128)(2,1)} %shard_map.91), calls=%async_computation.3 | async-start | bytes 524288 | tf_op jit(solution)/shard_map/all_to_all | solution.py:260
  116.4 1.6 %copy-start.1 = (bf16[4,2,256,512]{3,2,1,0:T(8,128)(2,1)S(1)}, bf16[4,2,256,512]{3,2,1,0:T(8,128)(2,1)}, u32[]{:S(2)}) copy-start(bf16[4,2,256,512]{3,2,1,0:T(8,128)(2,1)} %copy-done) | copy-start | bytes 6291460
  123.3 1.0 copy-start.5
  125.8 14.4 %collective-permute-start.7 = (bf16[256,512]{1,0:T(8,128)(2,1)S(1)}, bf16[256,512]{1,0:T(8,128)(2,1)S(1)}, u32[]{:S(2)}, u32[]{:S(2)}) collective-permute-start(bf16[256,512]{1,0:T(8,128)(2,1)S(1)} %get-tuple-element.25), channel_id=1, source_target_pairs={{0,1},{1,0},{2,3},{3,2},{4,5},{5,4},{6,7},{7,6},{8,9},{9,8},{10,11... | collective-permute-start | bytes 786440 | tf_op jit(solution)/shard_map/ppermute | solution.py:277
  134.0 15.2 %all-to-all-start.4 = ((f32[8,2,128]{2,1,0:T(2,128)}), f32[8,2,128]{2,1,0:T(2,128)S(1)}, u32[]{:S(2)}, u32[]{:S(2)}) async-start(f32[8,2,128]{2,1,0:T(2,128)} %get-tuple-element.24), calls=%async_computation.4 | async-start | bytes 16384 | tf_op jit(solution)/shard_map/all_to_all | solution.py:276
  149.1 4.2 %collective-permute-start.8 = (f32[8,2,128]{2,1,0:T(2,128)S(1)}, f32[8,2,128]{2,1,0:T(2,128)S(1)}, u32[]{:S(2)}, u32[]{:S(2)}) collective-permute-start(f32[8,2,128]{2,1,0:T(2,128)S(1)} %all-to-all-done.4.refs_1_), channel_id=1, source_target_pairs={{0,1},{1,0},{2,3},{3,2},{4,5},{5,4},{6,7},{7,6},{8,9},{9,8},{10,11... | collective-permute-start | bytes 24584 | tf_op jit(solution)/shard_map/ppermute | solution.py:281

commit v4 on v3

--- a/solution.py
+++ b/solution.py
@@ -38,7 +38,7 @@
             out_ref[:, columns] = (codes_ref[rows, columns].astype(F32) * factor).astype(BF16)
 
 
-def prepare_kernel(hidden_ref, cot_ref, sent_ref, hidden, cot, come, go):
+def prepare_kernel(hidden_ref, cot_ref, sent_ref, mark_ref, hidden, cot, come, go):
     peers, tok, part = hidden.shape
     loads = [
         pltpu.make_async_copy(hidden_ref.at[:, pl.ds(i * part, part)], hidden.at[i], come.at[i]) for i in range(peers)
@@ -60,6 +60,7 @@
     for i in range(peers):
         stores.append(pltpu.make_async_copy(cot, sent_ref.at[i, :, pl.ds(part, cot.shape[1])], go.at[peers + i]))
         stores[-1].start()
+    mark_ref[...] = square[:8]
     for store in stores:
         store.wait()
 
@@ -83,24 +84,30 @@
             out_ref[g] = value.astype(out_ref.dtype)
 
 
-def finish_kernel(place_ref, total_ref, codes_ref, scales_ref, gain_ref, grad_ref, part_ref):
+def dots_kernel(place_ref, total_ref, codes_ref, scales_ref, part_ref):
     half, cols = total_ref.shape
     blocks = scales_ref.shape[0]
     rows = pl.ds(pl.multiple_of(place_ref[0] * half, half), half)
-    gain = down(gain_ref[:, rows].astype(F32))
     dots = jnp.zeros((half, LANES), F32)
     for b in range(blocks):
         scale = down(scales_ref[b : b + 1, rows].astype(F32))
         for at in range(b * cols // blocks, (b + 1) * cols // blocks, LANES):
             columns = slice(at, at + LANES)
-            value = total_ref[:, columns].astype(F32)
             weight = (codes_ref[rows, columns].astype(F32) * scale).astype(BF16)
-            dots = dots + value * weight.astype(F32)
-            grad_ref[:, columns] = (value * gain).astype(BF16)
+            dots = dots + total_ref[:, columns].astype(F32) * weight.astype(F32)
     for i in range(half // LANES):
         row = jnp.sum(dots[i * LANES : (i + 1) * LANES].T, axis=0, keepdims=True)
         for peer in range(part_ref.shape[0]):
             part_ref[peer, i : i + 1, :] = row
+
+
+def finish_kernel(place_ref, total_ref, gain_ref, grad_ref):
+    half, cols = total_ref.shape
+    rows = pl.ds(pl.multiple_of(place_ref[0] * half, half), half)
+    gain = down(gain_ref[:, rows].astype(F32))
+    for at in range(0, cols, LANES):
+        columns = slice(at, at + LANES)
+        grad_ref[:, columns] = (total_ref[:, columns].astype(F32) * gain).astype(BF16)
 
 
 def tokens_kernel(place_ref, hidden_ref, cot_ref, own_ref, other_ref, keys_ref, grad_ref):
@@ -203,23 +210,23 @@
     place = jnp.stack([lax.axis_index(a) for a in ("c", "x", "yh", "zp")]).astype(jnp.int32)
     scales, gain = key_scales.T, norm_gain[None]
 
-    sent = pl.pallas_call(
+    sent, mark = pl.pallas_call(
         prepare_kernel,
-        out_shape=shape((nx, tok, part + cols), BF16),
+        out_shape=[shape((nx, tok, part + cols), BF16), shape((8, 1), F32)],
         in_specs=[HBM] * 2,
-        out_specs=HBM,
+        out_specs=[HBM, VMEM],
         scratch_shapes=[
             pltpu.VMEM((nx, tok, part), BF16),
             pltpu.VMEM((tok, cols), BF16),
             pltpu.SemaphoreType.DMA((nx + 1,)),
             pltpu.SemaphoreType.DMA((2 * nx,)),
         ],
-        compiler_params=PARAMS,
+        compiler_params=pltpu.CompilerParams(vmem_limit_bytes=60 * 1024 * 1024),
         cost_estimate=pl.CostEstimate(flops=4 * tok * width, bytes_accessed=4 * tok * width, transcendentals=0),
     )(hidden_in, key_cotangent)
     got = lax.all_to_all(sent, "x", 0, 0)
 
-    mine = call(gained_kernel, shape((half, cols), BF16), [SMEM, VMEM, VMEM, VMEM], half * cols, 4 * half * cols, [sent])(
+    mine = call(gained_kernel, shape((half, cols), BF16), [SMEM, VMEM, VMEM, VMEM], half * cols, 4 * half * cols, [mark])(
         place, key_codes, scales, gain
     )
     mate = lax.ppermute(mine, "yh", SWAP)
@@ -240,42 +247,45 @@
     own = [pair] + [lax.ppermute(pair, "x", [(i, (i + s) % nx) for i in range(nx)]) for s in range(1, nx)]
     terms = lax.all_to_all(product.reshape(nh * nl, quarter, cols), ("yh", "yl"), 0, 0)
     keep, send = call(
-        halve_kernel, [shape((eighth, cols), BF16)] * 2, [SMEM, VMEM], nh * nl * quarter * cols, 2 * half * cols
+        halve_kernel, [shape((eighth, cols), BF16)] * 2, [SMEM, VMEM], nh * nl * quarter * cols, 2 * half * cols, [own[1], own[-1]]
     )(place, terms)
     copies = call(
         add_kernel, shape((nz, eighth, cols), BF16), [VMEM, VMEM], eighth * cols, 2 * nz * eighth * cols
     )(keep, lax.ppermute(send, "zp", SWAP))
-    own = call(stack_kernel, shape((nx, nh, half, cols), BF16), [VMEM] * nx, 0, 4 * width * cols, [keep])(*own)
-    other = lax.ppermute(own, "c", SWAP)
     scale = float(total_tokens) ** -0.5
+    terms = lax.all_to_all(copies, "z", 0, 0)
     copies = call(
         functools.partial(total_kernel, scale),
         shape((nl * np, eighth, cols), BF16),
         [VMEM],
         nz * eighth * cols,
         2 * (nz + nl * np) * eighth * cols,
-        [other],
-    )(lax.all_to_all(copies, "z", 0, 0))
+    )(terms)
 
     whole = lax.all_to_all(copies, ("yl", "zp"), 0, 0).reshape(half, cols)
+    own = call(stack_kernel, shape((nx, nh, half, cols), BF16), [VMEM] * nx, 0, 4 * width * cols, [copies])(*own)
+    other = lax.ppermute(own, "c", SWAP)
+    gain_half = call(
+        dots_kernel,
+        shape((nx * nh, half // LANES, LANES), F32),
+        [SMEM, VMEM, VMEM, VMEM],
+        2 * half * cols,
+        4 * half * cols,
+    )(place, whole, key_codes, scales)
+    grad_half = call(
+        finish_kernel, shape((half, cols), BF16), [SMEM, VMEM, VMEM], half * cols, 4 * half * cols, [gain_half]
+    )(place, whole, gain)
     keys_out, input_gradient = call(
         tokens_kernel,
         [shape((tok, cols), BF16), shape((tok, width), BF16)],
         [SMEM, VMEM, VMEM, VMEM, VMEM],
         4 * tok * width * cols,
         4 * tok * width + 2 * width * cols,
+        [grad_half],
     )(place, hidden_in, key_cotangent, own, other)
-    whole, keys_out = tie(whole, keys_out)
-    grad_half, gain_half = call(
-        finish_kernel,
-        [shape((half, cols), BF16), shape((nx * nh, half // LANES, LANES), F32)],
-        [SMEM, VMEM, VMEM, VMEM, VMEM],
-        4 * half * cols,
-        6 * half * cols,
-    )(place, whole, key_codes, scales, gain)
     gains = lax.all_to_all(gain_half, ("x", "yh"), 0, 0)
     weight_grad = jnp.concatenate(by_core(grad_half, lax.ppermute(grad_half, "c", SWAP)), axis=0)
-    gains, weight_grad = tie(gains, weight_grad)
+    gains, keys_out = tie(gains, keys_out)
     gain_gradient = call(
         gains_kernel, shape((width // LANES, LANES), F32), [SMEM, VMEM, VMEM], width, 8 * width
     )(place, gains, lax.ppermute(gains, "c", SWAP)).reshape(width)

time: 155 us -> 140 us (0.903)
  waiting for transfers between devices: 35.9 us -> 19.6 us
  blocking collectives: 23.4 us -> 36.2 us
  local copies, waits for them, and re-layouts: 9.8 us -> 1.08 us
  starting transfers between devices: 71 us -> 63.2 us
  other arithmetic: 1.91 us -> 4.73 us
  Pallas kernels: 11.6 us -> 13.9 us
    all_to_all x1 -> x2, blocking collectives: 23.4 us -> 36.2 us  [the longest x1 23.5 us: body(): terms = lax.all_to_all(copies, 'z', 0, 0)]
    unnamed x28 -> x18, local copies, waits for them, and re-layouts: 9.79 us -> 1.08 us
    all_to_all x1, waiting for transfers between devices: 7.65 us -> 0.37 us  [body(): lax.all_to_all(product.reshape(nh * nl, quarter, cols), ('yh', 'yl'), 0, 0)]
    all_to_all x1, waiting for transfers between devices: 8.06 us -> 2.35 us  [body(): gains = lax.all_to_all(gain_half, ('x', 'yh'), 0, 0)]
    all_to_all x1 -> x0, starting transfers between devices: 5.1 us -> none  [body(): whole = lax.all_to_all(copies, ('yl', 'zp'), 0, 0).reshape(half, cols)]
    ppermute x1, starting transfers between devices: 8.19 us -> 3.58 us  [body(): lax.ppermute(grad_half, 'c', SWAP)]
    ppermute x1, starting transfers between devices: 3.6 us -> 5.78 us  [body(): other = lax.ppermute(own, 'c', SWAP)]
    select_n x1, other arithmetic: 0.04 us -> 1.8 us  [by_core(): return (jnp.where(first, own, other), jnp.where(first, other, own))]
  transfers between devices with their start and end apart: 13 -> 12, of which waited for: 10 -> 7; matrix products, arithmetic and copies ran while one was open for 1% -> 3% of each run, Pallas kernels for 3% -> 5%
where the time goes in v4:
time: 140 us
  starting transfers between devices  63.2 us (45%)
  blocking collectives  36.2 us (26%)
  waiting for transfers between devices  19.6 us (14%)
  Pallas kernels  13.9 us (10%)
  other arithmetic  4.73 us (3%)
    all_to_all x1, blocking collectives, body(): terms = lax.all_to_all(copies, 'z', 0, 0)  23.5 us
    ppermute x1, starting transfers between devices, body(): product = (keep + lax.ppermute(send, 'c', SWAP).astype(F32)).astype(BF16)  13.8 us
    all_to_all x1, blocking collectives, body(): whole = lax.all_to_all(copies, ('yl', 'zp'), 0, 0).reshape(half, cols)  12.7 us
    ppermute x3, waiting for transfers between devices, body(): lax.ppermute(pair, 'x', [(i, (i + s) % nx) for i in range(nx)])  11 us
    pallas_call x11, Pallas kernels, call(): return lambda *operands: made(*operands, *after)  10.8 us
    ppermute x3, starting transfers between devices, body(): lax.ppermute(pair, 'x', [(i, (i + s) % nx) for i in range(nx)])  10.7 us
    ppermute x1, starting transfers between devices, body(): mate = lax.ppermute(mine, 'yh', SWAP)  7.45 us
    ppermute x1, starting transfers between devices, body(): other = lax.ppermute(own, 'c', SWAP)  5.78 us
  transfers between devices with their start and end apart: 12, of which 7 were waited for; matrix products, arithmetic and copies ran while one was open for 3% of the time, Pallas kernels for 5%

profile of v4, /device:TPU:1, one launch (start us, length us, event | category | flops | bytes accessed | tf_op | source)
XLA Modules:
  0.0 139.6 jit_solution(5603357541841228624)
XLA Ops:
  0.6 0.0 copy-start.8
  0.6 0.0 copy-start.6
  0.7 0.0 copy-start.3
  0.7 3.1 %shard_map.84 = (bf16[4,128,1536]{2,1,0:T(8,128)(2,1)}, f32[8,1]{1,0:T(8,128)}) custom-call(bf16[128,4096]{1,0:T(8,128)(2,1)} %refs_1_.3, bf16[128,512]{1,0:T(8,128)(2,1)} %refs_2_.3), custom_call_target="tpu_custom_call" | custom-call | flops 2097152 | bytes 2097152 | tf_op jit(solution)/shard_map/pallas_call | solution.py:213
  3.8 0.0 copy-start.7
  3.8 4.9 %all-to-all-start = ((bf16[4,128,1536]{2,1,0:T(8,128)(2,1)}), bf16[4,128,1536]{2,1,0:T(8,128)(2,1)S(1)}, u32[]{:S(2)}, u32[]{:S(2)}) async-start(bf16[4,128,1536]{2,1,0:T(8,128)(2,1)} %get-tuple-element.14), calls=%async_computation | async-start | bytes 3145728 | tf_op jit(solution)/shard_map/all_to_all | solution.py:227
  8.6 0.0 copy-done.8
  8.6 0.1 pad_add_fusion.refs_0_
  8.7 0.0 copy-done.6
  8.7 0.0 copy-done.3
  8.7 0.0 copy-done.7
  8.7 0.7 shard_map.85.refs_0_
  9.4 7.5 %collective-permute-start = (bf16[256,512]{1,0:T(8,128)(2,1)S(1)}, bf16[256,512]{1,0:T(8,128)(2,1)S(1)}, u32[]{:S(2)}, u32[]{:S(2)}) collective-permute-start(bf16[256,512]{1,0:T(8,128)(2,1)S(1)} %shard_map.85.refs_0_), channel_id=1, source_target_pairs={{0,96},{96,0},{1,97},{97,1},{2,98},{98,2},{3,99},{99,3},{4,100},{1... | collective-permute-start | bytes 786440 | tf_op jit(solution)/shard_map/ppermute | solution.py:232
  16.9 3.8 %collective-permute-done.refs_2_.refs_1_ = bf16[256,512]{1,0:T(8,128)(2,1)S(1)} collective-permute-done((bf16[256,512]{1,0:T(8,128)(2,1)S(1)}, bf16[256,512]{1,0:T(8,128)(2,1)S(1)}, u32[]{:S(2)}, u32[]{:S(2)}) %collective-permute-start) | collective-permute-done | bytes 262176 | tf_op jit(solution)/shard_map/ppermute | solution.py:232
  20.7 0.5 all-to-all-done.refs_1_
  21.2 1.3 shard_map.86
  22.5 13.8 %collective-permute-start.1 = (bf16[2,256,512]{2,1,0:T(8,128)(2,1)S(1)}, bf16[2,256,512]{2,1,0:T(8,128)(2,1)S(1)}, u32[]{:S(2)}, u32[]{:S(2)}) collective-permute-start(bf16[2,256,512]{2,1,0:T(8,128)(2,1)S(1)} %get-tuple-element.17), channel_id=1, source_target_pairs={{0,1},{1,0},{2,3},{3,2},{4,5},{5,4},{6,7},{7,6},{8,9},{9,8},{10,11... | collective-permute-start | bytes 1572872 | tf_op jit(solution)/shard_map/ppermute | solution.py:242
  36.3 1.5 %collective-permute-done.1 = bf16[2,256,512]{2,1,0:T(8,128)(2,1)S(1)} collective-permute-done((bf16[2,256,512]{2,1,0:T(8,128)(2,1)S(1)}, bf16[2,256,512]{2,1,0:T(8,128)(2,1)S(1)}, u32[]{:S(2)}, u32[]{:S(2)}) %collective-permute-start.1) | collective-permute-done | bytes 524320 | tf_op jit(solution)/shard_map/ppermute | solution.py:242
  37.8 1.0 add_convert_fusion.refs_2_
  38.8 4.0 %all-to-all-start.1 = ((bf16[8,64,512]{2,1,0:T(8,128)(2,1)}), bf16[8,64,512]{2,1,0:T(8,128)(2,1)S(1)}, u32[]{:S(2)}, u32[]{:S(2)}) async-start(bf16[8,64,512]{2,1,0:T(8,128)(2,1)} %bitcast.5), calls=%async_computation.1 | async-start | bytes 1048576 | tf_op jit(solution)/shard_map/all_to_all | solution.py:248
  42.9 2.9 %collective-permute-start.2 = (bf16[2,256,512]{2,1,0:T(8,128)(2,1)S(1)}, bf16[2,256,512]{2,1,0:T(8,128)(2,1)S(1)}, u32[]{:S(2)}, u32[]{:S(2)}) collective-permute-start(bf16[2,256,512]{2,1,0:T(8,128)(2,1)S(1)} %shard_map.87.refs_0_), channel_id=1, source_target_pairs={{0,192},{192,384},{384,576},{576,0},{1,193},{193,385},{385,577},{5... | collective-permute-start | bytes 1572872 | tf_op jit(solution)/shard_map/ppermute | solution.py:247
  45.8 3.6 %collective-permute-start.3 = (bf16[2,256,512]{2,1,0:T(8,128)(2,1)S(1)}, bf16[2,256,512]{2,1,0:T(8,128)(2,1)S(1)}, u32[]{:S(2)}, u32[]{:S(2)}) collective-permute-start(bf16[2,256,512]{2,1,0:T(8,128)(2,1)S(1)} %shard_map.87.refs_0_), channel_id=1, source_target_pairs={{0,576},{192,0},{384,192},{576,384},{1,577},{193,1},{385,193},{577... | collective-permute-start | bytes 1572872 | tf_op jit(solution)/shard_map/ppermute | solution.py:247
  49.4 9.4 %collective-permute-done.2.refs_2_.refs_1_ = bf16[2,256,512]{2,1,0:T(8,128)(2,1)S(1)} collective-permute-done((bf16[2,256,512]{2,1,0:T(8,128)(2,1)S(1)}, bf16[2,256,512]{2,1,0:T(8,128)(2,1)S(1)}, u32[]{:S(2)}, u32[]{:S(2)}) %collective-permute-start.2) | collective-permute-done | bytes 524320 | tf_op jit(solution)/shard_map/ppermute | solution.py:247
  58.8 1.6 %collective-permute-done.3.refs_3_ = bf16[2,256,512]{2,1,0:T(8,128)(2,1)S(1)} collective-permute-done((bf16[2,256,512]{2,1,0:T(8,128)(2,1)S(1)}, bf16[2,256,512]{2,1,0:T(8,128)(2,1)S(1)}, u32[]{:S(2)}, u32[]{:S(2)}) %collective-permute-start.3) | collective-permute-done | bytes 524320 | tf_op jit(solution)/shard_map/ppermute | solution.py:247
  60.4 0.0 copy-start.1
  60.4 0.4 all-to-all-done.1.refs_1_
  60.8 0.6 shard_map.88
  61.4 4.0 %collective-permute-start.4 = (bf16[32,512]{1,0:T(8,128)(2,1)S(1)}, bf16[32,512]{1,0:T(8,128)(2,1)S(1)}, u32[]{:S(2)}, u32[]{:S(2)}) collective-permute-start(bf16[32,512]{1,0:T(8,128)(2,1)S(1)} %get-tuple-element.19), channel_id=1, source_target_pairs={{0,2},{2,0},{1,3},{3,1},{4,6},{6,4},{5,7},{7,5},{8,10},{10,8},{9,1... | collective-permute-start | bytes 98312 | tf_op jit(solution)/shard_map/ppermute | solution.py:254
  65.4 4.2 %collective-permute-start.5 = (bf16[2,256,512]{2,1,0:T(8,128)(2,1)S(1)}, bf16[2,256,512]{2,1,0:T(8,128)(2,1)S(1)}, u32[]{:S(2)}, u32[]{:S(2)}) collective-permute-start(bf16[2,256,512]{2,1,0:T(8,128)(2,1)S(1)} %shard_map.87.refs_0_), channel_id=1, source_target_pairs={{0,384},{192,576},{384,0},{576,192},{1,385},{193,577},{385,1},{577... | collective-permute-start | bytes 1572872 | tf_op jit(solution)/shard_map/ppermute | solution.py:247
  69.6 0.0 collective-permute-done.4.refs_1_
  69.6 23.5 %all_to_all.25.refs_0_ = bf16[6,32,512]{2,1,0:T(8,128)(2,1)S(1)} all-to-all(bf16[6,32,512]{2,1,0:T(8,128)(2,1)S(1)} %shard_map.89), channel_id=1, replica_groups=mesh['x'=4,'yh'=2,'yl'=4,'z'=6,'zp'=2,'c'=2] {'z'}, dimensions={0} | all-to-all | bytes 393216 | tf_op jit(solution)/shard_map/all_to_all | solution.py:256
  93.2 0.0 copy-done.1
  93.2 0.0 collective-permute-done.5.refs_2_
  93.2 0.0 copy-start.2
  93.3 1.0 copy-done.2
  94.3 0.0 copy-start.4
  94.3 0.1 shard_map.92.refs_3_
  94.4 0.0 copy-start
  94.4 0.0 copy-start.5
  94.5 5.8 %collective-permute-start.6 = (bf16[4,2,256,512]{3,2,1,0:T(8,128)(2,1)S(1)}, bf16[4,2,256,512]{3,2,1,0:T(8,128)(2,1)}, u32[]{:S(2)}, u32[]{:S(2)}) collective-permute-start(bf16[4,2,256,512]{3,2,1,0:T(8,128)(2,1)S(1)} %shard_map.92.refs_3_), channel_id=1, source_target_pairs={{0,1},{1,0},{2,3},{3,2},{4,5},{5,4},{6,7},{7,6},{8,9},{9,8},{10,11... | collective-permute-start | bytes 6291464 | tf_op jit(solution)/shard_map/ppermute | solution.py:267
  100.2 12.7 %all_to_all.26 = bf16[8,32,512]{2,1,0:T(8,128)(2,1)S(1)} all-to-all(bf16[8,32,512]{2,1,0:T(8,128)(2,1)S(1)} %shard_map.90.refs_4_), channel_id=1, replica_groups=mesh['x'=4,'yh'=2,'yl'=4,'z'=6,'zp'=2,'c'=2] {'yl','zp'}, dimensions={0} | all-to-all | bytes 524288 | tf_op jit(solution)/shard_map/all_to_all | solution.py:265
  112.9 0.0 copy-done.4
  112.9 1.4 %shard_map.91.refs_3_ = f32[8,2,128]{2,1,0:T(2,128)} custom-call(s32[4]{0:T(128)S(1)} %pad_add_fusion.refs_0_, bf16[256,512]{1,0:T(8,128)(2,1)S(1)} %bitcast.8, bf16[512,512]{1,0:T(8,128)(2,1)S(1)} %copy-done.4, bf16[2,512]{1,0:T(2,128)(2,1)S(1)} %bitcast.11), custom_call_target="tpu_custom_call" | custom-call | flops 262144 | bytes 524288 | tf_op jit(solution)/shard_map/pallas_call | solution.py:191
  114.3 0.7 shard_map.93.refs_5_
  115.0 3.6 %collective-permute-start.7 = (bf16[256,512]{1,0:T(8,128)(2,1)S(1)}, bf16[256,512]{1,0:T(8,128)(2,1)}, u32[]{:S(2)}, u32[]{:S(2)}) collective-permute-start(bf16[256,512]{1,0:T(8,128)(2,1)S(1)} %shard_map.93.refs_5_), channel_id=1, source_target_pairs={{0,1},{1,0},{2,3},{3,2},{4,5},{5,4},{6,7},{7,6},{8,9},{9,8},{10,11... | collective-permute-start | bytes 786440 | tf_op jit(solution)/shard_map/ppermute | solution.py:287
  118.6 5.7 %all-to-all-start.4 = ((f32[8,2,128]{2,1,0:T(2,128)}), f32[8,2,128]{2,1,0:T(2,128)S(1)}, u32[]{:S(2)}, u32[]{:S(2)}) async-start(f32[8,2,128]{2,1,0:T(2,128)} %shard_map.91.refs_3_), calls=%async_computation.4 | async-start | bytes 16384 | tf_op jit(solution)/shard_map/all_to_all | solution.py:286
  124.3 0.0 collective-permute-done.7
  124.3 1.8 %broadcast_select_fusion.1 = (bf16[256,512]{1,0:T(8,128)(2,1)}, bf16[256,512]{1,0:T(8,128)(2,1)}) fusion(bf16[256,512]{1,0:T(8,128)(2,1)S(1)} %shard_map.93.refs_5_, bf16[256,512]{1,0:T(8,128)(2,1)} %collective-permute-done.7, pred[]{:T(512)S(6)} %eq.3), kind=kLoop, calls=%fused_computation.3 | loop fusion | flops 262144 | bytes 1048577 | tf_op jit(solution)/shard_map/jit(_where)/select_n | solution.py:200
  126.1 0.0 collective-permute-done.6.refs_4_
  126.1 0.0 copy-done
  126.1 0.0 copy-done.5
  126.1 4.8 %shard_map.94 = (bf16[128,512]{1,0:T(8,128)(2,1)}, bf16[128,4096]{1,0:T(8,128)(2,1)}) custom-call(s32[4]{0:T(128)S(1)} %pad_add_fusion.refs_0_, bf16[128,4096]{1,0:T(8,128)(2,1)S(1)} %copy-done, bf16[128,512]{1,0:T(8,128)(2,1)S(1)} %copy-done.5, bf16[4,2,256,512]{3,2,1,0:T(8,128)(2,1)S(1)} %shard_map.92.refs_3_, ...), custom_call_target="tpu_custom_call" | custom-call | flops 1073741824 | bytes 6291456 | tf_op jit(solution)/shard_map/pallas_call | solution.py:191
  130.9 2.3 %all-to-all-done.4.refs_1_ = f32[8,2,128]{2,1,0:T(2,128)S(1)} async-done(((f32[8,2,128]{2,1,0:T(2,128)}), f32[8,2,128]{2,1,0:T(2,128)S(1)}, u32[]{:S(2)}, u32[]{:S(2)}) %all-to-all-start.4) | async-done | bytes 8224 | tf_op jit(solution)/shard_map/all_to_all | solution.py:286
  133.2 3.3 %collective-permute-start.8 = (f32[8,2,128]{2,1,0:T(2,128)S(1)}, f32[8,2,128]{2,1,0:T(2,128)S(1)}, u32[]{:S(2)}, u32[]{:S(2)}) collective-permute-start(f32[8,2,128]{2,1,0:T(2,128)S(1)} %all-to-all-done.4.refs_1_), channel_id=1, source_target_pairs={{0,1},{1,0},{2,3},{3,2},{4,5},{5,4},{6,7},{7,6},{8,9},{9,8},{10,11... | collective-permute-start | bytes 24584 | tf_op jit(solution)/shard_map/ppermute | solution.py:291
  136.6 1.9 %pad_maximum_fusion = bf16[512,512]{1,0:T(8,128)(2,1)} fusion(bf16[256,512]{1,0:T(8,128)(2,1)} %get-tuple-element.25, bf16[256,512]{1,0:T(8,128)(2,1)} %get-tuple-element.24), kind=kLoop, calls=%fused_computation.1 | loop fusion | flops 1048576 | bytes 1048576 | tf_op jit(solution)/shard_map/concatenate | solution.py:287
  138.5 0.0 collective-permute-done.8.refs_2_
  138.5 1.2 shard_map.95
  (4 shorter events, 0.1 us)
Async XLA Ops:
  0.6 8.0 %copy-start.8 = (bf16[512]{0:T(512)(128)(2,1)S(1)}, bf16[512]{0:T(512)(128)(2,1)}, u32[]{:S(2)}) copy-start(bf16[512]{0:T(512)(128)(2,1)} %param.6) | copy-start | bytes 3076
  0.6 8.1 %copy-start.6 = (bf16[512,2]{0,1:T(2,128)(2,1)S(1)}, bf16[512,2]{0,1:T(2,128)(2,1)}, u32[]{:S(2)}) copy-start(bf16[512,2]{0,1:T(2,128)(2,1)} %param.8) | copy-start | bytes 6148
  0.7 8.1 %copy-start.3 = (bf16[512,512]{1,0:T(8,128)(2,1)S(1)}, bf16[512,512]{1,0:T(8,128)(2,1)}, u32[]{:S(2)}) copy-start(bf16[512,512]{1,0:T(8,128)(2,1)} %refs_2_.2) | copy-start | bytes 1572868
  3.8 5.0 %copy-start.7 = (f32[8,1]{1,0:T(8,128)S(1)}, f32[8,1]{1,0:T(8,128)}, u32[]{:S(2)}) copy-start(f32[8,1]{1,0:T(8,128)} %get-tuple-element.15.refs_4_) | copy-start | bytes 100
  3.8 17.4 %all-to-all-start = ((bf16[4,128,1536]{2,1,0:T(8,128)(2,1)}), bf16[4,128,1536]{2,1,0:T(8,128)(2,1)S(1)}, u32[]{:S(2)}, u32[]{:S(2)}) async-start(bf16[4,128,1536]{2,1,0:T(8,128)(2,1)} %get-tuple-element.14), calls=%async_computation | async-start | bytes 3145728 | tf_op jit(solution)/shard_map/all_to_all | solution.py:227
  9.4 11.3 %collective-permute-start = (bf16[256,512]{1,0:T(8,128)(2,1)S(1)}, bf16[256,512]{1,0:T(8,128)(2,1)S(1)}, u32[]{:S(2)}, u32[]{:S(2)}) collective-permute-start(bf16[256,512]{1,0:T(8,128)(2,1)S(1)} %shard_map.85.refs_0_), channel_id=1, source_target_pairs={{0,96},{96,0},{1,97},{97,1},{2,98},{98,2},{3,99},{99,3},{4,100},{1... | collective-permute-start | bytes 786440 | tf_op jit(solution)/shard_map/ppermute | solution.py:232
  22.5 15.4 %collective-permute-start.1 = (bf16[2,256,512]{2,1,0:T(8,128)(2,1)S(1)}, bf16[2,256,512]{2,1,0:T(8,128)(2,1)S(1)}, u32[]{:S(2)}, u32[]{:S(2)}) collective-permute-start(bf16[2,256,512]{2,1,0:T(8,128)(2,1)S(1)} %get-tuple-element.17), channel_id=1, source_target_pairs={{0,1},{1,0},{2,3},{3,2},{4,5},{5,4},{6,7},{7,6},{8,9},{9,8},{10,11... | collective-permute-start | bytes 1572872 | tf_op jit(solution)/shard_map/ppermute | solution.py:242
  38.8 22.0 %all-to-all-start.1 = ((bf16[8,64,512]{2,1,0:T(8,128)(2,1)}), bf16[8,64,512]{2,1,0:T(8,128)(2,1)S(1)}, u32[]{:S(2)}, u32[]{:S(2)}) async-start(bf16[8,64,512]{2,1,0:T(8,128)(2,1)} %bitcast.5), calls=%async_computation.1 | async-start | bytes 1048576 | tf_op jit(solution)/shard_map/all_to_all | solution.py:248
  42.9 15.9 %collective-permute-start.2 = (bf16[2,256,512]{2,1,0:T(8,128)(2,1)S(1)}, bf16[2,256,512]{2,1,0:T(8,128)(2,1)S(1)}, u32[]{:S(2)}, u32[]{:S(2)}) collective-permute-start(bf16[2,256,512]{2,1,0:T(8,128)(2,1)S(1)} %shard_map.87.refs_0_), channel_id=1, source_target_pairs={{0,192},{192,384},{384,576},{576,0},{1,193},{193,385},{385,577},{5... | collective-permute-start | bytes 1572872 | tf_op jit(solution)/shard_map/ppermute | solution.py:247
  45.8 14.7 %collective-permute-start.3 = (bf16[2,256,512]{2,1,0:T(8,128)(2,1)S(1)}, bf16[2,256,512]{2,1,0:T(8,128)(2,1)S(1)}, u32[]{:S(2)}, u32[]{:S(2)}) collective-permute-start(bf16[2,256,512]{2,1,0:T(8,128)(2,1)S(1)} %shard_map.87.refs_0_), channel_id=1, source_target_pairs={{0,576},{192,0},{384,192},{576,384},{1,577},{193,1},{385,193},{577... | collective-permute-start | bytes 1572872 | tf_op jit(solution)/shard_map/ppermute | solution.py:247
  60.4 32.8 %copy-start.1 = (bf16[2,256,512]{2,1,0:T(8,128)(2,1)}, bf16[2,256,512]{2,1,0:T(8,128)(2,1)S(1)}, u32[]{:S(2)}) copy-start(bf16[2,256,512]{2,1,0:T(8,128)(2,1)S(1)} %collective-permute-done.3.refs_3_) | copy-start | bytes 1572868
  61.4 8.2 %collective-permute-start.4 = (bf16[32,512]{1,0:T(8,128)(2,1)S(1)}, bf16[32,512]{1,0:T(8,128)(2,1)S(1)}, u32[]{:S(2)}, u32[]{:S(2)}) collective-permute-start(bf16[32,512]{1,0:T(8,128)(2,1)S(1)} %get-tuple-element.19), channel_id=1, source_target_pairs={{0,2},{2,0},{1,3},{3,1},{4,6},{6,4},{5,7},{7,5},{8,10},{10,8},{9,1... | collective-permute-start | bytes 98312 | tf_op jit(solution)/shard_map/ppermute | solution.py:254
  65.4 27.8 %collective-permute-start.5 = (bf16[2,256,512]{2,1,0:T(8,128)(2,1)S(1)}, bf16[2,256,512]{2,1,0:T(8,128)(2,1)S(1)}, u32[]{:S(2)}, u32[]{:S(2)}) collective-permute-start(bf16[2,256,512]{2,1,0:T(8,128)(2,1)S(1)} %shard_map.87.refs_0_), channel_id=1, source_target_pairs={{0,384},{192,576},{384,0},{576,192},{1,385},{193,577},{385,1},{577... | collective-permute-start | bytes 1572872 | tf_op jit(solution)/shard_map/ppermute | solution.py:247
  93.2 1.0 copy-start.2
  94.3 18.6 %copy-start.4 = (bf16[512,512]{1,0:T(8,128)(2,1)S(1)}, bf16[512,512]{1,0:T(8,128)(2,1)}, u32[]{:S(2)}) copy-start(bf16[512,512]{1,0:T(8,128)(2,1)} %refs_2_.2) | copy-start | bytes 1572868
  94.4 31.7 %copy-start = (bf16[128,4096]{1,0:T(8,128)(2,1)S(1)}, bf16[128,4096]{1,0:T(8,128)(2,1)}, u32[]{:S(2)}) copy-start(bf16[128,4096]{1,0:T(8,128)(2,1)} %refs_1_.3) | copy-start | bytes 3145732
  94.4 31.7 %copy-start.5 = (bf16[128,512]{1,0:T(8,128)(2,1)S(1)}, bf16[128,512]{1,0:T(8,128)(2,1)}, u32[]{:S(2)}) copy-start(bf16[128,512]{1,0:T(8,128)(2,1)} %refs_2_.3) | copy-start | bytes 393220
  94.5 31.7 %collective-permute-start.6 = (bf16[4,2,256,512]{3,2,1,0:T(8,128)(2,1)S(1)}, bf16[4,2,256,512]{3,2,1,0:T(8,128)(2,1)}, u32[]{:S(2)}, u32[]{:S(2)}) collective-permute-start(bf16[4,2,256,512]{3,2,1,0:T(8,128)(2,1)S(1)} %shard_map.92.refs_3_), channel_id=1, source_target_pairs={{0,1},{1,0},{2,3},{3,2},{4,5},{5,4},{6,7},{7,6},{8,9},{9,8},{10,11... | collective-permute-start | bytes 6291464 | tf_op jit(solution)/shard_map/ppermute | solution.py:267
  115.0 9.3 %collective-permute-start.7 = (bf16[256,512]{1,0:T(8,128)(2,1)S(1)}, bf16[256,512]{1,0:T(8,128)(2,1)}, u32[]{:S(2)}, u32[]{:S(2)}) collective-permute-start(bf16[256,512]{1,0:T(8,128)(2,1)S(1)} %shard_map.93.refs_5_), channel_id=1, source_target_pairs={{0,1},{1,0},{2,3},{3,2},{4,5},{5,4},{6,7},{7,6},{8,9},{9,8},{10,11... | collective-permute-start | bytes 786440 | tf_op jit(solution)/shard_map/ppermute | solution.py:287
  118.6 14.7 %all-to-all-start.4 = ((f32[8,2,128]{2,1,0:T(2,128)}), f32[8,2,128]{2,1,0:T(2,128)S(1)}, u32[]{:S(2)}, u32[]{:S(2)}) async-start(f32[8,2,128]{2,1,0:T(2,128)} %shard_map.91.refs_3_), calls=%async_computation.4 | async-start | bytes 16384 | tf_op jit(solution)/shard_map/all_to_all | solution.py:286
  133.2 5.2 %collective-permute-start.8 = (f32[8,2,128]{2,1,0:T(2,128)S(1)}, f32[8,2,128]{2,1,0:T(2,128)S(1)}, u32[]{:S(2)}, u32[]{:S(2)}) collective-permute-start(f32[8,2,128]{2,1,0:T(2,128)S(1)} %all-to-all-done.4.refs_1_), channel_id=1, source_target_pairs={{0,1},{1,0},{2,3},{3,2},{4,5},{5,4},{6,7},{7,6},{8,9},{9,8},{10,11... | collective-permute-start | bytes 24584 | tf_op jit(solution)/shard_map/ppermute | solution.py:291

commit v5 on v4

--- a/solution.py
+++ b/solution.py
@@ -84,30 +84,50 @@
             out_ref[g] = value.astype(out_ref.dtype)
 
 
-def dots_kernel(place_ref, total_ref, codes_ref, scales_ref, part_ref):
+def marked_stack_kernel(*refs):
+    stack_kernel(*refs[:-1])
+    refs[-1][...] = refs[0][0, :16, :LANES]
+
+
+def row_dots(at, total_ref, codes_ref, scales_ref):
     half, cols = total_ref.shape
     blocks = scales_ref.shape[0]
-    rows = pl.ds(pl.multiple_of(place_ref[0] * half, half), half)
+    rows = pl.ds(pl.multiple_of(at, half), half)
     dots = jnp.zeros((half, LANES), F32)
     for b in range(blocks):
         scale = down(scales_ref[b : b + 1, rows].astype(F32))
-        for at in range(b * cols // blocks, (b + 1) * cols // blocks, LANES):
-            columns = slice(at, at + LANES)
+        for c in range(b * cols // blocks, (b + 1) * cols // blocks, LANES):
+            columns = slice(c, c + LANES)
             weight = (codes_ref[rows, columns].astype(F32) * scale).astype(BF16)
             dots = dots + total_ref[:, columns].astype(F32) * weight.astype(F32)
-    for i in range(half // LANES):
-        row = jnp.sum(dots[i * LANES : (i + 1) * LANES].T, axis=0, keepdims=True)
-        for peer in range(part_ref.shape[0]):
-            part_ref[peer, i : i + 1, :] = row
-
-
-def finish_kernel(place_ref, total_ref, gain_ref, grad_ref):
-    half, cols = total_ref.shape
-    rows = pl.ds(pl.multiple_of(place_ref[0] * half, half), half)
-    gain = down(gain_ref[:, rows].astype(F32))
-    for at in range(0, cols, LANES):
-        columns = slice(at, at + LANES)
-        grad_ref[:, columns] = (total_ref[:, columns].astype(F32) * gain).astype(BF16)
+    parts = [dots[i : i + LANES].T for i in range(0, half, LANES)]
+    return [jnp.sum(part, axis=0, keepdims=True) for part in parts]
+
+
+def dots_kernel(place_ref, total_ref, codes_ref, scales_ref, part_ref):
+    for i, row in enumerate(row_dots(place_ref[0] * total_ref.shape[0], total_ref, codes_ref, scales_ref)):
+        part_ref[i : i + 1, :] = row
+
+
+def pair_dots_kernel(place_ref, own_ref, total_ref, codes_ref, scales_ref, part_ref):
+    core = place_ref[0]
+    deep = own_ref.shape[0]
+    found = row_dots((1 - core) * total_ref.shape[0], total_ref, codes_ref, scales_ref)
+    for peer in range(part_ref.shape[0]):
+        part_ref[peer, pl.ds(core * deep, deep), :] = own_ref[...]
+        for i, row in enumerate(found):
+            part_ref[peer, pl.ds((1 - core) * deep + i, 1), :] = row
+
+
+def finish_kernel(place_ref, own_ref, other_ref, gain_ref, grad_ref):
+    half, cols = own_ref.shape
+    core = place_ref[0]
+    for ref, which in ((own_ref, core), (other_ref, 1 - core)):
+        rows = pl.ds(pl.multiple_of(which * half, half), half)
+        gain = down(gain_ref[:, rows].astype(F32))
+        for at in range(0, cols, LANES):
+            columns = slice(at, at + LANES)
+            grad_ref[rows, columns] = (ref[:, columns].astype(F32) * gain).astype(BF16)
 
 
 def tokens_kernel(place_ref, hidden_ref, cot_ref, own_ref, other_ref, keys_ref, grad_ref):
@@ -166,14 +186,6 @@
         copies_ref[i] = total
 
 
-def gains_kernel(place_ref, own_ref, other_ref, out_ref):
-    groups, deep, _ = own_ref.shape
-    core = place_ref[0]
-    for g in range(groups):
-        for ref, which in ((own_ref, core), (other_ref, 1 - core)):
-            out_ref[pl.ds((g * 2 + which) * deep, deep), :] = ref[g]
-
-
 def call(kernel, outs, specs, flops, moved, after=()):
     count = len(specs)
 
@@ -193,11 +205,6 @@
 
 def tie(*values):
     return lax.optimization_barrier(values)
-
-
-def by_core(own, other):
-    first = lax.axis_index("c") == 0
-    return jnp.where(first, own, other), jnp.where(first, other, own)
 
 
 def body(hidden_in, norm_gain, key_codes, key_scales, key_cotangent):
@@ -253,42 +260,48 @@
         add_kernel, shape((nz, eighth, cols), BF16), [VMEM, VMEM], eighth * cols, 2 * nz * eighth * cols
     )(keep, lax.ppermute(send, "zp", SWAP))
     scale = float(total_tokens) ** -0.5
-    terms = lax.all_to_all(copies, "z", 0, 0)
     copies = call(
-        functools.partial(total_kernel, scale),
+        functools.partial(total_kernel, float(total_tokens) ** -0.5),
         shape((nl * np, eighth, cols), BF16),
         [VMEM],
         nz * eighth * cols,
         2 * (nz + nl * np) * eighth * cols,
-    )(terms)
+    )(lax.all_to_all(copies, "z", 0, 0))
 
     whole = lax.all_to_all(copies, ("yl", "zp"), 0, 0).reshape(half, cols)
-    own = call(stack_kernel, shape((nx, nh, half, cols), BF16), [VMEM] * nx, 0, 4 * width * cols, [copies])(*own)
+    own, mark = call(
+        marked_stack_kernel,
+        [shape((nx, nh, half, cols), BF16), shape((16, LANES), BF16)],
+        [VMEM] * nx,
+        0,
+        4 * width * cols,
+        [copies],
+    )(*own)
     other = lax.ppermute(own, "c", SWAP)
-    gain_half = call(
-        dots_kernel,
-        shape((nx * nh, half // LANES, LANES), F32),
-        [SMEM, VMEM, VMEM, VMEM],
+    beside = lax.ppermute(whole, "c", SWAP)
+    mine = call(
+        dots_kernel, shape((half // LANES, LANES), F32), [SMEM, VMEM, VMEM, VMEM], 2 * half * cols, 4 * half * cols, [mark]
+    )(place, whole, key_codes, scales)
+    gain_part = call(
+        pair_dots_kernel,
+        shape((nx * nh, rows // LANES, LANES), F32),
+        [SMEM, VMEM, VMEM, VMEM, VMEM],
         2 * half * cols,
         4 * half * cols,
-    )(place, whole, key_codes, scales)
-    grad_half = call(
-        finish_kernel, shape((half, cols), BF16), [SMEM, VMEM, VMEM], half * cols, 4 * half * cols, [gain_half]
-    )(place, whole, gain)
+    )(place, mine, beside, key_codes, scales)
+    gain_gradient = lax.all_to_all(gain_part, ("x", "yh"), 0, 0).reshape(width)
+    weight_grad = call(
+        finish_kernel, shape((rows, cols), BF16), [SMEM, VMEM, VMEM, VMEM], rows * cols, 4 * rows * cols, [gain_part]
+    )(place, whole, beside, gain)
     keys_out, input_gradient = call(
         tokens_kernel,
         [shape((tok, cols), BF16), shape((tok, width), BF16)],
         [SMEM, VMEM, VMEM, VMEM, VMEM],
         4 * tok * width * cols,
         4 * tok * width + 2 * width * cols,
-        [grad_half],
+        [gain_part],
     )(place, hidden_in, key_cotangent, own, other)
-    gains = lax.all_to_all(gain_half, ("x", "yh"), 0, 0)
-    weight_grad = jnp.concatenate(by_core(grad_half, lax.ppermute(grad_half, "c", SWAP)), axis=0)
-    gains, keys_out = tie(gains, keys_out)
-    gain_gradient = call(
-        gains_kernel, shape((width // LANES, LANES), F32), [SMEM, VMEM, VMEM], width, 8 * width
-    )(place, gains, lax.ppermute(gains, "c", SWAP)).reshape(width)
+    gain_gradient, keys_out = tie(gain_gradient, keys_out)
     return (keys_out, input_gradient, weight_grad, gain_gradient)
 
 

time: 140 us -> 135 us (0.964)
  other arithmetic: 4.73 us -> 1.04 us
  starting transfers between devices: 63.2 us -> 59.9 us
  Pallas kernels: 13.9 us -> 16.5 us
    ppermute x2 -> x1, starting transfers between devices: 6.91 us -> 3.56 us  [body(): beside = lax.ppermute(whole, 'c', SWAP)]
    pallas_call x11, Pallas kernels: 10.8 us -> 13.3 us  [call(): return lambda *operands: made(*operands, *after)]
    concatenate x1 -> x0, other arithmetic: 1.86 us -> none  [body(): jnp.concatenate(by_core(grad_half, lax.ppermute(grad_half, 'c', SWAP)), a...]
    select_n x1 -> x0, other arithmetic: 1.8 us -> none  [by_core(): return (jnp.where(first, own, other), jnp.where(first, other, own))]
  transfers between devices with their start and end apart: 12 -> 11, of which waited for: 7 -> 8; matrix products, arithmetic and copies ran while one was open for 3% -> 0% of each run, Pallas kernels for 5% -> 7%
where the time goes in v5:
time: 135 us
  starting transfers between devices  59.9 us (44%)
  blocking collectives  36.2 us (27%)
  waiting for transfers between devices  19.6 us (15%)
  Pallas kernels  16.5 us (12%)
    all_to_all x1, blocking collectives, body(): lax.all_to_all(copies, 'z', 0, 0)  23.5 us
    ppermute x1, starting transfers between devices, body(): product = (keep + lax.ppermute(send, 'c', SWAP).astype(F32)).astype(BF16)  13.8 us
    pallas_call x11, Pallas kernels, call(): return lambda *operands: made(*operands, *after)  13.3 us
    all_to_all x1, blocking collectives, body(): whole = lax.all_to_all(copies, ('yl', 'zp'), 0, 0).reshape(half, cols)  12.7 us
    ppermute x3, waiting for transfers between devices, body(): lax.ppermute(pair, 'x', [(i, (i + s) % nx) for i in range(nx)])  11 us
    ppermute x3, starting transfers between devices, body(): lax.ppermute(pair, 'x', [(i, (i + s) % nx) for i in range(nx)])  10.7 us
    ppermute x1, starting transfers between devices, body(): mate = lax.ppermute(mine, 'yh', SWAP)  7.45 us
    ppermute x1, starting transfers between devices, body(): other = lax.ppermute(own, 'c', SWAP)  5.76 us
  transfers between devices with their start and end apart: 11, of which 8 were waited for; matrix products, arithmetic and copies ran while one was open for 0% of the time, Pallas kernels for 7%

profile of v5, /device:TPU:1, one launch (start us, length us, event | category | flops | bytes accessed | tf_op | source)
XLA Modules:
  0.0 134.6 jit_solution(12831325732081283865)
XLA Ops:
  0.6 0.0 copy-start.5
  0.6 0.0 copy-start.3
  0.7 0.0 copy-start
  0.7 3.2 %shard_map.84 = (bf16[4,128,1536]{2,1,0:T(8,128)(2,1)}, f32[8,1]{1,0:T(8,128)}) custom-call(bf16[128,4096]{1,0:T(8,128)(2,1)} %refs_1_.3, bf16[128,512]{1,0:T(8,128)(2,1)} %refs_2_.3), custom_call_target="tpu_custom_call" | custom-call | flops 2097152 | bytes 2097152 | tf_op jit(solution)/shard_map/pallas_call | solution.py:220
  3.8 0.0 copy-start.4
  3.8 4.9 %all-to-all-start = ((bf16[4,128,1536]{2,1,0:T(8,128)(2,1)}), bf16[4,128,1536]{2,1,0:T(8,128)(2,1)S(1)}, u32[]{:S(2)}, u32[]{:S(2)}) async-start(bf16[4,128,1536]{2,1,0:T(8,128)(2,1)} %get-tuple-element.16), calls=%async_computation | async-start | bytes 3145728 | tf_op jit(solution)/shard_map/all_to_all | solution.py:234
  8.7 0.0 copy-done.5
  8.7 0.1 pad_add_fusion.refs_0_
  8.8 0.0 copy-done.3
  8.8 0.0 copy-done
  8.8 0.0 copy-done.4
  8.8 0.7 shard_map.85.refs_0_
  9.5 7.5 %collective-permute-start = (bf16[256,512]{1,0:T(8,128)(2,1)S(1)}, bf16[256,512]{1,0:T(8,128)(2,1)S(1)}, u32[]{:S(2)}, u32[]{:S(2)}) collective-permute-start(bf16[256,512]{1,0:T(8,128)(2,1)S(1)} %shard_map.85.refs_0_), channel_id=1, source_target_pairs={{0,96},{96,0},{1,97},{97,1},{2,98},{98,2},{3,99},{99,3},{4,100},{1... | collective-permute-start | bytes 786440 | tf_op jit(solution)/shard_map/ppermute | solution.py:239
  17.0 3.8 %collective-permute-done.refs_2_.refs_1_ = bf16[256,512]{1,0:T(8,128)(2,1)S(1)} collective-permute-done((bf16[256,512]{1,0:T(8,128)(2,1)S(1)}, bf16[256,512]{1,0:T(8,128)(2,1)S(1)}, u32[]{:S(2)}, u32[]{:S(2)}) %collective-permute-start) | collective-permute-done | bytes 262176 | tf_op jit(solution)/shard_map/ppermute | solution.py:239
  20.8 0.5 all-to-all-done.refs_1_
  21.2 1.3 shard_map.86
  22.5 13.8 %collective-permute-start.1 = (bf16[2,256,512]{2,1,0:T(8,128)(2,1)S(1)}, bf16[2,256,512]{2,1,0:T(8,128)(2,1)S(1)}, u32[]{:S(2)}, u32[]{:S(2)}) collective-permute-start(bf16[2,256,512]{2,1,0:T(8,128)(2,1)S(1)} %get-tuple-element.19), channel_id=1, source_target_pairs={{0,1},{1,0},{2,3},{3,2},{4,5},{5,4},{6,7},{7,6},{8,9},{9,8},{10,11... | collective-permute-start | bytes 1572872 | tf_op jit(solution)/shard_map/ppermute | solution.py:249
  36.4 1.5 %collective-permute-done.1 = bf16[2,256,512]{2,1,0:T(8,128)(2,1)S(1)} collective-permute-done((bf16[2,256,512]{2,1,0:T(8,128)(2,1)S(1)}, bf16[2,256,512]{2,1,0:T(8,128)(2,1)S(1)}, u32[]{:S(2)}, u32[]{:S(2)}) %collective-permute-start.1) | collective-permute-done | bytes 524320 | tf_op jit(solution)/shard_map/ppermute | solution.py:249
  37.9 1.0 add_convert_fusion.refs_2_
  38.9 4.0 %all-to-all-start.1 = ((bf16[8,64,512]{2,1,0:T(8,128)(2,1)}), bf16[8,64,512]{2,1,0:T(8,128)(2,1)S(1)}, u32[]{:S(2)}, u32[]{:S(2)}) async-start(bf16[8,64,512]{2,1,0:T(8,128)(2,1)} %bitcast.5), calls=%async_computation.1 | async-start | bytes 1048576 | tf_op jit(solution)/shard_map/all_to_all | solution.py:255
  42.9 2.9 %collective-permute-start.2 = (bf16[2,256,512]{2,1,0:T(8,128)(2,1)S(1)}, bf16[2,256,512]{2,1,0:T(8,128)(2,1)S(1)}, u32[]{:S(2)}, u32[]{:S(2)}) collective-permute-start(bf16[2,256,512]{2,1,0:T(8,128)(2,1)S(1)} %shard_map.87.refs_0_), channel_id=1, source_target_pairs={{0,192},{192,384},{384,576},{576,0},{1,193},{193,385},{385,577},{5... | collective-permute-start | bytes 1572872 | tf_op jit(solution)/shard_map/ppermute | solution.py:254
  45.8 3.6 %collective-permute-start.3 = (bf16[2,256,512]{2,1,0:T(8,128)(2,1)S(1)}, bf16[2,256,512]{2,1,0:T(8,128)(2,1)S(1)}, u32[]{:S(2)}, u32[]{:S(2)}) collective-permute-start(bf16[2,256,512]{2,1,0:T(8,128)(2,1)S(1)} %shard_map.87.refs_0_), channel_id=1, source_target_pairs={{0,576},{192,0},{384,192},{576,384},{1,577},{193,1},{385,193},{577... | collective-permute-start | bytes 1572872 | tf_op jit(solution)/shard_map/ppermute | solution.py:254
  49.4 9.4 %collective-permute-done.2.refs_2_.refs_1_ = bf16[2,256,512]{2,1,0:T(8,128)(2,1)S(1)} collective-permute-done((bf16[2,256,512]{2,1,0:T(8,128)(2,1)S(1)}, bf16[2,256,512]{2,1,0:T(8,128)(2,1)S(1)}, u32[]{:S(2)}, u32[]{:S(2)}) %collective-permute-start.2) | collective-permute-done | bytes 524320 | tf_op jit(solution)/shard_map/ppermute | solution.py:254
  58.8 1.6 %collective-permute-done.3.refs_3_ = bf16[2,256,512]{2,1,0:T(8,128)(2,1)S(1)} collective-permute-done((bf16[2,256,512]{2,1,0:T(8,128)(2,1)S(1)}, bf16[2,256,512]{2,1,0:T(8,128)(2,1)S(1)}, u32[]{:S(2)}, u32[]{:S(2)}) %collective-permute-start.3) | collective-permute-done | bytes 524320 | tf_op jit(solution)/shard_map/ppermute | solution.py:254
  60.5 0.4 all-to-all-done.1.refs_1_
  60.8 0.6 shard_map.88
  61.5 4.0 %collective-permute-start.4 = (bf16[32,512]{1,0:T(8,128)(2,1)S(1)}, bf16[32,512]{1,0:T(8,128)(2,1)S(1)}, u32[]{:S(2)}, u32[]{:S(2)}) collective-permute-start(bf16[32,512]{1,0:T(8,128)(2,1)S(1)} %get-tuple-element.21), channel_id=1, source_target_pairs={{0,2},{2,0},{1,3},{3,1},{4,6},{6,4},{5,7},{7,5},{8,10},{10,8},{9,1... | collective-permute-start | bytes 98312 | tf_op jit(solution)/shard_map/ppermute | solution.py:261
  65.5 4.2 %collective-permute-start.5 = (bf16[2,256,512]{2,1,0:T(8,128)(2,1)S(1)}, bf16[2,256,512]{2,1,0:T(8,128)(2,1)S(1)}, u32[]{:S(2)}, u32[]{:S(2)}) collective-permute-start(bf16[2,256,512]{2,1,0:T(8,128)(2,1)S(1)} %shard_map.87.refs_0_), channel_id=1, source_target_pairs={{0,384},{192,576},{384,0},{576,192},{1,385},{193,577},{385,1},{577... | collective-permute-start | bytes 1572872 | tf_op jit(solution)/shard_map/ppermute | solution.py:254
  69.6 0.0 collective-permute-done.4.refs_1_
  69.7 23.5 %all_to_all.25.refs_0_ = bf16[6,32,512]{2,1,0:T(8,128)(2,1)S(1)} all-to-all(bf16[6,32,512]{2,1,0:T(8,128)(2,1)S(1)} %shard_map.89), channel_id=1, replica_groups=mesh['x'=4,'yh'=2,'yl'=4,'z'=6,'zp'=2,'c'=2] {'z'}, dimensions={0} | all-to-all | bytes 393216 | tf_op jit(solution)/shard_map/all_to_all | solution.py:269
  93.3 0.0 collective-permute-done.5.refs_2_
  93.3 1.5 %shard_map.91 = (bf16[4,2,256,512]{3,2,1,0:T(8,128)(2,1)}, bf16[16,128]{1,0:T(8,128)(2,1)S(1)}) custom-call(bf16[2,256,512]{2,1,0:T(8,128)(2,1)S(1)} %shard_map.87.refs_0_, bf16[2,256,512]{2,1,0:T(8,128)(2,1)S(1)} %collective-permute-done.2.refs_2_.refs_1_, bf16[2,256,512]{2,1,0:T(8,128)(2,1)S(1)} %collective-permute-done.5.refs_2_, ...), custom_call_target="tpu_custom_call" | custom-call | bytes 8388608 | tf_op jit(solution)/shard_map/pallas_call | solution.py:203
  94.7 0.0 copy-start.1
  94.7 0.0 copy-start.2
  94.7 5.8 %collective-permute-start.7 = (bf16[4,2,256,512]{3,2,1,0:T(8,128)(2,1)}, bf16[4,2,256,512]{3,2,1,0:T(8,128)(2,1)}, u32[]{:S(2)}, u32[]{:S(2)}) collective-permute-start(bf16[4,2,256,512]{3,2,1,0:T(8,128)(2,1)} %get-tuple-element.23.refs_3_), channel_id=1, source_target_pairs={{0,1},{1,0},{2,3},{3,2},{4,5},{5,4},{6,7},{7,6},{8,9},{9,8},{10,11... | collective-permute-start | bytes 6291464 | tf_op jit(solution)/shard_map/ppermute | solution.py:280
  100.5 12.7 %all_to_all.26 = bf16[8,32,512]{2,1,0:T(8,128)(2,1)S(1)} all-to-all(bf16[8,32,512]{2,1,0:T(8,128)(2,1)S(1)} %shard_map.90.refs_4_), channel_id=1, replica_groups=mesh['x'=4,'yh'=2,'yl'=4,'z'=6,'zp'=2,'c'=2] {'yl','zp'}, dimensions={0} | all-to-all | bytes 524288 | tf_op jit(solution)/shard_map/all_to_all | solution.py:271
  113.2 3.6 %collective-permute-start.6 = (bf16[256,512]{1,0:T(8,128)(2,1)S(1)}, bf16[256,512]{1,0:T(8,128)(2,1)S(1)}, u32[]{:S(2)}, u32[]{:S(2)}) collective-permute-start(bf16[256,512]{1,0:T(8,128)(2,1)S(1)} %bitcast.8), channel_id=1, source_target_pairs={{0,1},{1,0},{2,3},{3,2},{4,5},{5,4},{6,7},{7,6},{8,9},{9,8},{10,11... | collective-permute-start | bytes 786440 | tf_op jit(solution)/shard_map/ppermute | solution.py:281
  116.8 0.8 shard_map.92.refs_1_
  117.6 0.3 collective-permute-done.6.refs_2_
  117.9 1.4 %shard_map.93.refs_5_.refs_4_ = f32[8,4,128]{2,1,0:T(4,128)} custom-call(s32[4]{0:T(128)S(1)} %pad_add_fusion.refs_0_, f32[2,128]{1,0:T(2,128)S(1)} %shard_map.92.refs_1_, bf16[256,512]{1,0:T(8,128)(2,1)S(1)} %collective-permute-done.6.refs_2_, bf16[512,512]{1,0:T(8,128)(2,1)S(1)} %copy-done, bf16[2,512]{1,0:T(2,128)(2,1)S(1)} %bitcast.13), custom_call_target="tpu_custom_call" | custom-call | flops 262144 | bytes 524288 | tf_op jit(solution)/shard_map/pallas_call | solution.py:203
  119.3 5.7 %all-to-all-start.4 = ((f32[8,4,128]{2,1,0:T(4,128)}), f32[8,4,128]{2,1,0:T(4,128)S(1)}, u32[]{:S(2)}, u32[]{:S(2)}) async-start(f32[8,4,128]{2,1,0:T(4,128)} %shard_map.93.refs_5_.refs_4_), calls=%async_computation.4 | async-start | bytes 32768 | tf_op jit(solution)/shard_map/all_to_all | solution.py:292
  125.0 1.5 %shard_map.95 = bf16[512,512]{1,0:T(8,128)(2,1)} custom-call(s32[4]{0:T(128)S(1)} %pad_add_fusion.refs_0_, bf16[256,512]{1,0:T(8,128)(2,1)S(1)} %bitcast.10, bf16[256,512]{1,0:T(8,128)(2,1)S(1)} %collective-permute-done.6.refs_2_, bf16[1,512]{1,0:T(2,128)(2,1)S(1)} %broadcast_in_dim.3.refs_3_, f32[8,4,128]{2,1,0:T(4,128)} %shard_map.93.refs_5_.refs_4_), custom_call_target="tpu_custom_call" | custom-call | flops 262144 | bytes 1048576 | tf_op jit(solution)/shard_map/pallas_call | solution.py:203
  126.5 0.0 collective-permute-done.7.refs_4_
  126.5 0.0 copy-done.1
  126.5 0.0 copy-done.2
  126.6 5.4 %shard_map.94 = (bf16[128,512]{1,0:T(8,128)(2,1)}, bf16[128,4096]{1,0:T(8,128)(2,1)}) custom-call(s32[4]{0:T(128)S(1)} %pad_add_fusion.refs_0_, bf16[128,4096]{1,0:T(8,128)(2,1)S(1)} %copy-done.1, bf16[128,512]{1,0:T(8,128)(2,1)S(1)} %copy-done.2, bf16[4,2,256,512]{3,2,1,0:T(8,128)(2,1)} %get-tuple-element.23.refs_3_, ...), custom_call_target="tpu_custom_call" | custom-call | flops 1073741824 | bytes 6291456 | tf_op jit(solution)/shard_map/pallas_call | solution.py:203
  132.0 2.0 %all-to-all-done.4 = f32[8,4,128]{2,1,0:T(4,128)S(1)} async-done(((f32[8,4,128]{2,1,0:T(4,128)}), f32[8,4,128]{2,1,0:T(4,128)S(1)}, u32[]{:S(2)}, u32[]{:S(2)}) %all-to-all-start.4) | async-done | bytes 16416 | tf_op jit(solution)/shard_map/all_to_all | solution.py:292
  134.0 0.6 copy.10
  (4 shorter events, 0.1 us)
Async XLA Ops:
  0.6 8.1 %copy-start.5 = (bf16[512]{0:T(512)(128)(2,1)S(1)}, bf16[512]{0:T(512)(128)(2,1)}, u32[]{:S(2)}) copy-start(bf16[512]{0:T(512)(128)(2,1)} %param.6) | copy-start | bytes 3076
  0.6 8.1 %copy-start.3 = (bf16[512,2]{0,1:T(2,128)(2,1)S(1)}, bf16[512,2]{0,1:T(2,128)(2,1)}, u32[]{:S(2)}) copy-start(bf16[512,2]{0,1:T(2,128)(2,1)} %param.8) | copy-start | bytes 6148
  0.7 8.1 %copy-start = (bf16[512,512]{1,0:T(8,128)(2,1)S(1)}, bf16[512,512]{1,0:T(8,128)(2,1)}, u32[]{:S(2)}) copy-start(bf16[512,512]{1,0:T(8,128)(2,1)} %refs_3_.1) | copy-start | bytes 1572868
  3.8 5.0 %copy-start.4 = (f32[8,1]{1,0:T(8,128)S(1)}, f32[8,1]{1,0:T(8,128)}, u32[]{:S(2)}) copy-start(f32[8,1]{1,0:T(8,128)} %get-tuple-element.17.refs_4_) | copy-start | bytes 100
  3.8 17.4 %all-to-all-start = ((bf16[4,128,1536]{2,1,0:T(8,128)(2,1)}), bf16[4,128,1536]{2,1,0:T(8,128)(2,1)S(1)}, u32[]{:S(2)}, u32[]{:S(2)}) async-start(bf16[4,128,1536]{2,1,0:T(8,128)(2,1)} %get-tuple-element.16), calls=%async_computation | async-start | bytes 3145728 | tf_op jit(solution)/shard_map/all_to_all | solution.py:234
  9.5 11.3 %collective-permute-start = (bf16[256,512]{1,0:T(8,128)(2,1)S(1)}, bf16[256,512]{1,0:T(8,128)(2,1)S(1)}, u32[]{:S(2)}, u32[]{:S(2)}) collective-permute-start(bf16[256,512]{1,0:T(8,128)(2,1)S(1)} %shard_map.85.refs_0_), channel_id=1, source_target_pairs={{0,96},{96,0},{1,97},{97,1},{2,98},{98,2},{3,99},{99,3},{4,100},{1... | collective-permute-start | bytes 786440 | tf_op jit(solution)/shard_map/ppermute | solution.py:239
  22.5 15.4 %collective-permute-start.1 = (bf16[2,256,512]{2,1,0:T(8,128)(2,1)S(1)}, bf16[2,256,512]{2,1,0:T(8,128)(2,1)S(1)}, u32[]{:S(2)}, u32[]{:S(2)}) collective-permute-start(bf16[2,256,512]{2,1,0:T(8,128)(2,1)S(1)} %get-tuple-element.19), channel_id=1, source_target_pairs={{0,1},{1,0},{2,3},{3,2},{4,5},{5,4},{6,7},{7,6},{8,9},{9,8},{10,11... | collective-permute-start | bytes 1572872 | tf_op jit(solution)/shard_map/ppermute | solution.py:249
  38.9 22.0 %all-to-all-start.1 = ((bf16[8,64,512]{2,1,0:T(8,128)(2,1)}), bf16[8,64,512]{2,1,0:T(8,128)(2,1)S(1)}, u32[]{:S(2)}, u32[]{:S(2)}) async-start(bf16[8,64,512]{2,1,0:T(8,128)(2,1)} %bitcast.5), calls=%async_computation.1 | async-start | bytes 1048576 | tf_op jit(solution)/shard_map/all_to_all | solution.py:255
  42.9 15.9 %collective-permute-start.2 = (bf16[2,256,512]{2,1,0:T(8,128)(2,1)S(1)}, bf16[2,256,512]{2,1,0:T(8,128)(2,1)S(1)}, u32[]{:S(2)}, u32[]{:S(2)}) collective-permute-start(bf16[2,256,512]{2,1,0:T(8,128)(2,1)S(1)} %shard_map.87.refs_0_), channel_id=1, source_target_pairs={{0,192},{192,384},{384,576},{576,0},{1,193},{193,385},{385,577},{5... | collective-permute-start | bytes 1572872 | tf_op jit(solution)/shard_map/ppermute | solution.py:254
  45.8 14.7 %collective-permute-start.3 = (bf16[2,256,512]{2,1,0:T(8,128)(2,1)S(1)}, bf16[2,256,512]{2,1,0:T(8,128)(2,1)S(1)}, u32[]{:S(2)}, u32[]{:S(2)}) collective-permute-start(bf16[2,256,512]{2,1,0:T(8,128)(2,1)S(1)} %shard_map.87.refs_0_), channel_id=1, source_target_pairs={{0,576},{192,0},{384,192},{576,384},{1,577},{193,1},{385,193},{577... | collective-permute-start | bytes 1572872 | tf_op jit(solution)/shard_map/ppermute | solution.py:254
  61.5 8.2 %collective-permute-start.4 = (bf16[32,512]{1,0:T(8,128)(2,1)S(1)}, bf16[32,512]{1,0:T(8,128)(2,1)S(1)}, u32[]{:S(2)}, u32[]{:S(2)}) collective-permute-start(bf16[32,512]{1,0:T(8,128)(2,1)S(1)} %get-tuple-element.21), channel_id=1, source_target_pairs={{0,2},{2,0},{1,3},{3,1},{4,6},{6,4},{5,7},{7,5},{8,10},{10,8},{9,1... | collective-permute-start | bytes 98312 | tf_op jit(solution)/shard_map/ppermute | solution.py:261
  65.5 27.8 %collective-permute-start.5 = (bf16[2,256,512]{2,1,0:T(8,128)(2,1)S(1)}, bf16[2,256,512]{2,1,0:T(8,128)(2,1)S(1)}, u32[]{:S(2)}, u32[]{:S(2)}) collective-permute-start(bf16[2,256,512]{2,1,0:T(8,128)(2,1)S(1)} %shard_map.87.refs_0_), channel_id=1, source_target_pairs={{0,384},{192,576},{384,0},{576,192},{1,385},{193,577},{385,1},{577... | collective-permute-start | bytes 1572872 | tf_op jit(solution)/shard_map/ppermute | solution.py:254
  94.7 31.8 %copy-start.1 = (bf16[128,4096]{1,0:T(8,128)(2,1)S(1)}, bf16[128,4096]{1,0:T(8,128)(2,1)}, u32[]{:S(2)}) copy-start(bf16[128,4096]{1,0:T(8,128)(2,1)} %refs_1_.3) | copy-start | bytes 3145732
  94.7 31.8 %copy-start.2 = (bf16[128,512]{1,0:T(8,128)(2,1)S(1)}, bf16[128,512]{1,0:T(8,128)(2,1)}, u32[]{:S(2)}) copy-start(bf16[128,512]{1,0:T(8,128)(2,1)} %refs_2_.3) | copy-start | bytes 393220
  94.7 31.8 %collective-permute-start.7 = (bf16[4,2,256,512]{3,2,1,0:T(8,128)(2,1)}, bf16[4,2,256,512]{3,2,1,0:T(8,128)(2,1)}, u32[]{:S(2)}, u32[]{:S(2)}) collective-permute-start(bf16[4,2,256,512]{3,2,1,0:T(8,128)(2,1)} %get-tuple-element.23.refs_3_), channel_id=1, source_target_pairs={{0,1},{1,0},{2,3},{3,2},{4,5},{5,4},{6,7},{7,6},{8,9},{9,8},{10,11... | collective-permute-start | bytes 6291464 | tf_op jit(solution)/shard_map/ppermute | solution.py:280
  113.2 4.7 %collective-permute-start.6 = (bf16[256,512]{1,0:T(8,128)(2,1)S(1)}, bf16[256,512]{1,0:T(8,128)(2,1)S(1)}, u32[]{:S(2)}, u32[]{:S(2)}) collective-permute-start(bf16[256,512]{1,0:T(8,128)(2,1)S(1)} %bitcast.8), channel_id=1, source_target_pairs={{0,1},{1,0},{2,3},{3,2},{4,5},{5,4},{6,7},{7,6},{8,9},{9,8},{10,11... | collective-permute-start | bytes 786440 | tf_op jit(solution)/shard_map/ppermute | solution.py:281
  119.3 14.7 %all-to-all-start.4 = ((f32[8,4,128]{2,1,0:T(4,128)}), f32[8,4,128]{2,1,0:T(4,128)S(1)}, u32[]{:S(2)}, u32[]{:S(2)}) async-start(f32[8,4,128]{2,1,0:T(4,128)} %shard_map.93.refs_5_.refs_4_), calls=%async_computation.4 | async-start | bytes 32768 | tf_op jit(solution)/shard_map/all_to_all | solution.py:292

commit v6 on v5

--- a/solution.py
+++ b/solution.py
@@ -160,28 +160,11 @@
         grad_ref[:, columns] = (inv * (value - unit * mean)).astype(BF16)
 
 
-def halve_kernel(place_ref, terms_ref, keep_ref, send_ref):
-    rows = keep_ref.shape[0]
-    mine = place_ref[3]
-    for ref, which in ((send_ref, 1 - mine), (keep_ref, mine)):
-        at = pl.ds(pl.multiple_of(which * rows, rows), rows)
-        total = terms_ref[0, at, :].astype(F32)
-        for i in range(1, terms_ref.shape[0]):
-            total = total + terms_ref[i, at, :].astype(F32)
-        ref[...] = total.astype(BF16)
-
-
-def add_kernel(keep_ref, came_ref, copies_ref):
-    total = (keep_ref[...].astype(F32) + came_ref[...].astype(F32)).astype(BF16)
-    for i in range(copies_ref.shape[0]):
-        copies_ref[i] = total
-
-
 def total_kernel(scale, terms_ref, copies_ref):
     total = terms_ref[0].astype(F32)
     for i in range(1, terms_ref.shape[0]):
         total = total + terms_ref[i].astype(F32)
-    total = (total * scale).astype(BF16)
+    total = (total if scale == 1 else total * scale).astype(BF16)
     for i in range(copies_ref.shape[0]):
         copies_ref[i] = total
 
@@ -208,13 +191,13 @@
 
 
 def body(hidden_in, norm_gain, key_codes, key_scales, key_cotangent):
-    nx, nh, nl, nz, np, nc = (lax.axis_size(a) for a in ("x", "yh", "yl", "z", "zp", "c"))
+    nx, nh, nl, nz, nn, nc = (lax.axis_size(a) for a in ("x", "yh", "yl", "z", "zn", "c"))
     tok, width = hidden_in.shape
     rows, cols = key_codes.shape
-    total_tokens = tok * nx * nh * nl * nz * np * nc
+    total_tokens = tok * nx * nh * nl * nz * nn * nc
     half = rows // nc
     part = width // nx
-    place = jnp.stack([lax.axis_index(a) for a in ("c", "x", "yh", "zp")]).astype(jnp.int32)
+    place = jnp.stack([lax.axis_index(a) for a in ("c", "x", "yh")]).astype(jnp.int32)
     scales, gain = key_scales.T, norm_gain[None]
 
     sent, mark = pl.pallas_call(
@@ -250,25 +233,34 @@
     pair = call(stack_kernel, shape((nh, half, cols), BF16), [VMEM] * 2, 0, 4 * nh * half * cols, [product])(mine, mate)
 
     quarter = half // nl
-    eighth = quarter // np
+    share = quarter // nn
     own = [pair] + [lax.ppermute(pair, "x", [(i, (i + s) % nx) for i in range(nx)]) for s in range(1, nx)]
     terms = lax.all_to_all(product.reshape(nh * nl, quarter, cols), ("yh", "yl"), 0, 0)
-    keep, send = call(
-        halve_kernel, [shape((eighth, cols), BF16)] * 2, [SMEM, VMEM], nh * nl * quarter * cols, 2 * half * cols, [own[1], own[-1]]
-    )(place, terms)
-    copies = call(
-        add_kernel, shape((nz, eighth, cols), BF16), [VMEM, VMEM], eighth * cols, 2 * nz * eighth * cols
-    )(keep, lax.ppermute(send, "zp", SWAP))
-    scale = float(total_tokens) ** -0.5
+    terms = call(
+        functools.partial(total_kernel, 1.0),
+        shape((1, quarter, cols), BF16),
+        [VMEM],
+        nh * nl * quarter * cols,
+        2 * half * cols,
+    )(terms)
+    terms = lax.all_to_all(terms.reshape(nn, share, cols), "zn", 0, 0)
+    terms = call(
+        functools.partial(total_kernel, 1.0),
+        shape((nz, share, cols), BF16),
+        [VMEM],
+        nn * share * cols,
+        2 * (nn + nz) * share * cols,
+        [own[1], own[-1]],
+    )(terms)
     copies = call(
         functools.partial(total_kernel, float(total_tokens) ** -0.5),
-        shape((nl * np, eighth, cols), BF16),
+        shape((nl * nn, share, cols), BF16),
         [VMEM],
-        nz * eighth * cols,
-        2 * (nz + nl * np) * eighth * cols,
-    )(lax.all_to_all(copies, "z", 0, 0))
-
-    whole = lax.all_to_all(copies, ("yl", "zp"), 0, 0).reshape(half, cols)
+        nz * share * cols,
+        2 * (nz + nl * nn) * share * cols,
+    )(lax.all_to_all(terms, "z", 0, 0))
+
+    whole = lax.all_to_all(copies, ("yl", "zn"), 0, 0).reshape(half, cols)
     own, mark = call(
         marked_stack_kernel,
         [shape((nx, nh, half, cols), BF16), shape((16, LANES), BF16)],
@@ -306,8 +298,8 @@
 
 
 def solution(mesh):
-    axes = ("x", "yh", "yl", "z", "zp", "c")
-    fine = Mesh(mesh.devices.reshape(4, 2, 4, 6, 2, 2), axes)
+    axes = ("x", "yh", "yl", "z", "zn", "c")
+    fine = Mesh(mesh.devices.reshape(4, 2, 4, 3, 4, 2), axes)
     tokens = P(axes, None)
     group = ("x", "yh")
     in_specs = (tokens, P(group), P(group, None), P(group, None), tokens)

time: 135 us -> 140 us (1.037)
  starting transfers between devices: 59.9 us -> 62.8 us
    ppermute x3, waiting for transfers between devices: 11 us -> 0.01 us  [body(): lax.ppermute(pair, 'x', [(i, (i + s) % nx) for i in range(nx)])]
    all_to_all x1, waiting for transfers between devices: 0.37 us -> 8.25 us  [body(): lax.all_to_all(product.reshape(nh * nl, quarter, cols), ('yh', 'yl'), 0, 0)]
    all_to_all x0 -> x1, starting transfers between devices: none -> 6.98 us  [body(): terms = lax.all_to_all(terms.reshape(nn, share, cols), 'zn', 0, 0)]
    all_to_all x0 -> x1, waiting for transfers between devices: none -> 4.59 us  [body(): terms = lax.all_to_all(terms.reshape(nn, share, cols), 'zn', 0, 0)]
    ppermute x1 -> x0, starting transfers between devices: 4 us -> none  [body(): lax.ppermute(send, 'zp', SWAP)]
  transfers between devices with their start and end apart: 11 -> 11, of which waited for: 8 -> 7; matrix products, arithmetic and copies ran while one was open for 0% -> 0% of each run, Pallas kernels for 7% -> 8%
where the time goes in v6:
time: 140 us; the launch traced here: 139 us
  starting transfers between devices  62.8 us (45%)
  blocking collectives  36 us (26%)
  waiting for transfers between devices  21 us (15%)
  Pallas kernels  16.5 us (12%)
    all_to_all x1, blocking collectives, body(): whole = lax.all_to_all(copies, ('yl', 'zn'), 0, 0).reshape(half, cols)  18.3 us
    all_to_all x1, blocking collectives, body(): lax.all_to_all(terms, 'z', 0, 0)  17.7 us
    ppermute x1, starting transfers between devices, body(): product = (keep + lax.ppermute(send, 'c', SWAP).astype(F32)).astype(BF16)  13.8 us
    pallas_call x11, Pallas kernels, call(): return lambda *operands: made(*operands, *after)  13.4 us
    ppermute x3, starting transfers between devices, body(): lax.ppermute(pair, 'x', [(i, (i + s) % nx) for i in range(nx)])  9.65 us
    all_to_all x1, waiting for transfers between devices, body(): lax.all_to_all(product.reshape(nh * nl, quarter, cols), ('yh', 'yl'), 0, 0)  8.25 us
    ppermute x1, starting transfers between devices, body(): mate = lax.ppermute(mine, 'yh', SWAP)  7.45 us
    all_to_all x1, starting transfers between devices, body(): terms = lax.all_to_all(terms.reshape(nn, share, cols), 'zn', 0, 0)  6.98 us
  transfers between devices with their start and end apart: 11, of which 7 were waited for; matrix products, arithmetic and copies ran while one was open for 0% of the time, Pallas kernels for 8%

profile of v6, /device:TPU:1, one launch (start us, length us, event | category | flops | bytes accessed | tf_op | source)
XLA Modules:
  0.0 138.9 jit_solution(2525906683371896257)
XLA Ops:
  0.6 0.0 copy-start.5
  0.6 0.0 copy-start.3
  0.7 0.0 copy-start
  0.7 3.2 %shard_map.84 = (bf16[4,128,1536]{2,1,0:T(8,128)(2,1)}, f32[8,1]{1,0:T(8,128)}) custom-call(bf16[128,4096]{1,0:T(8,128)(2,1)} %refs_1_.3, bf16[128,512]{1,0:T(8,128)(2,1)} %refs_2_.3), custom_call_target="tpu_custom_call" | custom-call | flops 2097152 | bytes 2097152 | tf_op jit(solution)/shard_map/pallas_call | solution.py:203
  3.8 0.0 copy-start.4
  3.8 4.9 %all-to-all-start = ((bf16[4,128,1536]{2,1,0:T(8,128)(2,1)}), bf16[4,128,1536]{2,1,0:T(8,128)(2,1)S(1)}, u32[]{:S(2)}, u32[]{:S(2)}) async-start(bf16[4,128,1536]{2,1,0:T(8,128)(2,1)} %get-tuple-element.14), calls=%async_computation | async-start | bytes 3145728 | tf_op jit(solution)/shard_map/all_to_all | solution.py:217
  8.7 0.0 copy-done.5
  8.7 0.1 pad_add_fusion.refs_0_
  8.8 0.0 copy-done.3
  8.8 0.0 copy-done
  8.8 0.0 copy-done.4
  8.8 0.7 shard_map.85.refs_0_
  9.5 7.5 %collective-permute-start = (bf16[256,512]{1,0:T(8,128)(2,1)S(1)}, bf16[256,512]{1,0:T(8,128)(2,1)S(1)}, u32[]{:S(2)}, u32[]{:S(2)}) collective-permute-start(bf16[256,512]{1,0:T(8,128)(2,1)S(1)} %shard_map.85.refs_0_), channel_id=1, source_target_pairs={{0,96},{96,0},{1,97},{97,1},{2,98},{98,2},{3,99},{99,3},{4,100},{1... | collective-permute-start | bytes 786440 | tf_op jit(solution)/shard_map/ppermute | solution.py:222
  16.9 3.8 %collective-permute-done.refs_2_.refs_1_ = bf16[256,512]{1,0:T(8,128)(2,1)S(1)} collective-permute-done((bf16[256,512]{1,0:T(8,128)(2,1)S(1)}, bf16[256,512]{1,0:T(8,128)(2,1)S(1)}, u32[]{:S(2)}, u32[]{:S(2)}) %collective-permute-start) | collective-permute-done | bytes 262176 | tf_op jit(solution)/shard_map/ppermute | solution.py:222
  20.8 0.5 all-to-all-done.refs_1_
  21.2 1.3 shard_map.86
  22.5 13.8 %collective-permute-start.1 = (bf16[2,256,512]{2,1,0:T(8,128)(2,1)S(1)}, bf16[2,256,512]{2,1,0:T(8,128)(2,1)S(1)}, u32[]{:S(2)}, u32[]{:S(2)}) collective-permute-start(bf16[2,256,512]{2,1,0:T(8,128)(2,1)S(1)} %get-tuple-element.17), channel_id=1, source_target_pairs={{0,1},{1,0},{2,3},{3,2},{4,5},{5,4},{6,7},{7,6},{8,9},{9,8},{10,11... | collective-permute-start | bytes 1572872 | tf_op jit(solution)/shard_map/ppermute | solution.py:232
  36.4 1.5 %collective-permute-done.1 = bf16[2,256,512]{2,1,0:T(8,128)(2,1)S(1)} collective-permute-done((bf16[2,256,512]{2,1,0:T(8,128)(2,1)S(1)}, bf16[2,256,512]{2,1,0:T(8,128)(2,1)S(1)}, u32[]{:S(2)}, u32[]{:S(2)}) %collective-permute-start.1) | collective-permute-done | bytes 524320 | tf_op jit(solution)/shard_map/ppermute | solution.py:232
  37.9 1.0 add_convert_fusion.refs_2_
  38.9 4.0 %all-to-all-start.1 = ((bf16[8,64,512]{2,1,0:T(8,128)(2,1)}), bf16[8,64,512]{2,1,0:T(8,128)(2,1)S(1)}, u32[]{:S(2)}, u32[]{:S(2)}) async-start(bf16[8,64,512]{2,1,0:T(8,128)(2,1)} %bitcast.4), calls=%async_computation.1 | async-start | bytes 1048576 | tf_op jit(solution)/shard_map/all_to_all | solution.py:238
  42.9 2.9 %collective-permute-start.2 = (bf16[2,256,512]{2,1,0:T(8,128)(2,1)S(1)}, bf16[2,256,512]{2,1,0:T(8,128)(2,1)S(1)}, u32[]{:S(2)}, u32[]{:S(2)}) collective-permute-start(bf16[2,256,512]{2,1,0:T(8,128)(2,1)S(1)} %shard_map.88.refs_0_), channel_id=1, source_target_pairs={{0,192},{192,384},{384,576},{576,0},{1,193},{193,385},{385,577},{5... | collective-permute-start | bytes 1572872 | tf_op jit(solution)/shard_map/ppermute | solution.py:237
  45.8 3.6 %collective-permute-start.3 = (bf16[2,256,512]{2,1,0:T(8,128)(2,1)S(1)}, bf16[2,256,512]{2,1,0:T(8,128)(2,1)S(1)}, u32[]{:S(2)}, u32[]{:S(2)}) collective-permute-start(bf16[2,256,512]{2,1,0:T(8,128)(2,1)S(1)} %shard_map.88.refs_0_), channel_id=1, source_target_pairs={{0,576},{192,0},{384,192},{576,384},{1,577},{193,1},{385,193},{577... | collective-permute-start | bytes 1572872 | tf_op jit(solution)/shard_map/ppermute | solution.py:237
  49.4 3.2 %collective-permute-start.4 = (bf16[2,256,512]{2,1,0:T(8,128)(2,1)S(1)}, bf16[2,256,512]{2,1,0:T(8,128)(2,1)S(1)}, u32[]{:S(2)}, u32[]{:S(2)}) collective-permute-start(bf16[2,256,512]{2,1,0:T(8,128)(2,1)S(1)} %shard_map.88.refs_0_), channel_id=1, source_target_pairs={{0,384},{192,576},{384,0},{576,192},{1,385},{193,577},{385,1},{577... | collective-permute-start | bytes 1572872 | tf_op jit(solution)/shard_map/ppermute | solution.py:237
  52.6 8.2 %all-to-all-done.1.refs_0_ = bf16[8,64,512]{2,1,0:T(8,128)(2,1)S(1)} async-done(((bf16[8,64,512]{2,1,0:T(8,128)(2,1)}), bf16[8,64,512]{2,1,0:T(8,128)(2,1)S(1)}, u32[]{:S(2)}, u32[]{:S(2)}) %all-to-all-start.1) | async-done | bytes 524320 | tf_op jit(solution)/shard_map/all_to_all | solution.py:238
  60.8 0.7 shard_map.87
  61.5 7.0 %all-to-all-start.2 = ((bf16[4,16,512]{2,1,0:T(8,128)(2,1)}), bf16[4,16,512]{2,1,0:T(8,128)(2,1)S(1)}, u32[]{:S(2)}, u32[]{:S(2)}) async-start(bf16[4,16,512]{2,1,0:T(8,128)(2,1)} %bitcast.5), calls=%async_computation.2 | async-start | bytes 131072 | tf_op jit(solution)/shard_map/all_to_all | solution.py:246
  68.5 0.0 collective-permute-done.2.refs_1_
  68.5 0.0 collective-permute-done.3.refs_2_.refs_3_
  68.5 4.6 %all-to-all-done.2.refs_0_ = bf16[4,16,512]{2,1,0:T(8,128)(2,1)S(1)} async-done(((bf16[4,16,512]{2,1,0:T(8,128)(2,1)}), bf16[4,16,512]{2,1,0:T(8,128)(2,1)S(1)}, u32[]{:S(2)}, u32[]{:S(2)}) %all-to-all-start.2) | async-done | bytes 65568 | tf_op jit(solution)/shard_map/all_to_all | solution.py:246
  73.1 17.7 %all_to_all.30.refs_0_ = bf16[3,16,512]{2,1,0:T(8,128)(2,1)S(1)} all-to-all(bf16[3,16,512]{2,1,0:T(8,128)(2,1)S(1)} %shard_map.89), channel_id=1, replica_groups=mesh['x'=4,'yh'=2,'yl'=4,'z'=3,'zn'=4,'c'=2] {'z'}, dimensions={0} | all-to-all | bytes 98304 | tf_op jit(solution)/shard_map/all_to_all | solution.py:261
  90.9 0.0 collective-permute-done.4.refs_2_
  90.9 1.5 %shard_map.91 = (bf16[4,2,256,512]{3,2,1,0:T(8,128)(2,1)}, bf16[16,128]{1,0:T(8,128)(2,1)S(1)}) custom-call(bf16[2,256,512]{2,1,0:T(8,128)(2,1)S(1)} %shard_map.88.refs_0_, bf16[2,256,512]{2,1,0:T(8,128)(2,1)S(1)} %collective-permute-done.2.refs_1_, bf16[2,256,512]{2,1,0:T(8,128)(2,1)S(1)} %collective-permute-done.4.refs_2_, ...), custom_call_target="tpu_custom_call" | custom-call | bytes 8388608 | tf_op jit(solution)/shard_map/pallas_call | solution.py:186
  92.4 0.0 copy-start.1
  92.4 0.0 copy-start.2
  92.4 5.6 %collective-permute-start.6 = (bf16[4,2,256,512]{3,2,1,0:T(8,128)(2,1)}, bf16[4,2,256,512]{3,2,1,0:T(8,128)(2,1)}, u32[]{:S(2)}, u32[]{:S(2)}) collective-permute-start(bf16[4,2,256,512]{3,2,1,0:T(8,128)(2,1)} %get-tuple-element.19.refs_3_), channel_id=1, source_target_pairs={{0,1},{1,0},{2,3},{3,2},{4,5},{5,4},{6,7},{7,6},{8,9},{9,8},{10,11... | collective-permute-start | bytes 6291464 | tf_op jit(solution)/shard_map/ppermute | solution.py:272
  98.0 18.3 %all_to_all.31 = bf16[16,16,512]{2,1,0:T(8,128)(2,1)S(1)} all-to-all(bf16[16,16,512]{2,1,0:T(8,128)(2,1)S(1)} %shard_map.90.refs_4_), channel_id=1, replica_groups=mesh['x'=4,'yh'=2,'yl'=4,'z'=3,'zn'=4,'c'=2] {'yl','zn'}, dimensions={0} | all-to-all | bytes 524288 | tf_op jit(solution)/shard_map/all_to_all | solution.py:263
  116.3 3.7 %collective-permute-start.5 = (bf16[256,512]{1,0:T(8,128)(2,1)S(1)}, bf16[256,512]{1,0:T(8,128)(2,1)S(1)}, u32[]{:S(2)}, u32[]{:S(2)}) collective-permute-start(bf16[256,512]{1,0:T(8,128)(2,1)S(1)} %bitcast.8), channel_id=1, source_target_pairs={{0,1},{1,0},{2,3},{3,2},{4,5},{5,4},{6,7},{7,6},{8,9},{9,8},{10,11... | collective-permute-start | bytes 786440 | tf_op jit(solution)/shard_map/ppermute | solution.py:273
  119.9 0.8 shard_map.92.refs_1_
  120.8 0.3 collective-permute-done.5.refs_2_
  121.1 1.4 %shard_map.93.refs_5_.refs_4_ = f32[8,4,128]{2,1,0:T(4,128)} custom-call(s32[3]{0:T(128)S(1)} %pad_add_fusion.refs_0_, f32[2,128]{1,0:T(2,128)S(1)} %shard_map.92.refs_1_, bf16[256,512]{1,0:T(8,128)(2,1)S(1)} %collective-permute-done.5.refs_2_, bf16[512,512]{1,0:T(8,128)(2,1)S(1)} %copy-done, bf16[2,512]{1,0:T(2,128)(2,1)S(1)} %bitcast.13), custom_call_target="tpu_custom_call" | custom-call | flops 262144 | bytes 524288 | tf_op jit(solution)/shard_map/pallas_call | solution.py:186
  122.5 6.8 %all-to-all-start.5 = ((f32[8,4,128]{2,1,0:T(4,128)}), f32[8,4,128]{2,1,0:T(4,128)S(1)}, u32[]{:S(2)}, u32[]{:S(2)}) async-start(f32[8,4,128]{2,1,0:T(4,128)} %shard_map.93.refs_5_.refs_4_), calls=%async_computation.5 | async-start | bytes 32768 | tf_op jit(solution)/shard_map/all_to_all | solution.py:284
  129.3 1.5 %shard_map.95 = bf16[512,512]{1,0:T(8,128)(2,1)} custom-call(s32[3]{0:T(128)S(1)} %pad_add_fusion.refs_0_, bf16[256,512]{1,0:T(8,128)(2,1)S(1)} %bitcast.10, bf16[256,512]{1,0:T(8,128)(2,1)S(1)} %collective-permute-done.5.refs_2_, bf16[1,512]{1,0:T(2,128)(2,1)S(1)} %broadcast_in_dim.3.refs_3_, f32[8,4,128]{2,1,0:T(4,128)} %shard_map.93.refs_5_.refs_4_), custom_call_target="tpu_custom_call" | custom-call | flops 262144 | bytes 1048576 | tf_op jit(solution)/shard_map/pallas_call | solution.py:186
  130.8 0.0 collective-permute-done.6.refs_4_
  130.8 0.0 copy-done.1
  130.8 0.0 copy-done.2
  130.8 5.4 %shard_map.94 = (bf16[128,512]{1,0:T(8,128)(2,1)}, bf16[128,4096]{1,0:T(8,128)(2,1)}) custom-call(s32[3]{0:T(128)S(1)} %pad_add_fusion.refs_0_, bf16[128,4096]{1,0:T(8,128)(2,1)S(1)} %copy-done.1, bf16[128,512]{1,0:T(8,128)(2,1)S(1)} %copy-done.2, bf16[4,2,256,512]{3,2,1,0:T(8,128)(2,1)} %get-tuple-element.19.refs_3_, ...), custom_call_target="tpu_custom_call" | custom-call | flops 1073741824 | bytes 6291456 | tf_op jit(solution)/shard_map/pallas_call | solution.py:186
  136.2 2.0 %all-to-all-done.5 = f32[8,4,128]{2,1,0:T(4,128)S(1)} async-done(((f32[8,4,128]{2,1,0:T(4,128)}), f32[8,4,128]{2,1,0:T(4,128)S(1)}, u32[]{:S(2)}, u32[]{:S(2)}) %all-to-all-start.5) | async-done | bytes 16416 | tf_op jit(solution)/shard_map/all_to_all | solution.py:284
  138.3 0.6 copy.10
  (4 shorter events, 0.1 us)
Async XLA Ops:
  0.6 8.1 %copy-start.5 = (bf16[512]{0:T(512)(128)(2,1)S(1)}, bf16[512]{0:T(512)(128)(2,1)}, u32[]{:S(2)}) copy-start(bf16[512]{0:T(512)(128)(2,1)} %param.6) | copy-start | bytes 3076
  0.6 8.1 %copy-start.3 = (bf16[512,2]{0,1:T(2,128)(2,1)S(1)}, bf16[512,2]{0,1:T(2,128)(2,1)}, u32[]{:S(2)}) copy-start(bf16[512,2]{0,1:T(2,128)(2,1)} %param.8) | copy-start | bytes 6148
  0.7 8.1 %copy-start = (bf16[512,512]{1,0:T(8,128)(2,1)S(1)}, bf16[512,512]{1,0:T(8,128)(2,1)}, u32[]{:S(2)}) copy-start(bf16[512,512]{1,0:T(8,128)(2,1)} %refs_3_.1) | copy-start | bytes 1572868
  3.8 5.0 %copy-start.4 = (f32[8,1]{1,0:T(8,128)S(1)}, f32[8,1]{1,0:T(8,128)}, u32[]{:S(2)}) copy-start(f32[8,1]{1,0:T(8,128)} %get-tuple-element.15.refs_4_) | copy-start | bytes 100
  3.8 17.4 %all-to-all-start = ((bf16[4,128,1536]{2,1,0:T(8,128)(2,1)}), bf16[4,128,1536]{2,1,0:T(8,128)(2,1)S(1)}, u32[]{:S(2)}, u32[]{:S(2)}) async-start(bf16[4,128,1536]{2,1,0:T(8,128)(2,1)} %get-tuple-element.14), calls=%async_computation | async-start | bytes 3145728 | tf_op jit(solution)/shard_map/all_to_all | solution.py:217
  9.5 11.3 %collective-permute-start = (bf16[256,512]{1,0:T(8,128)(2,1)S(1)}, bf16[256,512]{1,0:T(8,128)(2,1)S(1)}, u32[]{:S(2)}, u32[]{:S(2)}) collective-permute-start(bf16[256,512]{1,0:T(8,128)(2,1)S(1)} %shard_map.85.refs_0_), channel_id=1, source_target_pairs={{0,96},{96,0},{1,97},{97,1},{2,98},{98,2},{3,99},{99,3},{4,100},{1... | collective-permute-start | bytes 786440 | tf_op jit(solution)/shard_map/ppermute | solution.py:222
  22.5 15.4 %collective-permute-start.1 = (bf16[2,256,512]{2,1,0:T(8,128)(2,1)S(1)}, bf16[2,256,512]{2,1,0:T(8,128)(2,1)S(1)}, u32[]{:S(2)}, u32[]{:S(2)}) collective-permute-start(bf16[2,256,512]{2,1,0:T(8,128)(2,1)S(1)} %get-tuple-element.17), channel_id=1, source_target_pairs={{0,1},{1,0},{2,3},{3,2},{4,5},{5,4},{6,7},{7,6},{8,9},{9,8},{10,11... | collective-permute-start | bytes 1572872 | tf_op jit(solution)/shard_map/ppermute | solution.py:232
  38.9 22.0 %all-to-all-start.1 = ((bf16[8,64,512]{2,1,0:T(8,128)(2,1)}), bf16[8,64,512]{2,1,0:T(8,128)(2,1)S(1)}, u32[]{:S(2)}, u32[]{:S(2)}) async-start(bf16[8,64,512]{2,1,0:T(8,128)(2,1)} %bitcast.4), calls=%async_computation.1 | async-start | bytes 1048576 | tf_op jit(solution)/shard_map/all_to_all | solution.py:238
  42.9 25.6 %collective-permute-start.2 = (bf16[2,256,512]{2,1,0:T(8,128)(2,1)S(1)}, bf16[2,256,512]{2,1,0:T(8,128)(2,1)S(1)}, u32[]{:S(2)}, u32[]{:S(2)}) collective-permute-start(bf16[2,256,512]{2,1,0:T(8,128)(2,1)S(1)} %shard_map.88.refs_0_), channel_id=1, source_target_pairs={{0,192},{192,384},{384,576},{576,0},{1,193},{193,385},{385,577},{5... | collective-permute-start | bytes 1572872 | tf_op jit(solution)/shard_map/ppermute | solution.py:237
  45.8 22.7 %collective-permute-start.3 = (bf16[2,256,512]{2,1,0:T(8,128)(2,1)S(1)}, bf16[2,256,512]{2,1,0:T(8,128)(2,1)S(1)}, u32[]{:S(2)}, u32[]{:S(2)}) collective-permute-start(bf16[2,256,512]{2,1,0:T(8,128)(2,1)S(1)} %shard_map.88.refs_0_), channel_id=1, source_target_pairs={{0,576},{192,0},{384,192},{576,384},{1,577},{193,1},{385,193},{577... | collective-permute-start | bytes 1572872 | tf_op jit(solution)/shard_map/ppermute | solution.py:237
  49.4 41.5 %collective-permute-start.4 = (bf16[2,256,512]{2,1,0:T(8,128)(2,1)S(1)}, bf16[2,256,512]{2,1,0:T(8,128)(2,1)S(1)}, u32[]{:S(2)}, u32[]{:S(2)}) collective-permute-start(bf16[2,256,512]{2,1,0:T(8,128)(2,1)S(1)} %shard_map.88.refs_0_), channel_id=1, source_target_pairs={{0,384},{192,576},{384,0},{576,192},{1,385},{193,577},{385,1},{577... | collective-permute-start | bytes 1572872 | tf_op jit(solution)/shard_map/ppermute | solution.py:237
  61.5 11.6 %all-to-all-start.2 = ((bf16[4,16,512]{2,1,0:T(8,128)(2,1)}), bf16[4,16,512]{2,1,0:T(8,128)(2,1)S(1)}, u32[]{:S(2)}, u32[]{:S(2)}) async-start(bf16[4,16,512]{2,1,0:T(8,128)(2,1)} %bitcast.5), calls=%async_computation.2 | async-start | bytes 131072 | tf_op jit(solution)/shard_map/all_to_all | solution.py:246
  92.4 38.4 %copy-start.1 = (bf16[128,4096]{1,0:T(8,128)(2,1)S(1)}, bf16[128,4096]{1,0:T(8,128)(2,1)}, u32[]{:S(2)}) copy-start(bf16[128,4096]{1,0:T(8,128)(2,1)} %refs_1_.3) | copy-start | bytes 3145732
  92.4 38.4 %copy-start.2 = (bf16[128,512]{1,0:T(8,128)(2,1)S(1)}, bf16[128,512]{1,0:T(8,128)(2,1)}, u32[]{:S(2)}) copy-start(bf16[128,512]{1,0:T(8,128)(2,1)} %refs_2_.3) | copy-start | bytes 393220
  92.4 38.4 %collective-permute-start.6 = (bf16[4,2,256,512]{3,2,1,0:T(8,128)(2,1)}, bf16[4,2,256,512]{3,2,1,0:T(8,128)(2,1)}, u32[]{:S(2)}, u32[]{:S(2)}) collective-permute-start(bf16[4,2,256,512]{3,2,1,0:T(8,128)(2,1)} %get-tuple-element.19.refs_3_), channel_id=1, source_target_pairs={{0,1},{1,0},{2,3},{3,2},{4,5},{5,4},{6,7},{7,6},{8,9},{9,8},{10,11... | collective-permute-start | bytes 6291464 | tf_op jit(solution)/shard_map/ppermute | solution.py:272
  116.3 4.8 %collective-permute-start.5 = (bf16[256,512]{1,0:T(8,128)(2,1)S(1)}, bf16[256,512]{1,0:T(8,128)(2,1)S(1)}, u32[]{:S(2)}, u32[]{:S(2)}) collective-permute-start(bf16[256,512]{1,0:T(8,128)(2,1)S(1)} %bitcast.8), channel_id=1, source_target_pairs={{0,1},{1,0},{2,3},{3,2},{4,5},{5,4},{6,7},{7,6},{8,9},{9,8},{10,11... | collective-permute-start | bytes 786440 | tf_op jit(solution)/shard_map/ppermute | solution.py:273
  122.5 15.7 %all-to-all-start.5 = ((f32[8,4,128]{2,1,0:T(4,128)}), f32[8,4,128]{2,1,0:T(4,128)S(1)}, u32[]{:S(2)}, u32[]{:S(2)}) async-start(f32[8,4,128]{2,1,0:T(4,128)} %shard_map.93.refs_5_.refs_4_), calls=%async_computation.5 | async-start | bytes 32768 | tf_op jit(solution)/shard_map/all_to_all | solution.py:284

commit v7 on v5

--- a/solution.py
+++ b/solution.py
@@ -46,12 +46,15 @@
     loads.append(pltpu.make_async_copy(cot_ref, cot, come.at[peers]))
     for load in loads:
         load.start()
-    stores = []
+    stores = [
+        pltpu.make_async_copy(hidden_ref.at[:, pl.ds(i * part, part)], sent_ref.at[i, :, pl.ds(0, part)], go.at[i])
+        for i in range(peers)
+    ]
+    for store in stores:
+        store.start()
     square = jnp.zeros((tok, 1), F32)
     for i in range(peers):
         loads[i].wait()
-        stores.append(pltpu.make_async_copy(hidden.at[i], sent_ref.at[i, :, pl.ds(0, part)], go.at[i]))
-        stores[-1].start()
         piece = hidden[i].astype(F32)
         square = square + jnp.sum(piece * piece, axis=1, keepdims=True)
     inv = lax.rsqrt(square / (peers * part) + 1e-05)
@@ -160,28 +163,11 @@
         grad_ref[:, columns] = (inv * (value - unit * mean)).astype(BF16)
 
 
-def halve_kernel(place_ref, terms_ref, keep_ref, send_ref):
-    rows = keep_ref.shape[0]
-    mine = place_ref[3]
-    for ref, which in ((send_ref, 1 - mine), (keep_ref, mine)):
-        at = pl.ds(pl.multiple_of(which * rows, rows), rows)
-        total = terms_ref[0, at, :].astype(F32)
-        for i in range(1, terms_ref.shape[0]):
-            total = total + terms_ref[i, at, :].astype(F32)
-        ref[...] = total.astype(BF16)
-
-
-def add_kernel(keep_ref, came_ref, copies_ref):
-    total = (keep_ref[...].astype(F32) + came_ref[...].astype(F32)).astype(BF16)
-    for i in range(copies_ref.shape[0]):
-        copies_ref[i] = total
-
-
 def total_kernel(scale, terms_ref, copies_ref):
     total = terms_ref[0].astype(F32)
     for i in range(1, terms_ref.shape[0]):
         total = total + terms_ref[i].astype(F32)
-    total = (total * scale).astype(BF16)
+    total = (total if scale == 1 else total * scale).astype(BF16)
     for i in range(copies_ref.shape[0]):
         copies_ref[i] = total
 
@@ -214,7 +200,7 @@
     total_tokens = tok * nx * nh * nl * nz * np * nc
     half = rows // nc
     part = width // nx
-    place = jnp.stack([lax.axis_index(a) for a in ("c", "x", "yh", "zp")]).astype(jnp.int32)
+    place = jnp.stack([lax.axis_index(a) for a in ("c", "x", "yh")]).astype(jnp.int32)
     scales, gain = key_scales.T, norm_gain[None]
 
     sent, mark = pl.pallas_call(
@@ -252,14 +238,15 @@
     quarter = half // nl
     eighth = quarter // np
     own = [pair] + [lax.ppermute(pair, "x", [(i, (i + s) % nx) for i in range(nx)]) for s in range(1, nx)]
-    terms = lax.all_to_all(product.reshape(nh * nl, quarter, cols), ("yh", "yl"), 0, 0)
-    keep, send = call(
-        halve_kernel, [shape((eighth, cols), BF16)] * 2, [SMEM, VMEM], nh * nl * quarter * cols, 2 * half * cols, [own[1], own[-1]]
-    )(place, terms)
+    terms = lax.all_to_all(product.reshape(nh * nl * np, eighth, cols), ("yh", "yl", "zp"), 0, 0)
     copies = call(
-        add_kernel, shape((nz, eighth, cols), BF16), [VMEM, VMEM], eighth * cols, 2 * nz * eighth * cols
-    )(keep, lax.ppermute(send, "zp", SWAP))
-    scale = float(total_tokens) ** -0.5
+        functools.partial(total_kernel, 1.0),
+        shape((nz, eighth, cols), BF16),
+        [VMEM],
+        nh * nl * quarter * cols,
+        2 * (nh * nl * np + nz) * eighth * cols,
+        [own[1]],
+    )(terms)
     copies = call(
         functools.partial(total_kernel, float(total_tokens) ** -0.5),
         shape((nl * np, eighth, cols), BF16),

time: 135 us -> 158 us (1.17)
  Pallas kernels: 16.5 us -> 46.4 us
  waiting for transfers between devices: 19.6 us -> 14 us
  starting transfers between devices: 59.9 us -> 58.3 us
    pallas_call x1, Pallas kernels: 3.16 us -> 33.6 us  [body(): pl.pallas_call(prepare_kernel, out_shape=[shape((nx, tok, part + cols), B...]
    ppermute x3, waiting for transfers between devices: 11 us -> 5.85 us  [body(): lax.ppermute(pair, 'x', [(i, (i + s) % nx) for i in range(nx)])]
    ppermute x1 -> x0, starting transfers between devices: 4 us -> none  [body(): lax.ppermute(send, 'zp', SWAP)]
    all_to_all x1, starting transfers between devices: 4.01 us -> 5.93 us  [body(): lax.all_to_all(product.reshape(nh * nl * np, eighth, cols), ('yh', 'yl',...]
    pallas_call x11 -> x10, Pallas kernels: 13.3 us -> 12.8 us  [call(): return lambda *operands: made(*operands, *after)]
  transfers between devices with their start and end apart: 11 -> 10, of which waited for: 8 -> 6; matrix products, arithmetic and copies ran while one was open for 0% -> 0% of each run, Pallas kernels for 7% -> 6%
where the time goes in v7:
time: 158 us; the launch traced here: 157 us
  starting transfers between devices  58.3 us (37%)
  Pallas kernels  46.4 us (29%)
  blocking collectives  36.1 us (23%)
  waiting for transfers between devices  14 us (9%)
    pallas_call x1, Pallas kernels, body(): pl.pallas_call(prepare_kernel, out_shape=[shape((nx, tok, part + cols), B...  33.6 us
    all_to_all x1, blocking collectives, body(): lax.all_to_all(copies, 'z', 0, 0)  23.7 us
    ppermute x1, starting transfers between devices, body(): product = (keep + lax.ppermute(send, 'c', SWAP).astype(F32)).astype(BF16)  13.8 us
    pallas_call x10, Pallas kernels, call(): return lambda *operands: made(*operands, *after)  12.8 us
    all_to_all x1, blocking collectives, body(): whole = lax.all_to_all(copies, ('yl', 'zp'), 0, 0).reshape(half, cols)  12.4 us
    ppermute x3, starting transfers between devices, body(): lax.ppermute(pair, 'x', [(i, (i + s) % nx) for i in range(nx)])  10.1 us
    ppermute x1, starting transfers between devices, body(): mate = lax.ppermute(mine, 'yh', SWAP)  7.45 us
    all_to_all x1, starting transfers between devices, body(): gain_gradient = lax.all_to_all(gain_part, ('x', 'yh'), 0, 0).reshape(width)  6.35 us
  transfers between devices with their start and end apart: 10, of which 6 were waited for; matrix products, arithmetic and copies ran while one was open for 0% of the time, Pallas kernels for 6%

profile of v7, /device:TPU:1, one launch (start us, length us, event | category | flops | bytes accessed | tf_op | source)
XLA Modules:
  0.0 157.2 jit_solution(472026782152926488)
XLA Ops:
  0.6 0.0 copy-start.5
  0.6 0.0 copy-start.3
  0.7 0.0 copy-start
  0.7 33.6 %shard_map.84 = (bf16[4,128,1536]{2,1,0:T(8,128)(2,1)}, f32[8,1]{1,0:T(8,128)}) custom-call(bf16[128,4096]{1,0:T(8,128)(2,1)} %refs_1_.3, bf16[128,512]{1,0:T(8,128)(2,1)} %refs_2_.3), custom_call_target="tpu_custom_call" | custom-call | flops 2097152 | bytes 2097152 | tf_op jit(solution)/shard_map/pallas_call | solution.py:206
  34.3 0.0 copy-start.4
  34.3 4.9 %all-to-all-start = ((bf16[4,128,1536]{2,1,0:T(8,128)(2,1)}), bf16[4,128,1536]{2,1,0:T(8,128)(2,1)S(1)}, u32[]{:S(2)}, u32[]{:S(2)}) async-start(bf16[4,128,1536]{2,1,0:T(8,128)(2,1)} %get-tuple-element.14), calls=%async_computation | async-start | bytes 3145728 | tf_op jit(solution)/shard_map/all_to_all | solution.py:220
  39.1 0.0 copy-done.5
  39.1 0.1 pad_add_fusion.refs_0_
  39.2 0.0 copy-done.3
  39.2 0.0 copy-done
  39.2 0.0 copy-done.4
  39.2 0.7 shard_map.85.refs_0_
  39.9 7.5 %collective-permute-start = (bf16[256,512]{1,0:T(8,128)(2,1)S(1)}, bf16[256,512]{1,0:T(8,128)(2,1)S(1)}, u32[]{:S(2)}, u32[]{:S(2)}) collective-permute-start(bf16[256,512]{1,0:T(8,128)(2,1)S(1)} %shard_map.85.refs_0_), channel_id=1, source_target_pairs={{0,96},{96,0},{1,97},{97,1},{2,98},{98,2},{3,99},{99,3},{4,100},{1... | collective-permute-start | bytes 786440 | tf_op jit(solution)/shard_map/ppermute | solution.py:225
  47.4 3.8 %collective-permute-done.refs_2_.refs_1_ = bf16[256,512]{1,0:T(8,128)(2,1)S(1)} collective-permute-done((bf16[256,512]{1,0:T(8,128)(2,1)S(1)}, bf16[256,512]{1,0:T(8,128)(2,1)S(1)}, u32[]{:S(2)}, u32[]{:S(2)}) %collective-permute-start) | collective-permute-done | bytes 262176 | tf_op jit(solution)/shard_map/ppermute | solution.py:225
  51.2 0.5 all-to-all-done.refs_1_
  51.7 1.3 shard_map.86
  53.0 13.8 %collective-permute-start.1 = (bf16[2,256,512]{2,1,0:T(8,128)(2,1)S(1)}, bf16[2,256,512]{2,1,0:T(8,128)(2,1)S(1)}, u32[]{:S(2)}, u32[]{:S(2)}) collective-permute-start(bf16[2,256,512]{2,1,0:T(8,128)(2,1)S(1)} %get-tuple-element.17), channel_id=1, source_target_pairs={{0,1},{1,0},{2,3},{3,2},{4,5},{5,4},{6,7},{7,6},{8,9},{9,8},{10,11... | collective-permute-start | bytes 1572872 | tf_op jit(solution)/shard_map/ppermute | solution.py:235
  66.8 1.5 collective-permute-done.1
  68.3 1.0 add_convert_fusion.refs_2_
  69.3 5.9 %all-to-all-start.1 = ((bf16[16,32,512]{2,1,0:T(8,128)(2,1)}), bf16[16,32,512]{2,1,0:T(8,128)(2,1)S(1)}, u32[]{:S(2)}, u32[]{:S(2)}) async-start(bf16[16,32,512]{2,1,0:T(8,128)(2,1)} %bitcast.4), calls=%async_computation.1 | async-start | bytes 1048576 | tf_op jit(solution)/shard_map/all_to_all | solution.py:241
  75.3 2.7 %collective-permute-start.2 = (bf16[2,256,512]{2,1,0:T(8,128)(2,1)S(1)}, bf16[2,256,512]{2,1,0:T(8,128)(2,1)S(1)}, u32[]{:S(2)}, u32[]{:S(2)}) collective-permute-start(bf16[2,256,512]{2,1,0:T(8,128)(2,1)S(1)} %shard_map.87.refs_0_), channel_id=1, source_target_pairs={{0,192},{192,384},{384,576},{576,0},{1,193},{193,385},{385,577},{5... | collective-permute-start | bytes 1572872 | tf_op jit(solution)/shard_map/ppermute | solution.py:240
  78.0 4.3 %collective-permute-start.3 = (bf16[2,256,512]{2,1,0:T(8,128)(2,1)S(1)}, bf16[2,256,512]{2,1,0:T(8,128)(2,1)S(1)}, u32[]{:S(2)}, u32[]{:S(2)}) collective-permute-start(bf16[2,256,512]{2,1,0:T(8,128)(2,1)S(1)} %shard_map.87.refs_0_), channel_id=1, source_target_pairs={{0,384},{192,576},{384,0},{576,192},{1,385},{193,577},{385,1},{577... | collective-permute-start | bytes 1572872 | tf_op jit(solution)/shard_map/ppermute | solution.py:240
  82.3 3.1 %collective-permute-start.4 = (bf16[2,256,512]{2,1,0:T(8,128)(2,1)S(1)}, bf16[2,256,512]{2,1,0:T(8,128)(2,1)S(1)}, u32[]{:S(2)}, u32[]{:S(2)}) collective-permute-start(bf16[2,256,512]{2,1,0:T(8,128)(2,1)S(1)} %shard_map.87.refs_0_), channel_id=1, source_target_pairs={{0,576},{192,0},{384,192},{576,384},{1,577},{193,1},{385,193},{577... | collective-permute-start | bytes 1572872 | tf_op jit(solution)/shard_map/ppermute | solution.py:240
  85.4 5.8 %collective-permute-done.2.refs_1_ = bf16[2,256,512]{2,1,0:T(8,128)(2,1)S(1)} collective-permute-done((bf16[2,256,512]{2,1,0:T(8,128)(2,1)S(1)}, bf16[2,256,512]{2,1,0:T(8,128)(2,1)S(1)}, u32[]{:S(2)}, u32[]{:S(2)}) %collective-permute-start.2) | collective-permute-done | bytes 524320 | tf_op jit(solution)/shard_map/ppermute | solution.py:240
  91.2 0.0 all-to-all-done.1.refs_0_
  91.2 0.1 shard_map.88
  91.3 23.7 %all_to_all.25.refs_0_ = bf16[6,32,512]{2,1,0:T(8,128)(2,1)S(1)} all-to-all(bf16[6,32,512]{2,1,0:T(8,128)(2,1)S(1)} %shard_map.88), channel_id=1, replica_groups=mesh['x'=4,'yh'=2,'yl'=4,'z'=6,'zp'=2,'c'=2] {'z'}, dimensions={0} | all-to-all | bytes 393216 | tf_op jit(solution)/shard_map/all_to_all | solution.py:256
  115.0 0.0 collective-permute-done.3.refs_2_
  115.0 0.0 collective-permute-done.4.refs_3_
  115.1 1.5 shard_map.90
  116.5 0.0 copy-start.1
  116.5 0.0 copy-start.2
  116.5 6.3 %collective-permute-start.6 = (bf16[4,2,256,512]{3,2,1,0:T(8,128)(2,1)}, bf16[4,2,256,512]{3,2,1,0:T(8,128)(2,1)}, u32[]{:S(2)}, u32[]{:S(2)}) collective-permute-start(bf16[4,2,256,512]{3,2,1,0:T(8,128)(2,1)} %get-tuple-element.19.refs_3_), channel_id=1, source_target_pairs={{0,1},{1,0},{2,3},{3,2},{4,5},{5,4},{6,7},{7,6},{8,9},{9,8},{10,11... | collective-permute-start | bytes 6291464 | tf_op jit(solution)/shard_map/ppermute | solution.py:267
  122.8 12.4 %all_to_all.26 = bf16[8,32,512]{2,1,0:T(8,128)(2,1)S(1)} all-to-all(bf16[8,32,512]{2,1,0:T(8,128)(2,1)S(1)} %shard_map.89.refs_4_), channel_id=1, replica_groups=mesh['x'=4,'yh'=2,'yl'=4,'z'=6,'zp'=2,'c'=2] {'yl','zp'}, dimensions={0} | all-to-all | bytes 524288 | tf_op jit(solution)/shard_map/all_to_all | solution.py:258
  135.1 3.6 %collective-permute-start.5 = (bf16[256,512]{1,0:T(8,128)(2,1)S(1)}, bf16[256,512]{1,0:T(8,128)(2,1)S(1)}, u32[]{:S(2)}, u32[]{:S(2)}) collective-permute-start(bf16[256,512]{1,0:T(8,128)(2,1)S(1)} %bitcast.7), channel_id=1, source_target_pairs={{0,1},{1,0},{2,3},{3,2},{4,5},{5,4},{6,7},{7,6},{8,9},{9,8},{10,11... | collective-permute-start | bytes 786440 | tf_op jit(solution)/shard_map/ppermute | solution.py:268
  138.7 0.8 shard_map.91.refs_1_
  139.5 0.3 collective-permute-done.5.refs_2_
  139.8 1.4 shard_map.92.refs_5_.refs_4_
  141.3 6.3 %all-to-all-start.4 = ((f32[8,4,128]{2,1,0:T(4,128)}), f32[8,4,128]{2,1,0:T(4,128)S(1)}, u32[]{:S(2)}, u32[]{:S(2)}) async-start(f32[8,4,128]{2,1,0:T(4,128)} %shard_map.92.refs_5_.refs_4_), calls=%async_computation.4 | async-start | bytes 32768 | tf_op jit(solution)/shard_map/all_to_all | solution.py:279
  147.6 1.5 shard_map.94
  149.1 0.0 collective-permute-done.6.refs_4_
  149.1 0.0 copy-done.1
  149.1 0.0 copy-done.2
  149.1 5.5 %shard_map.93 = (bf16[128,512]{1,0:T(8,128)(2,1)}, bf16[128,4096]{1,0:T(8,128)(2,1)}) custom-call(s32[3]{0:T(128)S(1)} %pad_add_fusion.refs_0_, bf16[128,4096]{1,0:T(8,128)(2,1)S(1)} %copy-done.1, bf16[128,512]{1,0:T(8,128)(2,1)S(1)} %copy-done.2, bf16[4,2,256,512]{3,2,1,0:T(8,128)(2,1)} %get-tuple-element.19.refs_3_, ...), custom_call_target="tpu_custom_call" | custom-call | flops 1073741824 | bytes 6291456 | tf_op jit(solution)/shard_map/pallas_call | solution.py:189
  154.6 2.0 %all-to-all-done.4 = f32[8,4,128]{2,1,0:T(4,128)S(1)} async-done(((f32[8,4,128]{2,1,0:T(4,128)}), f32[8,4,128]{2,1,0:T(4,128)S(1)}, u32[]{:S(2)}, u32[]{:S(2)}) %all-to-all-start.4) | async-done | bytes 16416 | tf_op jit(solution)/shard_map/all_to_all | solution.py:279
  156.6 0.6 copy.10
  (3 shorter events, 0.1 us)
Async XLA Ops:
  0.6 38.5 %copy-start.5 = (bf16[512]{0:T(512)(128)(2,1)S(1)}, bf16[512]{0:T(512)(128)(2,1)}, u32[]{:S(2)}) copy-start(bf16[512]{0:T(512)(128)(2,1)} %param.6) | copy-start | bytes 3076
  0.6 38.6 %copy-start.3 = (bf16[512,2]{0,1:T(2,128)(2,1)S(1)}, bf16[512,2]{0,1:T(2,128)(2,1)}, u32[]{:S(2)}) copy-start(bf16[512,2]{0,1:T(2,128)(2,1)} %param.8) | copy-start | bytes 6148
  0.7 38.6 %copy-start = (bf16[512,512]{1,0:T(8,128)(2,1)S(1)}, bf16[512,512]{1,0:T(8,128)(2,1)}, u32[]{:S(2)}) copy-start(bf16[512,512]{1,0:T(8,128)(2,1)} %refs_3_.1) | copy-start | bytes 1572868
  34.3 5.0 %copy-start.4 = (f32[8,1]{1,0:T(8,128)S(1)}, f32[8,1]{1,0:T(8,128)}, u32[]{:S(2)}) copy-start(f32[8,1]{1,0:T(8,128)} %get-tuple-element.15.refs_4_) | copy-start | bytes 100
  34.3 17.4 %all-to-all-start = ((bf16[4,128,1536]{2,1,0:T(8,128)(2,1)}), bf16[4,128,1536]{2,1,0:T(8,128)(2,1)S(1)}, u32[]{:S(2)}, u32[]{:S(2)}) async-start(bf16[4,128,1536]{2,1,0:T(8,128)(2,1)} %get-tuple-element.14), calls=%async_computation | async-start | bytes 3145728 | tf_op jit(solution)/shard_map/all_to_all | solution.py:220
  39.9 11.3 %collective-permute-start = (bf16[256,512]{1,0:T(8,128)(2,1)S(1)}, bf16[256,512]{1,0:T(8,128)(2,1)S(1)}, u32[]{:S(2)}, u32[]{:S(2)}) collective-permute-start(bf16[256,512]{1,0:T(8,128)(2,1)S(1)} %shard_map.85.refs_0_), channel_id=1, source_target_pairs={{0,96},{96,0},{1,97},{97,1},{2,98},{98,2},{3,99},{99,3},{4,100},{1... | collective-permute-start | bytes 786440 | tf_op jit(solution)/shard_map/ppermute | solution.py:225
  53.0 15.4 %collective-permute-start.1 = (bf16[2,256,512]{2,1,0:T(8,128)(2,1)S(1)}, bf16[2,256,512]{2,1,0:T(8,128)(2,1)S(1)}, u32[]{:S(2)}, u32[]{:S(2)}) collective-permute-start(bf16[2,256,512]{2,1,0:T(8,128)(2,1)S(1)} %get-tuple-element.17), channel_id=1, source_target_pairs={{0,1},{1,0},{2,3},{3,2},{4,5},{5,4},{6,7},{7,6},{8,9},{9,8},{10,11... | collective-permute-start | bytes 1572872 | tf_op jit(solution)/shard_map/ppermute | solution.py:235
  69.3 21.9 %all-to-all-start.1 = ((bf16[16,32,512]{2,1,0:T(8,128)(2,1)}), bf16[16,32,512]{2,1,0:T(8,128)(2,1)S(1)}, u32[]{:S(2)}, u32[]{:S(2)}) async-start(bf16[16,32,512]{2,1,0:T(8,128)(2,1)} %bitcast.4), calls=%async_computation.1 | async-start | bytes 1048576 | tf_op jit(solution)/shard_map/all_to_all | solution.py:241
  75.3 15.9 %collective-permute-start.2 = (bf16[2,256,512]{2,1,0:T(8,128)(2,1)S(1)}, bf16[2,256,512]{2,1,0:T(8,128)(2,1)S(1)}, u32[]{:S(2)}, u32[]{:S(2)}) collective-permute-start(bf16[2,256,512]{2,1,0:T(8,128)(2,1)S(1)} %shard_map.87.refs_0_), channel_id=1, source_target_pairs={{0,192},{192,384},{384,576},{576,0},{1,193},{193,385},{385,577},{5... | collective-permute-start | bytes 1572872 | tf_op jit(solution)/shard_map/ppermute | solution.py:240
  78.0 37.1 %collective-permute-start.3 = (bf16[2,256,512]{2,1,0:T(8,128)(2,1)S(1)}, bf16[2,256,512]{2,1,0:T(8,128)(2,1)S(1)}, u32[]{:S(2)}, u32[]{:S(2)}) collective-permute-start(bf16[2,256,512]{2,1,0:T(8,128)(2,1)S(1)} %shard_map.87.refs_0_), channel_id=1, source_target_pairs={{0,384},{192,576},{384,0},{576,192},{1,385},{193,577},{385,1},{577... | collective-permute-start | bytes 1572872 | tf_op jit(solution)/shard_map/ppermute | solution.py:240
  82.3 32.8 %collective-permute-start.4 = (bf16[2,256,512]{2,1,0:T(8,128)(2,1)S(1)}, bf16[2,256,512]{2,1,0:T(8,128)(2,1)S(1)}, u32[]{:S(2)}, u32[]{:S(2)}) collective-permute-start(bf16[2,256,512]{2,1,0:T(8,128)(2,1)S(1)} %shard_map.87.refs_0_), channel_id=1, source_target_pairs={{0,576},{192,0},{384,192},{576,384},{1,577},{193,1},{385,193},{577... | collective-permute-start | bytes 1572872 | tf_op jit(solution)/shard_map/ppermute | solution.py:240
  116.5 32.6 %copy-start.1 = (bf16[128,4096]{1,0:T(8,128)(2,1)S(1)}, bf16[128,4096]{1,0:T(8,128)(2,1)}, u32[]{:S(2)}) copy-start(bf16[128,4096]{1,0:T(8,128)(2,1)} %refs_1_.3) | copy-start | bytes 3145732
  116.5 32.6 %copy-start.2 = (bf16[128,512]{1,0:T(8,128)(2,1)S(1)}, bf16[128,512]{1,0:T(8,128)(2,1)}, u32[]{:S(2)}) copy-start(bf16[128,512]{1,0:T(8,128)(2,1)} %refs_2_.3) | copy-start | bytes 393220
  116.5 32.6 %collective-permute-start.6 = (bf16[4,2,256,512]{3,2,1,0:T(8,128)(2,1)}, bf16[4,2,256,512]{3,2,1,0:T(8,128)(2,1)}, u32[]{:S(2)}, u32[]{:S(2)}) collective-permute-start(bf16[4,2,256,512]{3,2,1,0:T(8,128)(2,1)} %get-tuple-element.19.refs_3_), channel_id=1, source_target_pairs={{0,1},{1,0},{2,3},{3,2},{4,5},{5,4},{6,7},{7,6},{8,9},{9,8},{10,11... | collective-permute-start | bytes 6291464 | tf_op jit(solution)/shard_map/ppermute | solution.py:267
  135.1 4.7 %collective-permute-start.5 = (bf16[256,512]{1,0:T(8,128)(2,1)S(1)}, bf16[256,512]{1,0:T(8,128)(2,1)S(1)}, u32[]{:S(2)}, u32[]{:S(2)}) collective-permute-start(bf16[256,512]{1,0:T(8,128)(2,1)S(1)} %bitcast.7), channel_id=1, source_target_pairs={{0,1},{1,0},{2,3},{3,2},{4,5},{5,4},{6,7},{7,6},{8,9},{9,8},{10,11... | collective-permute-start | bytes 786440 | tf_op jit(solution)/shard_map/ppermute | solution.py:268
  141.3 15.3 %all-to-all-start.4 = ((f32[8,4,128]{2,1,0:T(4,128)}), f32[8,4,128]{2,1,0:T(4,128)S(1)}, u32[]{:S(2)}, u32[]{:S(2)}) async-start(f32[8,4,128]{2,1,0:T(4,128)} %shard_map.92.refs_5_.refs_4_), calls=%async_computation.4 | async-start | bytes 32768 | tf_op jit(solution)/shard_map/all_to_all | solution.py:279

commit v8 on v7

--- a/solution.py
+++ b/solution.py
@@ -46,15 +46,12 @@
     loads.append(pltpu.make_async_copy(cot_ref, cot, come.at[peers]))
     for load in loads:
         load.start()
-    stores = [
-        pltpu.make_async_copy(hidden_ref.at[:, pl.ds(i * part, part)], sent_ref.at[i, :, pl.ds(0, part)], go.at[i])
-        for i in range(peers)
-    ]
-    for store in stores:
-        store.start()
+    stores = []
     square = jnp.zeros((tok, 1), F32)
     for i in range(peers):
         loads[i].wait()
+        stores.append(pltpu.make_async_copy(hidden.at[i], sent_ref.at[i, :, pl.ds(0, part)], go.at[i]))
+        stores[-1].start()
         piece = hidden[i].astype(F32)
         square = square + jnp.sum(piece * piece, axis=1, keepdims=True)
     inv = lax.rsqrt(square / (peers * part) + 1e-05)
@@ -245,7 +242,6 @@
         [VMEM],
         nh * nl * quarter * cols,
         2 * (nh * nl * np + nz) * eighth * cols,
-        [own[1]],
     )(terms)
     copies = call(
         functools.partial(total_kernel, float(total_tokens) ** -0.5),
@@ -253,6 +249,7 @@
         [VMEM],
         nz * eighth * cols,
         2 * (nz + nl * np) * eighth * cols,
+        own[1:],
     )(lax.all_to_all(copies, "z", 0, 0))
 
     whole = lax.all_to_all(copies, ("yl", "zp"), 0, 0).reshape(half, cols)

time: 158 us -> 127 us (0.80)
  Pallas kernels: 46.4 us -> 16.6 us
  blocking collectives: 36.1 us -> 12.5 us
  starting transfers between devices: 58.3 us -> 71.5 us
  waiting for transfers between devices: 14 us -> 22.8 us
    pallas_call x1, Pallas kernels: 33.6 us -> 3.16 us  [body(): pl.pallas_call(prepare_kernel, out_shape=[shape((nx, tok, part + cols), B...]
    all_to_all x1 -> x0, blocking collectives: 23.7 us -> none  [body(): lax.all_to_all(copies, 'z', 0, 0)]
    all_to_all x0 -> x1, starting transfers between devices: none -> 13.9 us  [body(): lax.all_to_all(copies, 'z', 0, 0)]
    all_to_all x0 -> x1, waiting for transfers between devices: none -> 9.72 us  [body(): lax.all_to_all(copies, 'z', 0, 0)]
    ppermute x3, waiting for transfers between devices: 5.85 us -> 0.02 us  [body(): lax.ppermute(pair, 'x', [(i, (i + s) % nx) for i in range(nx)])]
    all_to_all x1, waiting for transfers between devices: 0.01 us -> 4.87 us  [body(): lax.all_to_all(product.reshape(nh * nl * np, eighth, cols), ('yh', 'yl',...]
    all_to_all x1, starting transfers between devices: 6.35 us -> 4.52 us  [body(): gain_gradient = lax.all_to_all(gain_part, ('x', 'yh'), 0, 0).reshape(width)]
  transfers between devices with their start and end apart: 10 -> 11, of which waited for: 6 -> 7; matrix products, arithmetic and copies ran while one was open for 0% -> 0% of each run, Pallas kernels for 6% -> 8%
where the time goes in v8:
time: 127 us; the launch traced here: 126 us
  starting transfers between devices  71.5 us (56%)
  waiting for transfers between devices  22.8 us (18%)
  Pallas kernels  16.6 us (13%)
  blocking collectives  12.5 us (10%)
    all_to_all x1, starting transfers between devices, body(): lax.all_to_all(copies, 'z', 0, 0)  13.9 us
    ppermute x1, starting transfers between devices, body(): product = (keep + lax.ppermute(send, 'c', SWAP).astype(F32)).astype(BF16)  13.8 us
    pallas_call x10, Pallas kernels, call(): return lambda *operands: made(*operands, *after)  13.4 us
    all_to_all x1, blocking collectives, body(): whole = lax.all_to_all(copies, ('yl', 'zp'), 0, 0).reshape(half, cols)  12.5 us
    ppermute x3, starting transfers between devices, body(): lax.ppermute(pair, 'x', [(i, (i + s) % nx) for i in range(nx)])  10.1 us
    all_to_all x1, waiting for transfers between devices, body(): lax.all_to_all(copies, 'z', 0, 0)  9.72 us
    ppermute x1, starting transfers between devices, body(): mate = lax.ppermute(mine, 'yh', SWAP)  7.45 us
    ppermute x1, starting transfers between devices, body(): other = lax.ppermute(own, 'c', SWAP)  7.37 us
  transfers between devices with their start and end apart: 11, of which 7 were waited for; matrix products, arithmetic and copies ran while one was open for 0% of the time, Pallas kernels for 8%

profile of v8, /device:TPU:1, one launch (start us, length us, event | category | flops | bytes accessed | tf_op | source)
XLA Modules:
  0.0 125.8 jit_solution(16792036316560531143)
XLA Ops:
  0.6 0.0 copy-start.5
  0.6 0.0 copy-start.3
  0.7 0.0 copy-start
  0.7 3.2 %shard_map.84 = (bf16[4,128,1536]{2,1,0:T(8,128)(2,1)}, f32[8,1]{1,0:T(8,128)}) custom-call(bf16[128,4096]{1,0:T(8,128)(2,1)} %refs_1_.3, bf16[128,512]{1,0:T(8,128)(2,1)} %refs_2_.3), custom_call_target="tpu_custom_call" | custom-call | flops 2097152 | bytes 2097152 | tf_op jit(solution)/shard_map/pallas_call | solution.py:203
  3.8 0.0 copy-start.4
  3.8 4.9 %all-to-all-start = ((bf16[4,128,1536]{2,1,0:T(8,128)(2,1)}), bf16[4,128,1536]{2,1,0:T(8,128)(2,1)S(1)}, u32[]{:S(2)}, u32[]{:S(2)}) async-start(bf16[4,128,1536]{2,1,0:T(8,128)(2,1)} %get-tuple-element.14), calls=%async_computation | async-start | bytes 3145728 | tf_op jit(solution)/shard_map/all_to_all | solution.py:217
  8.7 0.0 copy-done.5
  8.7 0.1 pad_add_fusion.refs_0_
  8.8 0.0 copy-done.3
  8.8 0.0 copy-done
  8.8 0.0 copy-done.4
  8.8 0.7 shard_map.85.refs_0_
  9.5 7.5 %collective-permute-start = (bf16[256,512]{1,0:T(8,128)(2,1)S(1)}, bf16[256,512]{1,0:T(8,128)(2,1)S(1)}, u32[]{:S(2)}, u32[]{:S(2)}) collective-permute-start(bf16[256,512]{1,0:T(8,128)(2,1)S(1)} %shard_map.85.refs_0_), channel_id=1, source_target_pairs={{0,96},{96,0},{1,97},{97,1},{2,98},{98,2},{3,99},{99,3},{4,100},{1... | collective-permute-start | bytes 786440 | tf_op jit(solution)/shard_map/ppermute | solution.py:222
  16.9 3.8 %collective-permute-done.refs_2_.refs_1_ = bf16[256,512]{1,0:T(8,128)(2,1)S(1)} collective-permute-done((bf16[256,512]{1,0:T(8,128)(2,1)S(1)}, bf16[256,512]{1,0:T(8,128)(2,1)S(1)}, u32[]{:S(2)}, u32[]{:S(2)}) %collective-permute-start) | collective-permute-done | bytes 262176 | tf_op jit(solution)/shard_map/ppermute | solution.py:222
  20.8 0.5 all-to-all-done.refs_1_
  21.2 1.3 %shard_map.86 = (f32[2,256,512]{2,1,0:T(8,128)S(1)}, bf16[2,256,512]{2,1,0:T(8,128)(2,1)S(1)}) custom-call(s32[3]{0:T(128)S(1)} %pad_add_fusion.refs_0_, bf16[4,128,1536]{2,1,0:T(8,128)(2,1)S(1)} %all-to-all-done.refs_1_, bf16[256,512]{1,0:T(8,128)(2,1)S(1)} %collective-permute-done.refs_2_.refs_1_), custom_call_target="tpu_custom_call" | custom-call | flops 536870912 | bytes 3145728 | tf_op jit(solution)/shard_map/pallas_call | solution.py:186
  22.5 13.8 %collective-permute-start.1 = (bf16[2,256,512]{2,1,0:T(8,128)(2,1)S(1)}, bf16[2,256,512]{2,1,0:T(8,128)(2,1)S(1)}, u32[]{:S(2)}, u32[]{:S(2)}) collective-permute-start(bf16[2,256,512]{2,1,0:T(8,128)(2,1)S(1)} %get-tuple-element.17), channel_id=1, source_target_pairs={{0,1},{1,0},{2,3},{3,2},{4,5},{5,4},{6,7},{7,6},{8,9},{9,8},{10,11... | collective-permute-start | bytes 1572872 | tf_op jit(solution)/shard_map/ppermute | solution.py:232
  36.4 1.5 %collective-permute-done.1 = bf16[2,256,512]{2,1,0:T(8,128)(2,1)S(1)} collective-permute-done((bf16[2,256,512]{2,1,0:T(8,128)(2,1)S(1)}, bf16[2,256,512]{2,1,0:T(8,128)(2,1)S(1)}, u32[]{:S(2)}, u32[]{:S(2)}) %collective-permute-start.1) | collective-permute-done | bytes 524320 | tf_op jit(solution)/shard_map/ppermute | solution.py:232
  37.9 1.0 add_convert_fusion.refs_2_
  38.9 5.9 %all-to-all-start.1 = ((bf16[16,32,512]{2,1,0:T(8,128)(2,1)}), bf16[16,32,512]{2,1,0:T(8,128)(2,1)S(1)}, u32[]{:S(2)}, u32[]{:S(2)}) async-start(bf16[16,32,512]{2,1,0:T(8,128)(2,1)} %bitcast.4), calls=%async_computation.1 | async-start | bytes 1048576 | tf_op jit(solution)/shard_map/all_to_all | solution.py:238
  44.8 2.7 %collective-permute-start.2 = (bf16[2,256,512]{2,1,0:T(8,128)(2,1)S(1)}, bf16[2,256,512]{2,1,0:T(8,128)(2,1)S(1)}, u32[]{:S(2)}, u32[]{:S(2)}) collective-permute-start(bf16[2,256,512]{2,1,0:T(8,128)(2,1)S(1)} %shard_map.88.refs_0_), channel_id=1, source_target_pairs={{0,192},{192,384},{384,576},{576,0},{1,193},{193,385},{385,577},{5... | collective-permute-start | bytes 1572872 | tf_op jit(solution)/shard_map/ppermute | solution.py:237
  47.5 4.3 %collective-permute-start.3 = (bf16[2,256,512]{2,1,0:T(8,128)(2,1)S(1)}, bf16[2,256,512]{2,1,0:T(8,128)(2,1)S(1)}, u32[]{:S(2)}, u32[]{:S(2)}) collective-permute-start(bf16[2,256,512]{2,1,0:T(8,128)(2,1)S(1)} %shard_map.88.refs_0_), channel_id=1, source_target_pairs={{0,384},{192,576},{384,0},{576,192},{1,385},{193,577},{385,1},{577... | collective-permute-start | bytes 1572872 | tf_op jit(solution)/shard_map/ppermute | solution.py:237
  51.8 3.1 %collective-permute-start.4 = (bf16[2,256,512]{2,1,0:T(8,128)(2,1)S(1)}, bf16[2,256,512]{2,1,0:T(8,128)(2,1)S(1)}, u32[]{:S(2)}, u32[]{:S(2)}) collective-permute-start(bf16[2,256,512]{2,1,0:T(8,128)(2,1)S(1)} %shard_map.88.refs_0_), channel_id=1, source_target_pairs={{0,576},{192,0},{384,192},{576,384},{1,577},{193,1},{385,193},{577... | collective-permute-start | bytes 1572872 | tf_op jit(solution)/shard_map/ppermute | solution.py:237
  54.9 4.9 %all-to-all-done.1.refs_0_ = bf16[16,32,512]{2,1,0:T(8,128)(2,1)S(1)} async-done(((bf16[16,32,512]{2,1,0:T(8,128)(2,1)}), bf16[16,32,512]{2,1,0:T(8,128)(2,1)S(1)}, u32[]{:S(2)}, u32[]{:S(2)}) %all-to-all-start.1) | async-done | bytes 524320 | tf_op jit(solution)/shard_map/all_to_all | solution.py:238
  59.8 0.8 shard_map.87
  60.5 13.9 %all-to-all-start.2 = ((bf16[6,32,512]{2,1,0:T(8,128)(2,1)}), bf16[6,32,512]{2,1,0:T(8,128)(2,1)S(1)}, u32[]{:S(2)}, u32[]{:S(2)}) async-start(bf16[6,32,512]{2,1,0:T(8,128)(2,1)} %shard_map.87), calls=%async_computation.2 | async-start | bytes 393216 | tf_op jit(solution)/shard_map/all_to_all | solution.py:253
  74.5 0.0 collective-permute-done.2.refs_1_
  74.5 0.0 collective-permute-done.3.refs_2_
  74.5 0.0 collective-permute-done.4.refs_3_
  74.5 9.7 %all-to-all-done.2.refs_0_ = bf16[6,32,512]{2,1,0:T(8,128)(2,1)S(1)} async-done(((bf16[6,32,512]{2,1,0:T(8,128)(2,1)}), bf16[6,32,512]{2,1,0:T(8,128)(2,1)S(1)}, u32[]{:S(2)}, u32[]{:S(2)}) %all-to-all-start.2) | async-done | bytes 196640 | tf_op jit(solution)/shard_map/all_to_all | solution.py:253
  84.3 1.5 %shard_map.90 = (bf16[4,2,256,512]{3,2,1,0:T(8,128)(2,1)}, bf16[16,128]{1,0:T(8,128)(2,1)S(1)}) custom-call(bf16[2,256,512]{2,1,0:T(8,128)(2,1)S(1)} %shard_map.88.refs_0_, bf16[2,256,512]{2,1,0:T(8,128)(2,1)S(1)} %collective-permute-done.2.refs_1_, bf16[2,256,512]{2,1,0:T(8,128)(2,1)S(1)} %collective-permute-done.3.refs_2_, ...), custom_call_target="tpu_custom_call" | custom-call | bytes 8388608 | tf_op jit(solution)/shard_map/pallas_call | solution.py:186
  85.7 0.0 copy-start.1
  85.7 0.0 copy-start.2
  85.7 7.4 %collective-permute-start.6 = (bf16[4,2,256,512]{3,2,1,0:T(8,128)(2,1)}, bf16[4,2,256,512]{3,2,1,0:T(8,128)(2,1)}, u32[]{:S(2)}, u32[]{:S(2)}) collective-permute-start(bf16[4,2,256,512]{3,2,1,0:T(8,128)(2,1)} %get-tuple-element.19.refs_3_), channel_id=1, source_target_pairs={{0,1},{1,0},{2,3},{3,2},{4,5},{5,4},{6,7},{7,6},{8,9},{9,8},{10,11... | collective-permute-start | bytes 6291464 | tf_op jit(solution)/shard_map/ppermute | solution.py:264
  93.1 12.5 %all_to_all.25 = bf16[8,32,512]{2,1,0:T(8,128)(2,1)S(1)} all-to-all(bf16[8,32,512]{2,1,0:T(8,128)(2,1)S(1)} %shard_map.89.refs_4_), channel_id=1, replica_groups=mesh['x'=4,'yh'=2,'yl'=4,'z'=6,'zp'=2,'c'=2] {'yl','zp'}, dimensions={0} | all-to-all | bytes 524288 | tf_op jit(solution)/shard_map/all_to_all | solution.py:255
  105.6 3.6 %collective-permute-start.5 = (bf16[256,512]{1,0:T(8,128)(2,1)S(1)}, bf16[256,512]{1,0:T(8,128)(2,1)S(1)}, u32[]{:S(2)}, u32[]{:S(2)}) collective-permute-start(bf16[256,512]{1,0:T(8,128)(2,1)S(1)} %bitcast.7), channel_id=1, source_target_pairs={{0,1},{1,0},{2,3},{3,2},{4,5},{5,4},{6,7},{7,6},{8,9},{9,8},{10,11... | collective-permute-start | bytes 786440 | tf_op jit(solution)/shard_map/ppermute | solution.py:265
  109.2 0.8 shard_map.91.refs_1_
  110.0 0.3 collective-permute-done.5.refs_2_
  110.3 1.4 %shard_map.92.refs_5_.refs_4_ = f32[8,4,128]{2,1,0:T(4,128)} custom-call(s32[3]{0:T(128)S(1)} %pad_add_fusion.refs_0_, f32[2,128]{1,0:T(2,128)S(1)} %shard_map.91.refs_1_, bf16[256,512]{1,0:T(8,128)(2,1)S(1)} %collective-permute-done.5.refs_2_, bf16[512,512]{1,0:T(8,128)(2,1)S(1)} %copy-done, bf16[2,512]{1,0:T(2,128)(2,1)S(1)} %bitcast.12), custom_call_target="tpu_custom_call" | custom-call | flops 262144 | bytes 524288 | tf_op jit(solution)/shard_map/pallas_call | solution.py:186
  111.7 4.5 %all-to-all-start.4 = ((f32[8,4,128]{2,1,0:T(4,128)}), f32[8,4,128]{2,1,0:T(4,128)S(1)}, u32[]{:S(2)}, u32[]{:S(2)}) async-start(f32[8,4,128]{2,1,0:T(4,128)} %shard_map.92.refs_5_.refs_4_), calls=%async_computation.4 | async-start | bytes 32768 | tf_op jit(solution)/shard_map/all_to_all | solution.py:276
  116.2 1.5 %shard_map.94 = bf16[512,512]{1,0:T(8,128)(2,1)} custom-call(s32[3]{0:T(128)S(1)} %pad_add_fusion.refs_0_, bf16[256,512]{1,0:T(8,128)(2,1)S(1)} %bitcast.9, bf16[256,512]{1,0:T(8,128)(2,1)S(1)} %collective-permute-done.5.refs_2_, bf16[1,512]{1,0:T(2,128)(2,1)S(1)} %broadcast_in_dim.3.refs_3_, f32[8,4,128]{2,1,0:T(4,128)} %shard_map.92.refs_5_.refs_4_), custom_call_target="tpu_custom_call" | custom-call | flops 262144 | bytes 1048576 | tf_op jit(solution)/shard_map/pallas_call | solution.py:186
  117.8 0.0 collective-permute-done.6.refs_4_
  117.8 0.0 copy-done.1
  117.8 0.0 copy-done.2
  117.8 5.4 %shard_map.93 = (bf16[128,512]{1,0:T(8,128)(2,1)}, bf16[128,4096]{1,0:T(8,128)(2,1)}) custom-call(s32[3]{0:T(128)S(1)} %pad_add_fusion.refs_0_, bf16[128,4096]{1,0:T(8,128)(2,1)S(1)} %copy-done.1, bf16[128,512]{1,0:T(8,128)(2,1)S(1)} %copy-done.2, bf16[4,2,256,512]{3,2,1,0:T(8,128)(2,1)} %get-tuple-element.19.refs_3_, ...), custom_call_target="tpu_custom_call" | custom-call | flops 1073741824 | bytes 6291456 | tf_op jit(solution)/shard_map/pallas_call | solution.py:186
  123.2 2.0 %all-to-all-done.4 = f32[8,4,128]{2,1,0:T(4,128)S(1)} async-done(((f32[8,4,128]{2,1,0:T(4,128)}), f32[8,4,128]{2,1,0:T(4,128)S(1)}, u32[]{:S(2)}, u32[]{:S(2)}) %all-to-all-start.4) | async-done | bytes 16416 | tf_op jit(solution)/shard_map/all_to_all | solution.py:276
  125.2 0.6 copy.10
  (3 shorter events, 0.1 us)
Async XLA Ops:
  0.6 8.1 %copy-start.5 = (bf16[512]{0:T(512)(128)(2,1)S(1)}, bf16[512]{0:T(512)(128)(2,1)}, u32[]{:S(2)}) copy-start(bf16[512]{0:T(512)(128)(2,1)} %param.6) | copy-start | bytes 3076
  0.6 8.1 %copy-start.3 = (bf16[512,2]{0,1:T(2,128)(2,1)S(1)}, bf16[512,2]{0,1:T(2,128)(2,1)}, u32[]{:S(2)}) copy-start(bf16[512,2]{0,1:T(2,128)(2,1)} %param.8) | copy-start | bytes 6148
  0.7 8.1 %copy-start = (bf16[512,512]{1,0:T(8,128)(2,1)S(1)}, bf16[512,512]{1,0:T(8,128)(2,1)}, u32[]{:S(2)}) copy-start(bf16[512,512]{1,0:T(8,128)(2,1)} %refs_3_.1) | copy-start | bytes 1572868
  3.8 5.0 %copy-start.4 = (f32[8,1]{1,0:T(8,128)S(1)}, f32[8,1]{1,0:T(8,128)}, u32[]{:S(2)}) copy-start(f32[8,1]{1,0:T(8,128)} %get-tuple-element.15.refs_4_) | copy-start | bytes 100
  3.8 17.4 %all-to-all-start = ((bf16[4,128,1536]{2,1,0:T(8,128)(2,1)}), bf16[4,128,1536]{2,1,0:T(8,128)(2,1)S(1)}, u32[]{:S(2)}, u32[]{:S(2)}) async-start(bf16[4,128,1536]{2,1,0:T(8,128)(2,1)} %get-tuple-element.14), calls=%async_computation | async-start | bytes 3145728 | tf_op jit(solution)/shard_map/all_to_all | solution.py:217
  9.5 11.3 %collective-permute-start = (bf16[256,512]{1,0:T(8,128)(2,1)S(1)}, bf16[256,512]{1,0:T(8,128)(2,1)S(1)}, u32[]{:S(2)}, u32[]{:S(2)}) collective-permute-start(bf16[256,512]{1,0:T(8,128)(2,1)S(1)} %shard_map.85.refs_0_), channel_id=1, source_target_pairs={{0,96},{96,0},{1,97},{97,1},{2,98},{98,2},{3,99},{99,3},{4,100},{1... | collective-permute-start | bytes 786440 | tf_op jit(solution)/shard_map/ppermute | solution.py:222
  22.5 15.4 %collective-permute-start.1 = (bf16[2,256,512]{2,1,0:T(8,128)(2,1)S(1)}, bf16[2,256,512]{2,1,0:T(8,128)(2,1)S(1)}, u32[]{:S(2)}, u32[]{:S(2)}) collective-permute-start(bf16[2,256,512]{2,1,0:T(8,128)(2,1)S(1)} %get-tuple-element.17), channel_id=1, source_target_pairs={{0,1},{1,0},{2,3},{3,2},{4,5},{5,4},{6,7},{7,6},{8,9},{9,8},{10,11... | collective-permute-start | bytes 1572872 | tf_op jit(solution)/shard_map/ppermute | solution.py:232
  38.9 20.9 %all-to-all-start.1 = ((bf16[16,32,512]{2,1,0:T(8,128)(2,1)}), bf16[16,32,512]{2,1,0:T(8,128)(2,1)S(1)}, u32[]{:S(2)}, u32[]{:S(2)}) async-start(bf16[16,32,512]{2,1,0:T(8,128)(2,1)} %bitcast.4), calls=%async_computation.1 | async-start | bytes 1048576 | tf_op jit(solution)/shard_map/all_to_all | solution.py:238
  44.8 29.6 %collective-permute-start.2 = (bf16[2,256,512]{2,1,0:T(8,128)(2,1)S(1)}, bf16[2,256,512]{2,1,0:T(8,128)(2,1)S(1)}, u32[]{:S(2)}, u32[]{:S(2)}) collective-permute-start(bf16[2,256,512]{2,1,0:T(8,128)(2,1)S(1)} %shard_map.88.refs_0_), channel_id=1, source_target_pairs={{0,192},{192,384},{384,576},{576,0},{1,193},{193,385},{385,577},{5... | collective-permute-start | bytes 1572872 | tf_op jit(solution)/shard_map/ppermute | solution.py:237
  47.5 27.0 %collective-permute-start.3 = (bf16[2,256,512]{2,1,0:T(8,128)(2,1)S(1)}, bf16[2,256,512]{2,1,0:T(8,128)(2,1)S(1)}, u32[]{:S(2)}, u32[]{:S(2)}) collective-permute-start(bf16[2,256,512]{2,1,0:T(8,128)(2,1)S(1)} %shard_map.88.refs_0_), channel_id=1, source_target_pairs={{0,384},{192,576},{384,0},{576,192},{1,385},{193,577},{385,1},{577... | collective-permute-start | bytes 1572872 | tf_op jit(solution)/shard_map/ppermute | solution.py:237
  51.8 22.7 %collective-permute-start.4 = (bf16[2,256,512]{2,1,0:T(8,128)(2,1)S(1)}, bf16[2,256,512]{2,1,0:T(8,128)(2,1)S(1)}, u32[]{:S(2)}, u32[]{:S(2)}) collective-permute-start(bf16[2,256,512]{2,1,0:T(8,128)(2,1)S(1)} %shard_map.88.refs_0_), channel_id=1, source_target_pairs={{0,576},{192,0},{384,192},{576,384},{1,577},{193,1},{385,193},{577... | collective-permute-start | bytes 1572872 | tf_op jit(solution)/shard_map/ppermute | solution.py:237
  60.5 23.7 %all-to-all-start.2 = ((bf16[6,32,512]{2,1,0:T(8,128)(2,1)}), bf16[6,32,512]{2,1,0:T(8,128)(2,1)S(1)}, u32[]{:S(2)}, u32[]{:S(2)}) async-start(bf16[6,32,512]{2,1,0:T(8,128)(2,1)} %shard_map.87), calls=%async_computation.2 | async-start | bytes 393216 | tf_op jit(solution)/shard_map/all_to_all | solution.py:253
  85.7 32.0 %copy-start.1 = (bf16[128,4096]{1,0:T(8,128)(2,1)S(1)}, bf16[128,4096]{1,0:T(8,128)(2,1)}, u32[]{:S(2)}) copy-start(bf16[128,4096]{1,0:T(8,128)(2,1)} %refs_1_.3) | copy-start | bytes 3145732
  85.7 32.0 %copy-start.2 = (bf16[128,512]{1,0:T(8,128)(2,1)S(1)}, bf16[128,512]{1,0:T(8,128)(2,1)}, u32[]{:S(2)}) copy-start(bf16[128,512]{1,0:T(8,128)(2,1)} %refs_2_.3) | copy-start | bytes 393220
  85.7 32.0 %collective-permute-start.6 = (bf16[4,2,256,512]{3,2,1,0:T(8,128)(2,1)}, bf16[4,2,256,512]{3,2,1,0:T(8,128)(2,1)}, u32[]{:S(2)}, u32[]{:S(2)}) collective-permute-start(bf16[4,2,256,512]{3,2,1,0:T(8,128)(2,1)} %get-tuple-element.19.refs_3_), channel_id=1, source_target_pairs={{0,1},{1,0},{2,3},{3,2},{4,5},{5,4},{6,7},{7,6},{8,9},{9,8},{10,11... | collective-permute-start | bytes 6291464 | tf_op jit(solution)/shard_map/ppermute | solution.py:264
  105.6 4.7 %collective-permute-start.5 = (bf16[256,512]{1,0:T(8,128)(2,1)S(1)}, bf16[256,512]{1,0:T(8,128)(2,1)S(1)}, u32[]{:S(2)}, u32[]{:S(2)}) collective-permute-start(bf16[256,512]{1,0:T(8,128)(2,1)S(1)} %bitcast.7), channel_id=1, source_target_pairs={{0,1},{1,0},{2,3},{3,2},{4,5},{5,4},{6,7},{7,6},{8,9},{9,8},{10,11... | collective-permute-start | bytes 786440 | tf_op jit(solution)/shard_map/ppermute | solution.py:265
  111.7 13.5 %all-to-all-start.4 = ((f32[8,4,128]{2,1,0:T(4,128)}), f32[8,4,128]{2,1,0:T(4,128)S(1)}, u32[]{:S(2)}, u32[]{:S(2)}) async-start(f32[8,4,128]{2,1,0:T(4,128)} %shard_map.92.refs_5_.refs_4_), calls=%async_computation.4 | async-start | bytes 32768 | tf_op jit(solution)/shard_map/all_to_all | solution.py:276

commit v9 on v8

--- a/solution.py
+++ b/solution.py
@@ -243,16 +243,6 @@
         nh * nl * quarter * cols,
         2 * (nh * nl * np + nz) * eighth * cols,
     )(terms)
-    copies = call(
-        functools.partial(total_kernel, float(total_tokens) ** -0.5),
-        shape((nl * np, eighth, cols), BF16),
-        [VMEM],
-        nz * eighth * cols,
-        2 * (nz + nl * np) * eighth * cols,
-        own[1:],
-    )(lax.all_to_all(copies, "z", 0, 0))
-
-    whole = lax.all_to_all(copies, ("yl", "zp"), 0, 0).reshape(half, cols)
     own, mark = call(
         marked_stack_kernel,
         [shape((nx, nh, half, cols), BF16), shape((16, LANES), BF16)],
@@ -261,10 +251,22 @@
         4 * width * cols,
         [copies],
     )(*own)
+    copies = call(
+        functools.partial(total_kernel, float(total_tokens) ** -0.5),
+        shape((nl * np, eighth, cols), BF16),
+        [VMEM],
+        nz * eighth * cols,
+        2 * (nz + nl * np) * eighth * cols,
+        [mark],
+    )(lax.all_to_all(copies, "z", 0, 0))
+
+    copies, own = tie(copies, own)
+
+    whole = lax.all_to_all(copies, ("yl", "zp"), 0, 0).reshape(half, cols)
     other = lax.ppermute(own, "c", SWAP)
     beside = lax.ppermute(whole, "c", SWAP)
     mine = call(
-        dots_kernel, shape((half // LANES, LANES), F32), [SMEM, VMEM, VMEM, VMEM], 2 * half * cols, 4 * half * cols, [mark]
+        dots_kernel, shape((half // LANES, LANES), F32), [SMEM, VMEM, VMEM, VMEM], 2 * half * cols, 4 * half * cols
     )(place, whole, key_codes, scales)
     gain_part = call(
         pair_dots_kernel,

time: 127 us -> 125 us (0.984)
  local copies, waits for them, and re-layouts: 0.64 us -> 3.54 us
  waiting for transfers between devices: 22.8 us -> 20.3 us
  Pallas kernels: 16.6 us -> 14.6 us
    unnamed x13 -> x17, local copies, waits for them, and re-layouts: 0.63 us -> 3.54 us
    pallas_call x10, Pallas kernels: 13.4 us -> 11.5 us  [call(): return lambda *operands: made(*operands, *after)]
    all_to_all x1, waiting for transfers between devices: 9.72 us -> 8.24 us  [body(): lax.all_to_all(copies, 'z', 0, 0)]
where the time goes in v9:
time: 125 us; the launch traced here: 124 us
  starting transfers between devices  71.4 us (57%)
  waiting for transfers between devices  20.3 us (16%)
  Pallas kernels  14.6 us (12%)
  blocking collectives  12.5 us (10%)
  local copies, waits for them, and re-layouts  3.54 us (3%)
    all_to_all x1, starting transfers between devices, body(): lax.all_to_all(copies, 'z', 0, 0)  13.9 us
    ppermute x1, starting transfers between devices, body(): product = (keep + lax.ppermute(send, 'c', SWAP).astype(F32)).astype(BF16)  13.8 us
    all_to_all x1, blocking collectives, body(): whole = lax.all_to_all(copies, ('yl', 'zp'), 0, 0).reshape(half, cols)  12.5 us
    pallas_call x10, Pallas kernels, call(): return lambda *operands: made(*operands, *after)  11.5 us
    ppermute x3, starting transfers between devices, body(): lax.ppermute(pair, 'x', [(i, (i + s) % nx) for i in range(nx)])  10.1 us
    all_to_all x1, waiting for transfers between devices, body(): lax.all_to_all(copies, 'z', 0, 0)  8.24 us
    ppermute x1, starting transfers between devices, body(): mate = lax.ppermute(mine, 'yh', SWAP)  7.45 us
    ppermute x1, starting transfers between devices, body(): other = lax.ppermute(own, 'c', SWAP)  7.25 us
  transfers between devices with their start and end apart: 11, of which 7 were waited for; matrix products, arithmetic and copies ran while one was open for 0% of the time, Pallas kernels for 8%

profile of v9, /device:TPU:1, one launch (start us, length us, event | category | flops | bytes accessed | tf_op | source)
XLA Modules:
  0.0 124.2 jit_solution(10084878073000620252)
XLA Ops:
  0.6 0.0 copy-start.7
  0.6 0.0 copy-start.5
  0.7 0.0 copy-start
  0.7 3.1 %shard_map.84 = (bf16[4,128,1536]{2,1,0:T(8,128)(2,1)}, f32[8,1]{1,0:T(8,128)}) custom-call(bf16[128,4096]{1,0:T(8,128)(2,1)} %refs_1_.3, bf16[128,512]{1,0:T(8,128)(2,1)} %refs_2_.3), custom_call_target="tpu_custom_call" | custom-call | flops 2097152 | bytes 2097152 | tf_op jit(solution)/shard_map/pallas_call | solution.py:203
  3.8 0.0 copy-start.6
  3.8 4.9 %all-to-all-start = ((bf16[4,128,1536]{2,1,0:T(8,128)(2,1)}), bf16[4,128,1536]{2,1,0:T(8,128)(2,1)S(1)}, u32[]{:S(2)}, u32[]{:S(2)}) async-start(bf16[4,128,1536]{2,1,0:T(8,128)(2,1)} %get-tuple-element.16), calls=%async_computation | async-start | bytes 3145728 | tf_op jit(solution)/shard_map/all_to_all | solution.py:217
  8.6 0.0 copy-done.7
  8.7 0.1 pad_add_fusion.refs_0_
  8.7 0.0 copy-done.5
  8.7 0.0 copy-done
  8.7 0.0 copy-done.6
  8.7 0.7 shard_map.85.refs_0_
  9.4 7.5 %collective-permute-start = (bf16[256,512]{1,0:T(8,128)(2,1)S(1)}, bf16[256,512]{1,0:T(8,128)(2,1)S(1)}, u32[]{:S(2)}, u32[]{:S(2)}) collective-permute-start(bf16[256,512]{1,0:T(8,128)(2,1)S(1)} %shard_map.85.refs_0_), channel_id=1, source_target_pairs={{0,96},{96,0},{1,97},{97,1},{2,98},{98,2},{3,99},{99,3},{4,100},{1... | collective-permute-start | bytes 786440 | tf_op jit(solution)/shard_map/ppermute | solution.py:222
  16.9 3.8 %collective-permute-done.refs_2_.refs_1_ = bf16[256,512]{1,0:T(8,128)(2,1)S(1)} collective-permute-done((bf16[256,512]{1,0:T(8,128)(2,1)S(1)}, bf16[256,512]{1,0:T(8,128)(2,1)S(1)}, u32[]{:S(2)}, u32[]{:S(2)}) %collective-permute-start) | collective-permute-done | bytes 262176 | tf_op jit(solution)/shard_map/ppermute | solution.py:222
  20.7 0.5 all-to-all-done.refs_1_
  21.2 1.3 %shard_map.86 = (f32[2,256,512]{2,1,0:T(8,128)S(1)}, bf16[2,256,512]{2,1,0:T(8,128)(2,1)S(1)}) custom-call(s32[3]{0:T(128)S(1)} %pad_add_fusion.refs_0_, bf16[4,128,1536]{2,1,0:T(8,128)(2,1)S(1)} %all-to-all-done.refs_1_, bf16[256,512]{1,0:T(8,128)(2,1)S(1)} %collective-permute-done.refs_2_.refs_1_), custom_call_target="tpu_custom_call" | custom-call | flops 536870912 | bytes 3145728 | tf_op jit(solution)/shard_map/pallas_call | solution.py:186
  22.5 13.8 %collective-permute-start.1 = (bf16[2,256,512]{2,1,0:T(8,128)(2,1)S(1)}, bf16[2,256,512]{2,1,0:T(8,128)(2,1)S(1)}, u32[]{:S(2)}, u32[]{:S(2)}) collective-permute-start(bf16[2,256,512]{2,1,0:T(8,128)(2,1)S(1)} %get-tuple-element.19), channel_id=1, source_target_pairs={{0,1},{1,0},{2,3},{3,2},{4,5},{5,4},{6,7},{7,6},{8,9},{9,8},{10,11... | collective-permute-start | bytes 1572872 | tf_op jit(solution)/shard_map/ppermute | solution.py:232
  36.3 1.5 %collective-permute-done.1 = bf16[2,256,512]{2,1,0:T(8,128)(2,1)S(1)} collective-permute-done((bf16[2,256,512]{2,1,0:T(8,128)(2,1)S(1)}, bf16[2,256,512]{2,1,0:T(8,128)(2,1)S(1)}, u32[]{:S(2)}, u32[]{:S(2)}) %collective-permute-start.1) | collective-permute-done | bytes 524320 | tf_op jit(solution)/shard_map/ppermute | solution.py:232
  37.8 1.0 add_convert_fusion.refs_2_
  38.8 5.9 %all-to-all-start.1 = ((bf16[16,32,512]{2,1,0:T(8,128)(2,1)}), bf16[16,32,512]{2,1,0:T(8,128)(2,1)S(1)}, u32[]{:S(2)}, u32[]{:S(2)}) async-start(bf16[16,32,512]{2,1,0:T(8,128)(2,1)} %bitcast.4), calls=%async_computation.1 | async-start | bytes 1048576 | tf_op jit(solution)/shard_map/all_to_all | solution.py:238
  44.8 2.7 %collective-permute-start.2 = (bf16[2,256,512]{2,1,0:T(8,128)(2,1)S(1)}, bf16[2,256,512]{2,1,0:T(8,128)(2,1)S(1)}, u32[]{:S(2)}, u32[]{:S(2)}) collective-permute-start(bf16[2,256,512]{2,1,0:T(8,128)(2,1)S(1)} %shard_map.88.refs_0_), channel_id=1, source_target_pairs={{0,192},{192,384},{384,576},{576,0},{1,193},{193,385},{385,577},{5... | collective-permute-start | bytes 1572872 | tf_op jit(solution)/shard_map/ppermute | solution.py:237
  47.5 4.3 %collective-permute-start.3 = (bf16[2,256,512]{2,1,0:T(8,128)(2,1)S(1)}, bf16[2,256,512]{2,1,0:T(8,128)(2,1)S(1)}, u32[]{:S(2)}, u32[]{:S(2)}) collective-permute-start(bf16[2,256,512]{2,1,0:T(8,128)(2,1)S(1)} %shard_map.88.refs_0_), channel_id=1, source_target_pairs={{0,384},{192,576},{384,0},{576,192},{1,385},{193,577},{385,1},{577... | collective-permute-start | bytes 1572872 | tf_op jit(solution)/shard_map/ppermute | solution.py:237
  51.8 3.1 %collective-permute-start.4 = (bf16[2,256,512]{2,1,0:T(8,128)(2,1)S(1)}, bf16[2,256,512]{2,1,0:T(8,128)(2,1)S(1)}, u32[]{:S(2)}, u32[]{:S(2)}) collective-permute-start(bf16[2,256,512]{2,1,0:T(8,128)(2,1)S(1)} %shard_map.88.refs_0_), channel_id=1, source_target_pairs={{0,576},{192,0},{384,192},{576,384},{1,577},{193,1},{385,193},{577... | collective-permute-start | bytes 1572872 | tf_op jit(solution)/shard_map/ppermute | solution.py:237
  54.9 4.9 %all-to-all-done.1.refs_0_ = bf16[16,32,512]{2,1,0:T(8,128)(2,1)S(1)} async-done(((bf16[16,32,512]{2,1,0:T(8,128)(2,1)}), bf16[16,32,512]{2,1,0:T(8,128)(2,1)S(1)}, u32[]{:S(2)}, u32[]{:S(2)}) %all-to-all-start.1) | async-done | bytes 524320 | tf_op jit(solution)/shard_map/all_to_all | solution.py:238
  59.7 0.8 shard_map.87.refs_4_
  60.5 13.9 %all-to-all-start.2 = ((bf16[6,32,512]{2,1,0:T(8,128)(2,1)}), bf16[6,32,512]{2,1,0:T(8,128)(2,1)S(1)}, u32[]{:S(2)}, u32[]{:S(2)}) async-start(bf16[6,32,512]{2,1,0:T(8,128)(2,1)} %shard_map.87.refs_4_), calls=%async_computation.2 | async-start | bytes 393216 | tf_op jit(solution)/shard_map/all_to_all | solution.py:261
  74.4 0.0 collective-permute-done.2.refs_1_
  74.4 0.0 collective-permute-done.3.refs_2_
  74.4 0.0 collective-permute-done.4.refs_3_
  74.4 0.1 shard_map.89
  74.6 0.0 copy-start.2
  74.6 1.3 %copy-done.2 = bf16[4,2,256,512]{3,2,1,0:T(8,128)(2,1)} copy-done((bf16[4,2,256,512]{3,2,1,0:T(8,128)(2,1)}, bf16[4,2,256,512]{3,2,1,0:T(8,128)(2,1)S(1)}, u32[]{:S(2)}) %copy-start.2) | copy-done | bytes 2097176
  75.9 0.0 copy-start.1
  75.9 0.0 copy-start.4
  75.9 8.2 %all-to-all-done.2.refs_0_ = bf16[6,32,512]{2,1,0:T(8,128)(2,1)S(1)} async-done(((bf16[6,32,512]{2,1,0:T(8,128)(2,1)}), bf16[6,32,512]{2,1,0:T(8,128)(2,1)S(1)}, u32[]{:S(2)}, u32[]{:S(2)}) %all-to-all-start.2) | async-done | bytes 196640 | tf_op jit(solution)/shard_map/all_to_all | solution.py:261
  84.2 7.2 %collective-permute-start.6 = (bf16[4,2,256,512]{3,2,1,0:T(8,128)(2,1)}, bf16[4,2,256,512]{3,2,1,0:T(8,128)(2,1)}, u32[]{:S(2)}, u32[]{:S(2)}) collective-permute-start(bf16[4,2,256,512]{3,2,1,0:T(8,128)(2,1)} %copy-done.2), channel_id=1, source_target_pairs={{0,1},{1,0},{2,3},{3,2},{4,5},{5,4},{6,7},{7,6},{8,9},{9,8},{10,11... | collective-permute-start | bytes 6291464 | tf_op jit(solution)/shard_map/ppermute | solution.py:266
  91.5 12.5 %all_to_all.25 = bf16[8,32,512]{2,1,0:T(8,128)(2,1)S(1)} all-to-all(bf16[8,32,512]{2,1,0:T(8,128)(2,1)S(1)} %shard_map.90), channel_id=1, replica_groups=mesh['x'=4,'yh'=2,'yl'=4,'z'=6,'zp'=2,'c'=2] {'yl','zp'}, dimensions={0} | all-to-all | bytes 524288 | tf_op jit(solution)/shard_map/all_to_all | solution.py:265
  103.9 3.6 %collective-permute-start.5 = (bf16[256,512]{1,0:T(8,128)(2,1)S(1)}, bf16[256,512]{1,0:T(8,128)(2,1)S(1)}, u32[]{:S(2)}, u32[]{:S(2)}) collective-permute-start(bf16[256,512]{1,0:T(8,128)(2,1)S(1)} %bitcast.7), channel_id=1, source_target_pairs={{0,1},{1,0},{2,3},{3,2},{4,5},{5,4},{6,7},{7,6},{8,9},{9,8},{10,11... | collective-permute-start | bytes 786440 | tf_op jit(solution)/shard_map/ppermute | solution.py:267
  107.5 0.8 shard_map.91.refs_1_
  108.3 0.3 collective-permute-done.5.refs_2_
  108.6 1.4 %shard_map.92.refs_5_.refs_4_ = f32[8,4,128]{2,1,0:T(4,128)} custom-call(s32[3]{0:T(128)S(1)} %pad_add_fusion.refs_0_, f32[2,128]{1,0:T(2,128)S(1)} %shard_map.91.refs_1_, bf16[256,512]{1,0:T(8,128)(2,1)S(1)} %collective-permute-done.5.refs_2_, bf16[512,512]{1,0:T(8,128)(2,1)S(1)} %copy-done, bf16[2,512]{1,0:T(2,128)(2,1)S(1)} %bitcast.12), custom_call_target="tpu_custom_call" | custom-call | flops 262144 | bytes 524288 | tf_op jit(solution)/shard_map/pallas_call | solution.py:186
  110.1 4.5 %all-to-all-start.4 = ((f32[8,4,128]{2,1,0:T(4,128)}), f32[8,4,128]{2,1,0:T(4,128)S(1)}, u32[]{:S(2)}, u32[]{:S(2)}) async-start(f32[8,4,128]{2,1,0:T(4,128)} %shard_map.92.refs_5_.refs_4_), calls=%async_computation.4 | async-start | bytes 32768 | tf_op jit(solution)/shard_map/all_to_all | solution.py:278
  114.6 1.5 %shard_map.94 = bf16[512,512]{1,0:T(8,128)(2,1)} custom-call(s32[3]{0:T(128)S(1)} %pad_add_fusion.refs_0_, bf16[256,512]{1,0:T(8,128)(2,1)S(1)} %bitcast.9, bf16[256,512]{1,0:T(8,128)(2,1)S(1)} %collective-permute-done.5.refs_2_, bf16[1,512]{1,0:T(2,128)(2,1)S(1)} %broadcast_in_dim.3.refs_3_, f32[8,4,128]{2,1,0:T(4,128)} %shard_map.92.refs_5_.refs_4_), custom_call_target="tpu_custom_call" | custom-call | flops 262144 | bytes 1048576 | tf_op jit(solution)/shard_map/pallas_call | solution.py:186
  116.1 0.0 collective-permute-done.6.refs_4_
  116.1 0.0 copy-done.1
  116.1 0.0 copy-done.4
  116.1 0.0 copy-start.3
  116.1 1.6 %copy-done.3 = bf16[4,2,256,512]{3,2,1,0:T(8,128)(2,1)S(1)} copy-done((bf16[4,2,256,512]{3,2,1,0:T(8,128)(2,1)S(1)}, bf16[4,2,256,512]{3,2,1,0:T(8,128)(2,1)}, u32[]{:S(2)}) %copy-start.3) | copy-done | bytes 2097176
  117.7 4.8 %shard_map.93 = (bf16[128,512]{1,0:T(8,128)(2,1)}, bf16[128,4096]{1,0:T(8,128)(2,1)}) custom-call(s32[3]{0:T(128)S(1)} %pad_add_fusion.refs_0_, bf16[128,4096]{1,0:T(8,128)(2,1)S(1)} %copy-done.1, bf16[128,512]{1,0:T(8,128)(2,1)S(1)} %copy-done.4, bf16[4,2,256,512]{3,2,1,0:T(8,128)(2,1)S(1)} %copy-done.3, ...), custom_call_target="tpu_custom_call" | custom-call | flops 1073741824 | bytes 6291456 | tf_op jit(solution)/shard_map/pallas_call | solution.py:186
  122.5 1.0 all-to-all-done.4
  123.6 0.6 copy.10
  (3 shorter events, 0.1 us)
Async XLA Ops:
  0.6 8.0 %copy-start.7 = (bf16[512]{0:T(512)(128)(2,1)S(1)}, bf16[512]{0:T(512)(128)(2,1)}, u32[]{:S(2)}) copy-start(bf16[512]{0:T(512)(128)(2,1)} %param.6) | copy-start | bytes 3076
  0.6 8.1 %copy-start.5 = (bf16[512,2]{0,1:T(2,128)(2,1)S(1)}, bf16[512,2]{0,1:T(2,128)(2,1)}, u32[]{:S(2)}) copy-start(bf16[512,2]{0,1:T(2,128)(2,1)} %param.8) | copy-start | bytes 6148
  0.7 8.1 %copy-start = (bf16[512,512]{1,0:T(8,128)(2,1)S(1)}, bf16[512,512]{1,0:T(8,128)(2,1)}, u32[]{:S(2)}) copy-start(bf16[512,512]{1,0:T(8,128)(2,1)} %refs_3_.1) | copy-start | bytes 1572868
  3.8 5.0 %copy-start.6 = (f32[8,1]{1,0:T(8,128)S(1)}, f32[8,1]{1,0:T(8,128)}, u32[]{:S(2)}) copy-start(f32[8,1]{1,0:T(8,128)} %get-tuple-element.17.refs_4_) | copy-start | bytes 100
  3.8 17.4 %all-to-all-start = ((bf16[4,128,1536]{2,1,0:T(8,128)(2,1)}), bf16[4,128,1536]{2,1,0:T(8,128)(2,1)S(1)}, u32[]{:S(2)}, u32[]{:S(2)}) async-start(bf16[4,128,1536]{2,1,0:T(8,128)(2,1)} %get-tuple-element.16), calls=%async_computation | async-start | bytes 3145728 | tf_op jit(solution)/shard_map/all_to_all | solution.py:217
  9.4 11.3 %collective-permute-start = (bf16[256,512]{1,0:T(8,128)(2,1)S(1)}, bf16[256,512]{1,0:T(8,128)(2,1)S(1)}, u32[]{:S(2)}, u32[]{:S(2)}) collective-permute-start(bf16[256,512]{1,0:T(8,128)(2,1)S(1)} %shard_map.85.refs_0_), channel_id=1, source_target_pairs={{0,96},{96,0},{1,97},{97,1},{2,98},{98,2},{3,99},{99,3},{4,100},{1... | collective-permute-start | bytes 786440 | tf_op jit(solution)/shard_map/ppermute | solution.py:222
  22.5 15.4 %collective-permute-start.1 = (bf16[2,256,512]{2,1,0:T(8,128)(2,1)S(1)}, bf16[2,256,512]{2,1,0:T(8,128)(2,1)S(1)}, u32[]{:S(2)}, u32[]{:S(2)}) collective-permute-start(bf16[2,256,512]{2,1,0:T(8,128)(2,1)S(1)} %get-tuple-element.19), channel_id=1, source_target_pairs={{0,1},{1,0},{2,3},{3,2},{4,5},{5,4},{6,7},{7,6},{8,9},{9,8},{10,11... | collective-permute-start | bytes 1572872 | tf_op jit(solution)/shard_map/ppermute | solution.py:232
  38.8 20.9 %all-to-all-start.1 = ((bf16[16,32,512]{2,1,0:T(8,128)(2,1)}), bf16[16,32,512]{2,1,0:T(8,128)(2,1)S(1)}, u32[]{:S(2)}, u32[]{:S(2)}) async-start(bf16[16,32,512]{2,1,0:T(8,128)(2,1)} %bitcast.4), calls=%async_computation.1 | async-start | bytes 1048576 | tf_op jit(solution)/shard_map/all_to_all | solution.py:238
  44.8 29.6 %collective-permute-start.2 = (bf16[2,256,512]{2,1,0:T(8,128)(2,1)S(1)}, bf16[2,256,512]{2,1,0:T(8,128)(2,1)S(1)}, u32[]{:S(2)}, u32[]{:S(2)}) collective-permute-start(bf16[2,256,512]{2,1,0:T(8,128)(2,1)S(1)} %shard_map.88.refs_0_), channel_id=1, source_target_pairs={{0,192},{192,384},{384,576},{576,0},{1,193},{193,385},{385,577},{5... | collective-permute-start | bytes 1572872 | tf_op jit(solution)/shard_map/ppermute | solution.py:237
  47.5 27.0 %collective-permute-start.3 = (bf16[2,256,512]{2,1,0:T(8,128)(2,1)S(1)}, bf16[2,256,512]{2,1,0:T(8,128)(2,1)S(1)}, u32[]{:S(2)}, u32[]{:S(2)}) collective-permute-start(bf16[2,256,512]{2,1,0:T(8,128)(2,1)S(1)} %shard_map.88.refs_0_), channel_id=1, source_target_pairs={{0,384},{192,576},{384,0},{576,192},{1,385},{193,577},{385,1},{577... | collective-permute-start | bytes 1572872 | tf_op jit(solution)/shard_map/ppermute | solution.py:237
  51.8 22.7 %collective-permute-start.4 = (bf16[2,256,512]{2,1,0:T(8,128)(2,1)S(1)}, bf16[2,256,512]{2,1,0:T(8,128)(2,1)S(1)}, u32[]{:S(2)}, u32[]{:S(2)}) collective-permute-start(bf16[2,256,512]{2,1,0:T(8,128)(2,1)S(1)} %shard_map.88.refs_0_), channel_id=1, source_target_pairs={{0,576},{192,0},{384,192},{576,384},{1,577},{193,1},{385,193},{577... | collective-permute-start | bytes 1572872 | tf_op jit(solution)/shard_map/ppermute | solution.py:237
  60.5 23.7 %all-to-all-start.2 = ((bf16[6,32,512]{2,1,0:T(8,128)(2,1)}), bf16[6,32,512]{2,1,0:T(8,128)(2,1)S(1)}, u32[]{:S(2)}, u32[]{:S(2)}) async-start(bf16[6,32,512]{2,1,0:T(8,128)(2,1)} %shard_map.87.refs_4_), calls=%async_computation.2 | async-start | bytes 393216 | tf_op jit(solution)/shard_map/all_to_all | solution.py:261
  74.6 1.3 %copy-start.2 = (bf16[4,2,256,512]{3,2,1,0:T(8,128)(2,1)}, bf16[4,2,256,512]{3,2,1,0:T(8,128)(2,1)S(1)}, u32[]{:S(2)}) copy-start(bf16[4,2,256,512]{3,2,1,0:T(8,128)(2,1)S(1)} %get-tuple-element.23.refs_3_) | copy-start | bytes 6291460
  75.9 40.2 %copy-start.1 = (bf16[128,4096]{1,0:T(8,128)(2,1)S(1)}, bf16[128,4096]{1,0:T(8,128)(2,1)}, u32[]{:S(2)}) copy-start(bf16[128,4096]{1,0:T(8,128)(2,1)} %refs_1_.3) | copy-start | bytes 3145732
  75.9 40.2 %copy-start.4 = (bf16[128,512]{1,0:T(8,128)(2,1)S(1)}, bf16[128,512]{1,0:T(8,128)(2,1)}, u32[]{:S(2)}) copy-start(bf16[128,512]{1,0:T(8,128)(2,1)} %refs_2_.3) | copy-start | bytes 393220
  84.2 31.9 %collective-permute-start.6 = (bf16[4,2,256,512]{3,2,1,0:T(8,128)(2,1)}, bf16[4,2,256,512]{3,2,1,0:T(8,128)(2,1)}, u32[]{:S(2)}, u32[]{:S(2)}) collective-permute-start(bf16[4,2,256,512]{3,2,1,0:T(8,128)(2,1)} %copy-done.2), channel_id=1, source_target_pairs={{0,1},{1,0},{2,3},{3,2},{4,5},{5,4},{6,7},{7,6},{8,9},{9,8},{10,11... | collective-permute-start | bytes 6291464 | tf_op jit(solution)/shard_map/ppermute | solution.py:266
  103.9 4.7 %collective-permute-start.5 = (bf16[256,512]{1,0:T(8,128)(2,1)S(1)}, bf16[256,512]{1,0:T(8,128)(2,1)S(1)}, u32[]{:S(2)}, u32[]{:S(2)}) collective-permute-start(bf16[256,512]{1,0:T(8,128)(2,1)S(1)} %bitcast.7), channel_id=1, source_target_pairs={{0,1},{1,0},{2,3},{3,2},{4,5},{5,4},{6,7},{7,6},{8,9},{9,8},{10,11... | collective-permute-start | bytes 786440 | tf_op jit(solution)/shard_map/ppermute | solution.py:267
  110.1 13.5 %all-to-all-start.4 = ((f32[8,4,128]{2,1,0:T(4,128)}), f32[8,4,128]{2,1,0:T(4,128)S(1)}, u32[]{:S(2)}, u32[]{:S(2)}) async-start(f32[8,4,128]{2,1,0:T(4,128)} %shard_map.92.refs_5_.refs_4_), calls=%async_computation.4 | async-start | bytes 32768 | tf_op jit(solution)/shard_map/all_to_all | solution.py:278
  116.1 1.6 %copy-start.3 = (bf16[4,2,256,512]{3,2,1,0:T(8,128)(2,1)S(1)}, bf16[4,2,256,512]{3,2,1,0:T(8,128)(2,1)}, u32[]{:S(2)}) copy-start(bf16[4,2,256,512]{3,2,1,0:T(8,128)(2,1)} %copy-done.2) | copy-start | bytes 6291460
